TPU v7x, 256 devices: a whole 4x4x8 slice. The times are simulated.
256 devices in a mesh: seq: 64 (over z, x, core), kvh: 4 (over y).
Axes of the slice: x: 4, y: 4, z: 8, core: 2. Of those that a mesh axis runs over, the one named last changes fastest.
Arguments:
- queries: bfloat16 [64, 2, 128, 128], P('seq', None, 'kvh'), may hold values from -64 to 64
- new_keys: bfloat16 [64, 2, 8, 128], P('seq', None, 'kvh'), may hold values from -6 to 6
- new_values: bfloat16 [64, 2, 8, 128], P('seq', None, 'kvh'), may hold values from -6 to 6
- cache_keys: bfloat16 [64, 8192, 8, 128], P('kvh', 'seq'), may hold values from -36 to 36
- cache_values: bfloat16 [64, 8192, 8, 128], P('kvh', 'seq'), may hold values from -6 to 6
- decode_order: int32 [64], replicated, may hold values from 0 to 63, each once
- cache_len: int32 [64], replicated, may hold values from 1 to 8192, as said below
Outputs:
- attended: bfloat16 [64, 2, 128, 128], P('seq', None, 'kvh')
Inputs may be any that keep to these rules, and one draw needn't show every extreme that they name: `cache_len`: every row holds at least one valid position, and some row holds all 8192.
All inputs are finite; a program needn't handle non-finite values.
Results may differ from a plain program's by a relative error of at most 0.0045.
Values may be sent and summed in bfloat16 or wider, within the bound.
No kernel may reach another device: no remote copies, remote signals or barrier semaphores. Data moves between devices by JAX's collectives and lax.ppermute only.
A program may use at most 64 MiB of HBM per device.

v0:
```python
import jax
import jax.numpy as jnp
from jax import lax
from jax.sharding import PartitionSpec as P

NEG_FILL = -1e30


def on_device(queries, new_keys, new_values, cache_keys, cache_values, decode_order, cache_len):
    rows_dev, steps, heads_local, head_size = queries.shape
    kv_local = new_keys.shape[2]
    group = heads_local // kv_local
    scale = head_size ** (-0.5)
    lengths = cache_len[decode_order]
    query_local = queries.reshape(rows_dev, steps, kv_local, group, head_size)
    causal = jnp.arange(steps)[:, None] >= jnp.arange(steps)[None, :]
    causal_own = causal.reshape(1, steps, 1, 1, steps)
    fresh = (
        jnp.einsum("rtkgd,rukd->rtkgu", query_local, new_keys, preferred_element_type=jnp.float32)
        * scale
    )
    fresh = jnp.where(causal_own, fresh, NEG_FILL)
    first_row = lax.axis_index("seq") * rows_dev
    keys_heads, values_heads = (
        lax.all_to_all(cache_keys, "kvh", split_axis=2, concat_axis=0, tiled=True),
        lax.all_to_all(cache_values, "kvh", split_axis=2, concat_axis=0, tiled=True),
    )
    keys_heads = keys_heads[decode_order]
    values_heads = values_heads[decode_order]
    keys_own, values_own = (
        lax.all_to_all(keys_heads, "seq", split_axis=0, concat_axis=1, tiled=True),
        lax.all_to_all(values_heads, "seq", split_axis=0, concat_axis=1, tiled=True),
    )
    own_len = lax.dynamic_slice_in_dim(lengths, first_row, rows_dev)
    positions = jnp.arange(keys_own.shape[1])
    valid = (positions[None, :] < own_len[:, None]).reshape(rows_dev, 1, 1, 1, keys_own.shape[1])
    scores = (
        jnp.einsum("rtkgd,rskd->rtkgs", query_local, keys_own, preferred_element_type=jnp.float32)
        * scale
    )
    scores = jnp.where(valid, scores, NEG_FILL)
    top = jnp.maximum(jnp.max(scores, -1), jnp.max(fresh, -1))
    weights = jnp.where(valid, jnp.exp(scores - top[..., None]), 0.0)
    total = jnp.sum(weights, -1)
    accum = jnp.einsum(
        "rtkgs,rskd->rtkgd",
        weights.astype(jnp.bfloat16),
        values_own,
        preferred_element_type=jnp.float32,
    )
    fresh_weights = jnp.where(causal_own, jnp.exp(fresh - top[..., None]), 0.0)
    total = total + jnp.sum(fresh_weights, -1)
    accum = accum + jnp.einsum(
        "rtkgu,rukd->rtkgd",
        fresh_weights.astype(jnp.bfloat16),
        new_values,
        preferred_element_type=jnp.float32,
    )
    attended = (accum / total[..., None]).astype(jnp.bfloat16)
    return attended.reshape(rows_dev, steps, heads_local, head_size)


def solution(mesh):
    return jax.shard_map(
        on_device,
        mesh=mesh,
        in_specs=(
            P("seq", None, "kvh", None),
            P("seq", None, "kvh", None),
            P("seq", None, "kvh", None),
            P("kvh", "seq", None, None),
            P("kvh", "seq", None, None),
            P(),
            P(),
        ),
        out_specs=P("seq", None, "kvh", None),
        check_vma=False,
    )
```

profile of v0, /device:TPU:2, one launch (start us, length us, event | category | flops | bytes accessed | tf_op | source)
XLA Modules:
  0.0 326.6 jit_solution(14941874737875909727)
XLA Ops:
  0.0 0.0 copy-start
  0.0 5.2 %copy.43 = bf16[16,128,8,128]{3,1,0,2:T(8,128)(2,1)} copy(bf16[16,128,8,128]{3,2,1,0:T(8,128)(2,1)} %param.10) | data formatting | bytes 8388608 | tf_op args[3]
  5.2 4.8 %all-to-all-start.2 = ((bf16[16,128,8,128]{3,1,0,2:T(8,128)(2,1)}), bf16[16,128,8,128]{3,1,0,2:T(8,128)(2,1)}, u32[]{:S(2)}, u32[]{:S(2)}) async-start(bf16[16,128,8,128]{3,1,0,2:T(8,128)(2,1)} %copy.43), calls=%async_computation.2 | async-start | bytes 8388608 | tf_op jit(solution)/shard_map/all_to_all | solution.py:25
  10.1 5.2 %copy.39 = bf16[16,128,8,128]{3,1,0,2:T(8,128)(2,1)} copy(bf16[16,128,8,128]{3,2,1,0:T(8,128)(2,1)} %param.11) | data formatting | bytes 8388608 | tf_op args[4]
  15.3 0.0 copy-start.4
  15.3 43.9 %all-to-all-done.2 = bf16[16,128,8,128]{3,1,0,2:T(8,128)(2,1)} async-done(((bf16[16,128,8,128]{3,1,0,2:T(8,128)(2,1)}), bf16[16,128,8,128]{3,1,0,2:T(8,128)(2,1)}, u32[]{:S(2)}, u32[]{:S(2)}) %all-to-all-start.2) | async-done | bytes 4194336 | tf_op jit(solution)/shard_map/all_to_all | solution.py:25
  59.2 4.8 %all-to-all-start = ((bf16[16,128,8,128]{3,1,0,2:T(8,128)(2,1)}), bf16[16,128,8,128]{3,1,0,2:T(8,128)(2,1)}, u32[]{:S(2)}, u32[]{:S(2)}) async-start(bf16[16,128,8,128]{3,1,0,2:T(8,128)(2,1)} %copy.39), calls=%async_computation | async-start | bytes 8388608 | tf_op jit(solution)/shard_map/all_to_all | solution.py:26
  64.1 0.0 copy-done.4
  64.1 4.7 %copy.45 = bf16[4,16,128,2,128]{4,2,3,1,0:T(8,128)(2,1)} copy(bf16[4,16,128,2,128]{4,2,1,3,0:T(8,128)(2,1)} %bitcast.10) | data formatting | bytes 8388608 | tf_op jit(solution)/shard_map/all_to_all | solution.py:25
  68.8 5.2 %gather_fusion.2 = bf16[64,128,2,128]{3,1,2,0:T(8,128)(2,1)} fusion(bf16[64,128,2,128]{3,1,2,0:T(8,128)(2,1)} %bitcast.68, s32[1024]{0:T(1024)S(1)} %pad_clamp_fusion), kind=kCustom, calls=%fused_computation.2 | custom fusion | bytes 8388864 | tf_op jit(solution)/shard_map/gather | solution.py:28
  74.1 38.3 %all-to-all-done = bf16[16,128,8,128]{3,1,0,2:T(8,128)(2,1)} async-done(((bf16[16,128,8,128]{3,1,0,2:T(8,128)(2,1)}), bf16[16,128,8,128]{3,1,0,2:T(8,128)(2,1)}, u32[]{:S(2)}, u32[]{:S(2)}) %all-to-all-start) | async-done | bytes 4194336 | tf_op jit(solution)/shard_map/all_to_all | solution.py:26
  112.3 12.2 %all-to-all-start.3 = ((bf16[64,128,2,128]{3,1,2,0:T(8,128)(2,1)}), bf16[64,128,2,128]{3,1,2,0:T(8,128)(2,1)}, u32[]{:S(2)}, u32[]{:S(2)}) async-start(bf16[64,128,2,128]{3,1,2,0:T(8,128)(2,1)} %gather_fusion.2), calls=%async_computation.3 | async-start | bytes 8388608 | tf_op jit(solution)/shard_map/all_to_all | solution.py:31
  124.6 4.7 %copy.41 = bf16[4,16,128,2,128]{4,2,3,1,0:T(8,128)(2,1)} copy(bf16[4,16,128,2,128]{4,2,1,3,0:T(8,128)(2,1)} %bitcast.2) | data formatting | bytes 8388608 | tf_op jit(solution)/shard_map/all_to_all | solution.py:26
  129.3 5.2 %gather_fusion = bf16[64,128,2,128]{3,1,2,0:T(8,128)(2,1)} fusion(bf16[64,128,2,128]{3,1,2,0:T(8,128)(2,1)} %bitcast.69, s32[1024]{0:T(1024)S(1)} %pad_clamp_fusion), kind=kCustom, calls=%fused_computation | custom fusion | bytes 8388864 | tf_op jit(solution)/shard_map/gather | solution.py:29
  134.5 0.0 copy-start.1
  134.5 0.0 copy-start.3
  134.5 86.2 %all-to-all-done.3 = bf16[64,128,2,128]{3,1,2,0:T(8,128)(2,1)} async-done(((bf16[64,128,2,128]{3,1,2,0:T(8,128)(2,1)}), bf16[64,128,2,128]{3,1,2,0:T(8,128)(2,1)}, u32[]{:S(2)}, u32[]{:S(2)}) %all-to-all-start.3) | async-done | bytes 4194336 | tf_op jit(solution)/shard_map/all_to_all | solution.py:31
  220.7 5.7 %all-to-all-start.1 = ((bf16[64,128,2,128]{3,1,2,0:T(8,128)(2,1)}), bf16[64,128,2,128]{3,1,2,0:T(8,128)(2,1)}, u32[]{:S(2)}, u32[]{:S(2)}) async-start(bf16[64,128,2,128]{3,1,2,0:T(8,128)(2,1)} %gather_fusion), calls=%async_computation.1 | async-start | bytes 8388608 | tf_op jit(solution)/shard_map/all_to_all | solution.py:32
  226.4 0.0 copy-done.1
  226.4 0.8 gather_fusion.1
  227.1 0.6 dynamic_slice.3
  227.7 0.7 iota_compare_fusion
  228.4 0.0 copy-done
  228.4 0.0 copy-done.3
  228.4 0.1 convolution_multiply_fusion.1
  228.6 0.1 fusion.15
  228.6 2.5 copy.46
  231.2 0.0 copy-start.2
  231.2 1.6 fusion.21
  232.8 0.1 fusion.20
  232.9 0.6 fusion.3
  233.5 0.0 copy-done.2
  233.5 0.2 convolution_bitcast_fusion
  233.7 88.9 %all-to-all-done.1 = bf16[64,128,2,128]{3,1,2,0:T(8,128)(2,1)} async-done(((bf16[64,128,2,128]{3,1,2,0:T(8,128)(2,1)}), bf16[64,128,2,128]{3,1,2,0:T(8,128)(2,1)}, u32[]{:S(2)}, u32[]{:S(2)}) %all-to-all-start.1) | async-done | bytes 4194336 | tf_op jit(solution)/shard_map/all_to_all | solution.py:32
  322.6 2.5 copy.42
  325.1 0.9 fusion.7
  325.9 0.6 copy.54
  (5 shorter events, 0.0 us)
Async XLA Ops:
  0.0 228.4 %copy-start = (bf16[1,2,32,128]{3,2,1,0:T(8,128)(2,1)S(1)}, bf16[1,2,32,128]{3,2,1,0:T(8,128)(2,1)}, u32[]{:S(2)}) copy-start(bf16[1,2,32,128]{3,2,1,0:T(8,128)(2,1)} %param.7) | copy-start | bytes 49156
  5.2 54.0 %all-to-all-start.2 = ((bf16[16,128,8,128]{3,1,0,2:T(8,128)(2,1)}), bf16[16,128,8,128]{3,1,0,2:T(8,128)(2,1)}, u32[]{:S(2)}, u32[]{:S(2)}) async-start(bf16[16,128,8,128]{3,1,0,2:T(8,128)(2,1)} %copy.43), calls=%async_computation.2 | async-start | bytes 8388608 | tf_op jit(solution)/shard_map/all_to_all | solution.py:25
  15.3 48.7 %copy-start.4 = (s32[64]{0:T(128)S(1)}, s32[64]{0:T(128)}, u32[]{:S(2)}) copy-start(s32[64]{0:T(128)} %param.12) | copy-start | bytes 772
  59.2 53.1 %all-to-all-start = ((bf16[16,128,8,128]{3,1,0,2:T(8,128)(2,1)}), bf16[16,128,8,128]{3,1,0,2:T(8,128)(2,1)}, u32[]{:S(2)}, u32[]{:S(2)}) async-start(bf16[16,128,8,128]{3,1,0,2:T(8,128)(2,1)} %copy.39), calls=%async_computation | async-start | bytes 8388608 | tf_op jit(solution)/shard_map/all_to_all | solution.py:26
  112.3 108.3 %all-to-all-start.3 = ((bf16[64,128,2,128]{3,1,2,0:T(8,128)(2,1)}), bf16[64,128,2,128]{3,1,2,0:T(8,128)(2,1)}, u32[]{:S(2)}, u32[]{:S(2)}) async-start(bf16[64,128,2,128]{3,1,2,0:T(8,128)(2,1)} %gather_fusion.2), calls=%async_computation.3 | async-start | bytes 8388608 | tf_op jit(solution)/shard_map/all_to_all | solution.py:31
  134.5 91.9 %copy-start.1 = (s32[64]{0:T(128)S(1)}, s32[64]{0:T(128)}, u32[]{:S(2)}) copy-start(s32[64]{0:T(128)} %param.13) | copy-start | bytes 772
  134.5 93.9 %copy-start.3 = (bf16[1,2,2,128]{3,2,1,0:T(2,128)(2,1)S(1)}, bf16[1,2,2,128]{3,2,1,0:T(2,128)(2,1)}, u32[]{:S(2)}) copy-start(bf16[1,2,2,128]{3,2,1,0:T(2,128)(2,1)} %param.8) | copy-start | bytes 3076
  220.7 101.9 %all-to-all-start.1 = ((bf16[64,128,2,128]{3,1,2,0:T(8,128)(2,1)}), bf16[64,128,2,128]{3,1,2,0:T(8,128)(2,1)}, u32[]{:S(2)}, u32[]{:S(2)}) async-start(bf16[64,128,2,128]{3,1,2,0:T(8,128)(2,1)} %gather_fusion), calls=%async_computation.1 | async-start | bytes 8388608 | tf_op jit(solution)/shard_map/all_to_all | solution.py:32
  231.2 2.3 copy-start.2
where the time goes:
time: 327 us
  waiting for transfers between devices  257 us (79%)
  local copies, waits for them, and re-layouts  37.4 us (11%)
  starting transfers between devices  27.5 us (8%)
    all_to_all x1, waiting for transfers between devices, on_device(): lax.all_to_all(values_heads, 'seq', split_axis=0, concat_axis=1, tiled=True)  88.9 us
    all_to_all x1, waiting for transfers between devices, on_device(): lax.all_to_all(keys_heads, 'seq', split_axis=0, concat_axis=1, tiled=True)  86.2 us
    all_to_all x1, waiting for transfers between devices, on_device(): lax.all_to_all(cache_keys, 'kvh', split_axis=2, concat_axis=0, tiled=True)  43.9 us
    all_to_all x1, waiting for transfers between devices, on_device(): lax.all_to_all(cache_values, 'kvh', split_axis=2, concat_axis=0, tiled=True)  38.3 us
    all_to_all x1, starting transfers between devices, on_device(): lax.all_to_all(keys_heads, 'seq', split_axis=0, concat_axis=1, tiled=True)  12.2 us
    unnamed x12, local copies, waits for them, and re-layouts  10.5 us
  transfers between devices with their start and end apart: 4, of which 4 were waited for; matrix products, arithmetic and copies ran while one was open for 10% of the time, Pallas kernels for 0%

commit v1 on v0

v1 whole, which is shorter than its diff:
```python
import jax
import jax.numpy as jnp
from jax import lax
from jax.experimental import pallas as pl
from jax.experimental.pallas import tpu as pltpu
from jax.sharding import PartitionSpec as P

NEG_FILL = -1e30
NC, NY = 2, 4
CHIPS = 32
GROUP = 16
ROWS = 8
LINES = 64
TAIL = 8
BLOCK = LINES + TAIL
F32 = jnp.float32
BF16 = jnp.bfloat16
SMEM = pl.BlockSpec(memory_space=pltpu.SMEM)
VMEM = pl.BlockSpec(memory_space=pltpu.VMEM)
PARAMS = pltpu.CompilerParams(vmem_limit_bytes=16 * 2**20)
BRINGING = pl.CostEstimate(flops=2**30, bytes_accessed=2**24, transcendentals=0)


def split_pair(x):
    high = x.astype(BF16).astype(F32)
    low = (x - high).astype(BF16).astype(F32)
    return high, low


def coordinates():
    s = lax.axis_index("seq")
    return s // NC, lax.rem(s, NC), lax.axis_index("kvh")


def spread_kernel(own_ref, out_ref, core_ref):
    for chip in range(CHIPS):
        out_ref[chip] = own_ref[...]
    core_ref[0] = coordinates()[1]


def spread(own):
    return pl.pallas_call(
        spread_kernel,
        in_specs=[VMEM],
        out_specs=[VMEM, SMEM],
        out_shape=[
            jax.ShapeDtypeStruct((CHIPS,) + own.shape, BF16),
            jax.ShapeDtypeStruct((1,), jnp.int32),
        ],
        compiler_params=PARAMS,
    )(own)


def pass_on_kernel(token, got_ref, out_ref, token_out):
    out_ref[...] = got_ref[...]
    token_out[0] = token[0]


def pass_on(token, got):
    return pl.pallas_call(
        pass_on_kernel,
        in_specs=[SMEM, VMEM],
        out_specs=[VMEM, SMEM],
        out_shape=[
            jax.ShapeDtypeStruct(got.shape, got.dtype),
            jax.ShapeDtypeStruct((1,), jnp.int32),
        ],
        compiler_params=PARAMS,
        cost_estimate=BRINGING,
    )(token, got)


def to_groups_kernel(order, own_ref, other_ref, *refs):
    outs, slots = refs[:NY], refs[NY]
    _, core, y = coordinates()
    for slot in range(CHIPS * NC):
        slots[order[slot]] = slot
    for d in range(NY):
        group = lax.rem(y + d, NY)
        for row in range(ROWS):
            slot = slots[(group * NC + core) * ROWS + row]
            chip = slot // NC
            mine = lax.rem(slot, NC) == core
            outs[d][row] = jnp.where(mine, own_ref[chip], other_ref[chip])


def to_groups(order, own, other):
    _, lines, size = own.shape
    return pl.pallas_call(
        to_groups_kernel,
        in_specs=[SMEM, VMEM, VMEM],
        out_specs=[VMEM] * NY,
        out_shape=[jax.ShapeDtypeStruct((ROWS, lines, size), BF16)] * NY,
        scratch_shapes=[pltpu.SMEM((CHIPS * NC,), jnp.int32)],
        compiler_params=PARAMS,
        cost_estimate=BRINGING,
    )(order, own, other)


def by_head_kernel(core, *refs):
    ins, outs = refs[:4], refs[4 : 4 + NY]
    token, keep = refs[-2:]
    _, positions, kv, size = ins[0].shape
    y = coordinates()[2]
    token[0] = core[0]
    for slot in range(4):
        keep[slot] = ins[slot][0].reshape(positions * kv, size).astype(F32)
    for d in range(NY):
        quarter = lax.rem(y + NY - d, NY)
        for k in range(2):
            head = pl.ds(2 * quarter + k, positions, stride=kv)
            for i in range(2):
                outs[d][0, i * 2 + k] = keep[i, head, :].astype(BF16).T
                outs[d][0, 4 + i * 2 + k] = keep[2 + i, head, :].astype(BF16)


def by_head(core, keys, values):
    _, positions, kv, size = keys[0].shape
    rows = pl.BlockSpec((1, positions, kv, size), lambda i, core: (core[0] * ROWS + i, 0, 0, 0))
    tiles = (8, size, positions)
    outs = pl.pallas_call(
        by_head_kernel,
        grid_spec=pltpu.PrefetchScalarGridSpec(
            num_scalar_prefetch=1,
            grid=(ROWS,),
            in_specs=[rows] * 4,
            out_specs=[pl.BlockSpec((1,) + tiles, lambda i, core: (i, 0, 0, 0))] * NY + [SMEM],
            scratch_shapes=[pltpu.VMEM((4, positions * kv, size), F32)],
        ),
        out_shape=[jax.ShapeDtypeStruct((ROWS,) + tiles, BF16)] * NY
        + [jax.ShapeDtypeStruct((1,), jnp.int32)],
        cost_estimate=pl.CostEstimate(
            flops=0, bytes_accessed=16 * ROWS * positions * kv * size, transcendentals=0
        ),
    )(core, *keys, *values)
    return outs[:NY], outs[NY]


def attend_kernel(lens, token, q_ref, cache_ref, out_ref, token_out):
    rows, _, size, half = cache_ref.shape
    positions = 2 * half
    scale = size ** (-0.5)
    token_out[0] = token[0]
    chip, core, group = coordinates()
    first = (group * NC + core) * ROWS
    at = lax.broadcasted_iota(jnp.int32, (1, positions), 1)
    own = (chip * NC + core) * half
    other = (chip * NC + 1 - core) * half - half
    start = jnp.where(at < half, own, other)
    stats = [[], [], [], []]
    for j in range(rows):
        valid = at < lens[first + j] - start
        weights, pairs = [], []
        for k in range(2):
            lines = [slice(t * 32 + k * GROUP, t * 32 + (k + 1) * GROUP) for t in range(2)]
            q = jnp.concatenate([q_ref[j, part, :] for part in lines], 0)
            keys = jnp.concatenate([cache_ref[j, k], cache_ref[j, 2 + k]], 1)
            scores = jnp.dot(q, keys, preferred_element_type=F32) * scale
            scores = jnp.where(valid, scores, NEG_FILL)
            high, low = split_pair(jnp.max(scores, 1, keepdims=True))
            weight = jnp.where(valid, jnp.exp(scores - (high + low)), 0.0)
            pairs.append((high, low) + split_pair(jnp.sum(weight, 1, keepdims=True)))
            weights.append(weight.astype(BF16))
        values = jnp.concatenate(
            [
                jnp.concatenate([cache_ref[j, 4 + 2 * i], cache_ref[j, 5 + 2 * i]], 1)
                for i in range(2)
            ],
            0,
        )
        o = jnp.dot(jnp.concatenate(weights, 0), values, preferred_element_type=F32)
        for t in range(2):
            for k in range(2):
                line = t * 32 + k * GROUP
                part = o[k * 32 + t * GROUP : k * 32 + (t + 1) * GROUP, k * size : (k + 1) * size]
                out_ref[j, line : line + GROUP, :] = part.astype(BF16)
                for i in range(4):
                    stats[i].append(pairs[k][i][t * GROUP : (t + 1) * GROUP])
    stats = [jnp.concatenate(stat, 0) for stat in stats]
    lane = lax.broadcasted_iota(jnp.int32, (rows * LINES, 128), 1)
    table = jnp.where(lane == 0, stats[0], 0.0)
    for i in range(1, 4):
        table = jnp.where(lane == i, stats[i], table)
    table = table.T[:TAIL]
    for j in range(rows):
        tail = table[:, (j // 2) * 128 : (j // 2 + 1) * 128]
        if j % 2 == 1:
            tail = pltpu.roll(tail, LINES, 1)
        out_ref[j, LINES:, :] = tail.astype(BF16)


def attend(lens, token, queries, cache):
    rows, _, size, positions = cache.shape
    return pl.pallas_call(
        attend_kernel,
        in_specs=[SMEM] * 2 + [VMEM] * 2,
        out_specs=[VMEM, SMEM],
        out_shape=[
            jax.ShapeDtypeStruct((rows, BLOCK, size), BF16),
            jax.ShapeDtypeStruct((1,), jnp.int32),
        ],
        compiler_params=PARAMS,
        cost_estimate=pl.CostEstimate(
            flops=120 * ROWS * LINES * positions * size,
            bytes_accessed=160 * ROWS * positions * size,
            transcendentals=0,
        ),
    )(lens, token, queries, cache)


def to_owners_kernel(order, *refs):
    own, other, out_ref, slots = refs[:NY], refs[NY : 2 * NY], refs[2 * NY], refs[2 * NY + 1]
    _, core, y = coordinates()
    for slot in range(CHIPS * NC):
        slots[order[slot]] = slot
    for d in range(NY):
        group = lax.rem(y + d, NY)
        for c, source in ((core, own[d]), (1 - core, other[d])):
            for row in range(ROWS):
                slot = slots[(group * NC + c) * ROWS + row]

                @pl.when(lax.rem(slot, NC) == core)
                def _():
                    out_ref[slot // NC] = source[row]


def to_owners(order, own, other):
    return pl.pallas_call(
        to_owners_kernel,
        in_specs=[SMEM] + [VMEM] * (2 * NY),
        out_specs=VMEM,
        out_shape=jax.ShapeDtypeStruct((CHIPS,) + own[0].shape[1:], BF16),
        scratch_shapes=[pltpu.SMEM((CHIPS * NC,), jnp.int32)],
        compiler_params=PARAMS,
    )(order, *own, *other)


def finish_kernel(part_ref, q_ref, key_ref, value_ref, out_ref):
    size = q_ref.shape[1]
    scale = size ** (-0.5)
    tail = part_ref[:, LINES:, :].astype(F32)
    tops = tail[:, 0, :] + tail[:, 1, :]
    totals = tail[:, 2, :] + tail[:, 3, :]
    table = jnp.concatenate([tops, totals, jnp.zeros((128 - 2 * CHIPS, 128), F32)], 0).T[:LINES]
    tops, totals = table[:, :CHIPS], table[:, CHIPS : 2 * CHIPS]
    line = lax.broadcasted_iota(jnp.int32, (LINES, 1), 0)
    step = line // 32
    first = (line % 32) // GROUP == 0
    q = q_ref[...].astype(F32)
    top = jnp.max(tops, 1, keepdims=True)
    scores, values = [], []
    for u in range(2):
        pair = key_ref[u].astype(F32)
        key = jnp.where(first, pair[0:1], pair[1:2])
        pair = value_ref[u].astype(F32)
        values.append(jnp.where(first, pair[0:1], pair[1:2]))
        score = jnp.sum(q * key, -1, keepdims=True) * scale
        scores.append(jnp.where(u <= step, score, NEG_FILL))
        top = jnp.maximum(top, scores[u])
    factors = jnp.exp(tops - top)
    total = jnp.sum(factors * totals, 1, keepdims=True)
    accum = jnp.zeros((LINES, size), F32)
    for chip in range(CHIPS):
        accum = accum + factors[:, chip : chip + 1] * part_ref[chip, :LINES, :].astype(F32)
    for u in range(2):
        weight = jnp.where(u <= step, jnp.exp(scores[u] - top), 0.0)
        total = total + weight
        accum = accum + weight.astype(BF16).astype(F32) * values[u]
    out_ref[...] = (accum / total).astype(BF16)


def finish(parts, queries, new_keys, new_values):
    return pl.pallas_call(
        finish_kernel,
        in_specs=[VMEM] * 4,
        out_specs=VMEM,
        out_shape=jax.ShapeDtypeStruct(queries.shape, BF16),
        compiler_params=PARAMS,
    )(parts, queries, new_keys, new_values)


def over_chips(x):
    groups = [[chip * NC + c for chip in range(CHIPS)] for c in range(NC)]
    return lax.all_to_all(
        x, "seq", split_axis=0, concat_axis=0, axis_index_groups=groups, tiled=True
    )


def along_kvh(x, d):
    return lax.ppermute(x, "kvh", [(y, (y + d) % NY) for y in range(NY)])


def to_other_core(x):
    return lax.ppermute(x, "seq", [(i, i ^ 1) for i in range(CHIPS * NC)])


def on_device(queries, new_keys, new_values, cache_keys, cache_values, decode_order, cache_len):
    size = queries.shape[-1]

    other_keys, other_values = to_other_core(cache_keys), to_other_core(cache_values)

    own = queries.reshape(LINES, size)
    send, core = spread(own)
    got = over_chips(send)
    caches, token = by_head(core, (cache_keys, other_keys), (cache_values, other_values))
    passed, token = pass_on(token, got)
    sends = to_groups(decode_order, got, to_other_core(passed))

    parts = [None] * NY
    near = (1, 3, 2, 0)
    gots = {d: along_kvh(sends[d], d) if d else sends[d] for d in near}
    for d in near:
        part, token = attend(cache_len, token, gots[d], caches[d])
        parts[d] = along_kvh(part, NY - d) if d else part

    part = over_chips(to_owners(decode_order, parts, [to_other_core(part) for part in parts]))
    out = finish(part, own, new_keys[0], new_values[0])
    return out.reshape(queries.shape)


def solution(mesh):
    return jax.shard_map(
        on_device,
        mesh=mesh,
        in_specs=(
            P("seq", None, "kvh", None),
            P("seq", None, "kvh", None),
            P("seq", None, "kvh", None),
            P("kvh", "seq", None, None),
            P("kvh", "seq", None, None),
            P(),
            P(),
        ),
        out_specs=P("seq", None, "kvh", None),
        check_vma=False,
    )
```

time: 327 us -> 89.4 us (0.27)
  waiting for transfers between devices: 257 us -> 12.3 us
  local copies, waits for them, and re-layouts: 37.4 us -> 0.76 us
  Pallas kernels: 0 us -> 27.7 us
  blocking collectives: 0 us -> 24.3 us
  starting transfers between devices: 27.5 us -> 23.6 us
    all_to_all x4 -> x1, waiting for transfers between devices: 257 us -> 6.14 us  [over_chips(): lax.all_to_all(x, 'seq', split_axis=0, concat_axis=0, axis_index_groups=g...]
    pallas_call x0 -> x10, Pallas kernels: none -> 27.7 us  [the longest x4 11 us: attend(): pl.pallas_call(attend_kernel, in_specs=[SMEM] * 2 + [VMEM] * 2, out_specs...]
    all_to_all x0 -> x1, blocking collectives: none -> 24.3 us  [over_chips(): lax.all_to_all(x, 'seq', split_axis=0, concat_axis=0, axis_index_groups=g...]
    all_to_all x4 -> x1, starting transfers between devices: 27.5 us -> 11.6 us  [over_chips(): lax.all_to_all(x, 'seq', split_axis=0, concat_axis=0, axis_index_groups=g...]
    all_to_all x4 -> x0, local copies, waits for them, and re-layouts: 14.4 us -> none  [the longest x1 4.71 us: on_device(): lax.all_to_all(cache_keys, 'kvh', split_axis=2, concat_axis=0, tiled=True)]
    ppermute x0 -> x13, starting transfers between devices: none -> 12 us  [the longest x6 10.5 us: along_kvh(): return lax.ppermute(x, 'kvh', [(y, (y + d) % NY) for y in range(NY)])]
    gather x3 -> x0, local copies, waits for them, and re-layouts: 11.2 us -> none  [the longest x1 5.24 us: on_device(): keys_heads = keys_heads[decode_order]]
    unnamed x12 -> x20, local copies, waits for them, and re-layouts: 10.5 us -> 0.76 us
  transfers between devices with their start and end apart: 4 -> 14, of which waited for: 4 -> 7; matrix products, arithmetic and copies ran while one was open for 10% -> 0% of each run, Pallas kernels for 0% -> 22%
where the time goes in v1:
time: 89.4 us; the launch traced here: 88.9 us
  Pallas kernels  27.7 us (31%)
  blocking collectives  24.3 us (27%)
  starting transfers between devices  23.6 us (26%)
  waiting for transfers between devices  12.3 us (14%)
    all_to_all x1, blocking collectives, over_chips(): lax.all_to_all(x, 'seq', split_axis=0, concat_axis=0, axis_index_groups=g...  24.3 us
    all_to_all x1, starting transfers between devices, over_chips(): lax.all_to_all(x, 'seq', split_axis=0, concat_axis=0, axis_index_groups=g...  11.6 us
    pallas_call x4, Pallas kernels, attend(): pl.pallas_call(attend_kernel, in_specs=[SMEM] * 2 + [VMEM] * 2, out_specs...  11 us
    pallas_call x1, Pallas kernels, by_head(): pl.pallas_call(by_head_kernel, grid_spec=pltpu.PrefetchScalarGridSpec(num...  10.8 us
    ppermute x6, starting transfers between devices, along_kvh(): return lax.ppermute(x, 'kvh', [(y, (y + d) % NY) for y in range(NY)])  10.5 us
    all_to_all x1, waiting for transfers between devices, over_chips(): lax.all_to_all(x, 'seq', split_axis=0, concat_axis=0, axis_index_groups=g...  6.14 us
    ppermute x6, waiting for transfers between devices, along_kvh(): return lax.ppermute(x, 'kvh', [(y, (y + d) % NY) for y in range(NY)])  3.22 us
    ppermute x7, waiting for transfers between devices, to_other_core(): return lax.ppermute(x, 'seq', [(i, i ^ 1) for i in range(CHIPS * NC)])  2.97 us
  transfers between devices with their start and end apart: 14, of which 7 were waited for; matrix products, arithmetic and copies ran while one was open for 0% of the time, Pallas kernels for 22%

profile of v1, /device:TPU:2, one launch (start us, length us, event | category | flops | bytes accessed | tf_op | source)
XLA Modules:
  0.0 88.9 jit_solution(14299560426423190719)
XLA Ops:
  0.0 0.0 collective-permute-start
  0.0 0.5 collective-permute-start.1
  0.5 0.7 copy-done
  1.2 0.9 shard_map.73
  2.1 11.6 %all-to-all-start = ((bf16[32,64,128]{2,1,0:T(8,128)(2,1)}), bf16[32,64,128]{2,1,0:T(8,128)(2,1)S(1)}, u32[]{:S(2)}, u32[]{:S(2)}) async-start(bf16[32,64,128]{2,1,0:T(8,128)(2,1)} %get-tuple-element.27), calls=%async_computation | async-start | bytes 1048576 | tf_op jit(solution)/shard_map/all_to_all | solution.py:284
  13.8 0.0 collective-permute-done.refs_1_
  13.8 0.0 collective-permute-done.1.refs_3_
  13.8 0.0 copy-start.4
  13.8 10.8 %shard_map.74 = (bf16[8,8,128,128]{3,2,1,0:T(8,128)(2,1)}, bf16[8,8,128,128]{3,2,1,0:T(8,128)(2,1)}, bf16[8,8,128,128]{3,2,1,0:T(8,128)(2,1)}, bf16[8,8,128,128]{3,2,1,0:T(8,128)(2,1)}, s32[1]{0:T(128)}) custom-call(s32[1]{0:T(128)} %get-tuple-element.25.core, bf16[16,128,8,128]{3,2,1,0:T(8,128)(2,1)} %refs_0_.1, ...), custom_call_target="tpu_custom_call" | custom-call | bytes 16777216 | tf_op jit(solution)/shard_map/pallas_call | solution.py:121
  24.6 0.0 copy-start.9
  24.6 6.1 %all-to-all-done.got_ref.own_ref = bf16[32,64,128]{2,1,0:T(8,128)(2,1)S(1)} async-done(((bf16[32,64,128]{2,1,0:T(8,128)(2,1)}), bf16[32,64,128]{2,1,0:T(8,128)(2,1)S(1)}, u32[]{:S(2)}, u32[]{:S(2)}) %all-to-all-start) | async-done | bytes 524320 | tf_op jit(solution)/shard_map/all_to_all | solution.py:284
  30.8 1.2 %shard_map.75 = (bf16[32,64,128]{2,1,0:T(8,128)(2,1)S(1)}, s32[1]{0:T(128)}) custom-call(s32[1]{0:T(128)} %get-tuple-element.26.token, bf16[32,64,128]{2,1,0:T(8,128)(2,1)S(1)} %all-to-all-done.got_ref.own_ref), custom_call_target="tpu_custom_call" | custom-call | flops 1073741824 | bytes 16777216 | tf_op jit(solution)/shard_map/pallas_call | solution.py:60
  32.0 0.1 collective-permute-start.2
  32.1 1.9 %collective-permute-done.2.other_ref = bf16[32,64,128]{2,1,0:T(8,128)(2,1)S(1)} collective-permute-done((bf16[32,64,128]{2,1,0:T(8,128)(2,1)S(1)}, bf16[32,64,128]{2,1,0:T(8,128)(2,1)S(1)}, u32[]{:S(2)}, u32[]{:S(2)}) %collective-permute-start.2) | collective-permute-done | bytes 524320 | tf_op jit(solution)/shard_map/ppermute | solution.py:294
  34.0 0.9 %shard_map.76 = (bf16[8,64,128]{2,1,0:T(8,128)(2,1)S(1)}, bf16[8,64,128]{2,1,0:T(8,128)(2,1)S(1)}, bf16[8,64,128]{2,1,0:T(8,128)(2,1)S(1)}, bf16[8,64,128]{2,1,0:T(8,128)(2,1)S(1)}) custom-call(s32[64]{0:T(128)S(1)} %copy-done.4, bf16[32,64,128]{2,1,0:T(8,128)(2,1)S(1)} %all-to-all-done.got_ref.own_ref, bf16[32,64,128]{2,1,0:T(8,128)(2,1)S(1)} %collective-permute-done.2.other_ref), custom_call_target="tpu_custom_call" | custom-call | flops 1073741824 | bytes 16777216 | tf_op jit(solution)/shard_map/pallas_call | solution.py:89
  34.9 0.0 copy-start.6
  35.0 1.7 %collective-permute-start.3 = (bf16[8,64,128]{2,1,0:T(8,128)(2,1)S(1)}, bf16[8,64,128]{2,1,0:T(8,128)(2,1)S(1)}, u32[]{:S(2)}, u32[]{:S(2)}) collective-permute-start(bf16[8,64,128]{2,1,0:T(8,128)(2,1)S(1)} %get-tuple-element.30), channel_id=1, source_target_pairs={{0,1},{1,2},{2,3},{3,0},{4,5},{5,6},{6,7},{7,4},{8,9},{9,10},{10,1... | collective-permute-start | bytes 393224 | tf_op jit(solution)/shard_map/ppermute | solution.py:290
  36.6 1.7 %collective-permute-start.4 = (bf16[8,64,128]{2,1,0:T(8,128)(2,1)S(1)}, bf16[8,64,128]{2,1,0:T(8,128)(2,1)S(1)}, u32[]{:S(2)}, u32[]{:S(2)}) collective-permute-start(bf16[8,64,128]{2,1,0:T(8,128)(2,1)S(1)} %get-tuple-element.33), channel_id=1, source_target_pairs={{0,3},{1,0},{2,1},{3,2},{4,7},{5,4},{6,5},{7,6},{8,11},{9,8},{10,9... | collective-permute-start | bytes 393224 | tf_op jit(solution)/shard_map/ppermute | solution.py:290
  38.3 2.0 %collective-permute-start.5 = (bf16[8,64,128]{2,1,0:T(8,128)(2,1)S(1)}, bf16[8,64,128]{2,1,0:T(8,128)(2,1)S(1)}, u32[]{:S(2)}, u32[]{:S(2)}) collective-permute-start(bf16[8,64,128]{2,1,0:T(8,128)(2,1)S(1)} %get-tuple-element.36), channel_id=1, source_target_pairs={{0,2},{1,3},{2,0},{3,1},{4,6},{5,7},{6,4},{7,5},{8,10},{9,11},{10,... | collective-permute-start | bytes 393224 | tf_op jit(solution)/shard_map/ppermute | solution.py:290
  40.3 1.6 %collective-permute-done.3.q_ref = bf16[8,64,128]{2,1,0:T(8,128)(2,1)S(1)} collective-permute-done((bf16[8,64,128]{2,1,0:T(8,128)(2,1)S(1)}, bf16[8,64,128]{2,1,0:T(8,128)(2,1)S(1)}, u32[]{:S(2)}, u32[]{:S(2)}) %collective-permute-start.3) | collective-permute-done | bytes 131104 | tf_op jit(solution)/shard_map/ppermute | solution.py:290
  41.8 0.0 copy-done.9
  41.9 2.8 %shard_map.77 = (bf16[8,72,128]{2,1,0:T(8,128)(2,1)S(1)}, s32[1]{0:T(128)}) custom-call(s32[64]{0:T(128)S(1)} %copy-done.9, s32[1]{0:T(128)} %get-tuple-element.28.token, bf16[8,64,128]{2,1,0:T(8,128)(2,1)S(1)} %collective-permute-done.3.q_ref, bf16[8,8,128,128]{3,2,1,0:T(8,128)(2,1)S(1)} %copy-done.8), custom_call_target="tpu_custom_call" | custom-call | flops 1006632960 | bytes 20971520 | tf_op jit(solution)/shard_map/pallas_call | solution.py:194
  44.6 0.0 collective-permute-done.4.q_ref
  44.6 2.8 %shard_map.78 = (bf16[8,72,128]{2,1,0:T(8,128)(2,1)S(1)}, s32[1]{0:T(128)}) custom-call(s32[64]{0:T(128)S(1)} %copy-done.9, s32[1]{0:T(128)} %get-tuple-element.32.token, bf16[8,64,128]{2,1,0:T(8,128)(2,1)S(1)} %collective-permute-done.4.q_ref, bf16[8,8,128,128]{3,2,1,0:T(8,128)(2,1)S(1)} %copy-done.7), custom_call_target="tpu_custom_call" | custom-call | flops 1006632960 | bytes 20971520 | tf_op jit(solution)/shard_map/pallas_call | solution.py:194
  47.5 0.0 collective-permute-done.5.q_ref
  47.5 2.8 %shard_map.79 = (bf16[8,72,128]{2,1,0:T(8,128)(2,1)S(1)}, s32[1]{0:T(128)}) custom-call(s32[64]{0:T(128)S(1)} %copy-done.9, s32[1]{0:T(128)} %get-tuple-element.35.token, bf16[8,64,128]{2,1,0:T(8,128)(2,1)S(1)} %collective-permute-done.5.q_ref, bf16[8,8,128,128]{3,2,1,0:T(8,128)(2,1)S(1)} %copy-done.6), custom_call_target="tpu_custom_call" | custom-call | flops 1006632960 | bytes 20971520 | tf_op jit(solution)/shard_map/pallas_call | solution.py:194
  50.2 0.0 copy-start.1
  50.3 0.0 copy-start.2
  50.3 0.0 copy-start.3
  50.3 2.0 %collective-permute-start.7 = (bf16[8,72,128]{2,1,0:T(8,128)(2,1)S(1)}, bf16[8,72,128]{2,1,0:T(8,128)(2,1)S(1)}, u32[]{:S(2)}, u32[]{:S(2)}) collective-permute-start(bf16[8,72,128]{2,1,0:T(8,128)(2,1)S(1)} %get-tuple-element.43), channel_id=1, source_target_pairs={{0,2},{1,3},{2,0},{3,1},{4,6},{5,7},{6,4},{7,5},{8,10},{9,11},{10,... | collective-permute-start | bytes 442376 | tf_op jit(solution)/shard_map/ppermute | solution.py:290
  52.3 1.9 %collective-permute-start.8 = (bf16[8,72,128]{2,1,0:T(8,128)(2,1)S(1)}, bf16[8,72,128]{2,1,0:T(8,128)(2,1)S(1)}, u32[]{:S(2)}, u32[]{:S(2)}) collective-permute-start(bf16[8,72,128]{2,1,0:T(8,128)(2,1)S(1)} %get-tuple-element.44), channel_id=1, source_target_pairs={{0,1},{1,2},{2,3},{3,0},{4,5},{5,6},{6,7},{7,4},{8,9},{9,10},{10,1... | collective-permute-start | bytes 442376 | tf_op jit(solution)/shard_map/ppermute | solution.py:290
  54.2 1.3 %collective-permute-start.6 = (bf16[8,72,128]{2,1,0:T(8,128)(2,1)S(1)}, bf16[8,72,128]{2,1,0:T(8,128)(2,1)S(1)}, u32[]{:S(2)}, u32[]{:S(2)}) collective-permute-start(bf16[8,72,128]{2,1,0:T(8,128)(2,1)S(1)} %get-tuple-element.42), channel_id=1, source_target_pairs={{0,3},{1,0},{2,1},{3,2},{4,7},{5,4},{6,5},{7,6},{8,11},{9,8},{10,9... | collective-permute-start | bytes 442376 | tf_op jit(solution)/shard_map/ppermute | solution.py:290
  55.5 0.0 copy-done.5
  55.5 2.7 %shard_map.80 = (bf16[8,72,128]{2,1,0:T(8,128)(2,1)S(1)}, s32[1]{0:T(128)}) custom-call(s32[64]{0:T(128)S(1)} %copy-done.9, s32[1]{0:T(128)} %get-tuple-element.38.token, bf16[8,64,128]{2,1,0:T(8,128)(2,1)S(1)} %get-tuple-element.39.q_ref, bf16[8,8,128,128]{3,2,1,0:T(8,128)(2,1)S(1)} %copy-done.5), custom_call_target="tpu_custom_call" | custom-call | flops 1006632960 | bytes 20971520 | tf_op jit(solution)/shard_map/pallas_call | solution.py:194
  58.2 0.1 collective-permute-start.9
  58.3 0.3 collective-permute-done.7.refs_2_
  58.6 0.2 collective-permute-start.11
  58.8 1.3 %collective-permute-done.8.refs_3_ = bf16[8,72,128]{2,1,0:T(8,128)(2,1)S(1)} collective-permute-done((bf16[8,72,128]{2,1,0:T(8,128)(2,1)S(1)}, bf16[8,72,128]{2,1,0:T(8,128)(2,1)S(1)}, u32[]{:S(2)}, u32[]{:S(2)}) %collective-permute-start.8) | collective-permute-done | bytes 147488 | tf_op jit(solution)/shard_map/ppermute | solution.py:290
  60.2 0.0 collective-permute-start.12
  60.2 0.0 collective-permute-done.6.refs_1_
  60.2 0.5 collective-permute-start.10
  60.7 0.0 collective-permute-done.9.refs_4_
  60.7 0.0 collective-permute-done.11.refs_6_
  60.7 0.9 collective-permute-done.12.refs_7_
  61.5 0.2 collective-permute-done.10.refs_5_
  61.7 1.5 %shard_map.81 = bf16[32,72,128]{2,1,0:T(8,128)(2,1)S(1)} custom-call(s32[64]{0:T(128)S(1)} %copy-done.4, bf16[8,72,128]{2,1,0:T(8,128)(2,1)S(1)} %get-tuple-element.41.refs_0_, bf16[8,72,128]{2,1,0:T(8,128)(2,1)S(1)} %collective-permute-done.6.refs_1_, bf16[8,72,128]{2,1,0:T(8,128)(2,1)S(1)} %collective-permute-done.7.refs_2_, ...), custom_call_target="tpu_custom_call" | custom-call | tf_op jit(solution)/shard_map/pallas_call | solution.py:228
  63.3 24.3 %all_to_all.10.part_ref = bf16[32,72,128]{2,1,0:T(8,128)(2,1)S(1)} all-to-all(bf16[32,72,128]{2,1,0:T(8,128)(2,1)S(1)} %shard_map.81), channel_id=1, replica_groups={{0,8,16,24,32,40,48,56,64,72,80,88,96,104,112,120,128,136,144,152,160,1..., dimensions={0} | all-to-all | bytes 1179648 | tf_op jit(solution)/shard_map/all_to_all | solution.py:284
  87.5 1.4 %shard_map.82 = bf16[64,128]{1,0:T(8,128)(2,1)} custom-call(bf16[32,72,128]{2,1,0:T(8,128)(2,1)S(1)} %all_to_all.10.part_ref, bf16[64,128]{1,0:T(8,128)(2,1)S(1)} %bitcast.5, bf16[2,2,128]{2,1,0:T(2,128)(2,1)S(1)} %bitcast.6, bf16[2,2,128]{2,1,0:T(2,128)(2,1)S(1)} %bitcast.7), custom_call_target="tpu_custom_call" | custom-call | tf_op jit(solution)/shard_map/pallas_call | solution.py:273
  (11 shorter events, 0.0 us)
Async XLA Ops:
  0.0 13.8 %collective-permute-start = (bf16[16,128,8,128]{3,2,1,0:T(8,128)(2,1)}, bf16[16,128,8,128]{3,2,1,0:T(8,128)(2,1)}, u32[]{:S(2)}, u32[]{:S(2)}) collective-permute-start(bf16[16,128,8,128]{3,2,1,0:T(8,128)(2,1)} %refs_0_.1), channel_id=1, source_target_pairs={{0,4},{4,0},{8,12},{12,8},{16,20},{20,16},{24,28},{28,24},{32,36},... | collective-permute-start | bytes 12582920 | tf_op jit(solution)/shard_map/ppermute | solution.py:294
  0.0 13.8 %collective-permute-start.1 = (bf16[16,128,8,128]{3,2,1,0:T(8,128)(2,1)}, bf16[16,128,8,128]{3,2,1,0:T(8,128)(2,1)}, u32[]{:S(2)}, u32[]{:S(2)}) collective-permute-start(bf16[16,128,8,128]{3,2,1,0:T(8,128)(2,1)} %refs_2_.1), channel_id=1, source_target_pairs={{0,4},{4,0},{8,12},{12,8},{16,20},{20,16},{24,28},{28,24},{32,36},... | collective-permute-start | bytes 12582920 | tf_op jit(solution)/shard_map/ppermute | solution.py:294
  0.5 0.7 copy-start
  2.1 28.6 %all-to-all-start = ((bf16[32,64,128]{2,1,0:T(8,128)(2,1)}), bf16[32,64,128]{2,1,0:T(8,128)(2,1)S(1)}, u32[]{:S(2)}, u32[]{:S(2)}) async-start(bf16[32,64,128]{2,1,0:T(8,128)(2,1)} %get-tuple-element.27), calls=%async_computation | async-start | bytes 1048576 | tf_op jit(solution)/shard_map/all_to_all | solution.py:284
  13.8 20.2 %copy-start.4 = (s32[64]{0:T(128)S(1)}, s32[64]{0:T(128)}, u32[]{:S(2)}) copy-start(s32[64]{0:T(128)} %order.3) | copy-start | bytes 772
  24.6 17.3 %copy-start.8 = (bf16[8,8,128,128]{3,2,1,0:T(8,128)(2,1)S(1)}, bf16[8,8,128,128]{3,2,1,0:T(8,128)(2,1)}, u32[]{:S(2)}) copy-start(bf16[8,8,128,128]{3,2,1,0:T(8,128)(2,1)} %get-tuple-element.31.cache_ref) | copy-start | bytes 6291460
  24.6 17.3 %copy-start.9 = (s32[64]{0:T(128)S(1)}, s32[64]{0:T(128)}, u32[]{:S(2)}) copy-start(s32[64]{0:T(128)} %lens.7) | copy-start | bytes 772
  32.0 12.6 %copy-start.7 = (bf16[8,8,128,128]{3,2,1,0:T(8,128)(2,1)S(1)}, bf16[8,8,128,128]{3,2,1,0:T(8,128)(2,1)}, u32[]{:S(2)}) copy-start(bf16[8,8,128,128]{3,2,1,0:T(8,128)(2,1)} %get-tuple-element.34.cache_ref) | copy-start | bytes 6291460
  32.0 2.0 %collective-permute-start.2 = (bf16[32,64,128]{2,1,0:T(8,128)(2,1)S(1)}, bf16[32,64,128]{2,1,0:T(8,128)(2,1)S(1)}, u32[]{:S(2)}, u32[]{:S(2)}) collective-permute-start(bf16[32,64,128]{2,1,0:T(8,128)(2,1)S(1)} %get-tuple-element.29), channel_id=1, source_target_pairs={{0,4},{4,0},{8,12},{12,8},{16,20},{20,16},{24,28},{28,24},{32,36},... | collective-permute-start | bytes 1572872 | tf_op jit(solution)/shard_map/ppermute | solution.py:294
  34.9 12.5 %copy-start.6 = (bf16[8,8,128,128]{3,2,1,0:T(8,128)(2,1)S(1)}, bf16[8,8,128,128]{3,2,1,0:T(8,128)(2,1)}, u32[]{:S(2)}) copy-start(bf16[8,8,128,128]{3,2,1,0:T(8,128)(2,1)} %get-tuple-element.37.cache_ref) | copy-start | bytes 6291460
  35.0 6.9 %collective-permute-start.3 = (bf16[8,64,128]{2,1,0:T(8,128)(2,1)S(1)}, bf16[8,64,128]{2,1,0:T(8,128)(2,1)S(1)}, u32[]{:S(2)}, u32[]{:S(2)}) collective-permute-start(bf16[8,64,128]{2,1,0:T(8,128)(2,1)S(1)} %get-tuple-element.30), channel_id=1, source_target_pairs={{0,1},{1,2},{2,3},{3,0},{4,5},{5,6},{6,7},{7,4},{8,9},{9,10},{10,1... | collective-permute-start | bytes 393224 | tf_op jit(solution)/shard_map/ppermute | solution.py:290
  36.6 8.0 %collective-permute-start.4 = (bf16[8,64,128]{2,1,0:T(8,128)(2,1)S(1)}, bf16[8,64,128]{2,1,0:T(8,128)(2,1)S(1)}, u32[]{:S(2)}, u32[]{:S(2)}) collective-permute-start(bf16[8,64,128]{2,1,0:T(8,128)(2,1)S(1)} %get-tuple-element.33), channel_id=1, source_target_pairs={{0,3},{1,0},{2,1},{3,2},{4,7},{5,4},{6,5},{7,6},{8,11},{9,8},{10,9... | collective-permute-start | bytes 393224 | tf_op jit(solution)/shard_map/ppermute | solution.py:290
  38.3 9.2 %collective-permute-start.5 = (bf16[8,64,128]{2,1,0:T(8,128)(2,1)S(1)}, bf16[8,64,128]{2,1,0:T(8,128)(2,1)S(1)}, u32[]{:S(2)}, u32[]{:S(2)}) collective-permute-start(bf16[8,64,128]{2,1,0:T(8,128)(2,1)S(1)} %get-tuple-element.36), channel_id=1, source_target_pairs={{0,2},{1,3},{2,0},{3,1},{4,6},{5,7},{6,4},{7,5},{8,10},{9,11},{10,... | collective-permute-start | bytes 393224 | tf_op jit(solution)/shard_map/ppermute | solution.py:290
  44.6 10.9 %copy-start.5 = (bf16[8,8,128,128]{3,2,1,0:T(8,128)(2,1)S(1)}, bf16[8,8,128,128]{3,2,1,0:T(8,128)(2,1)}, u32[]{:S(2)}) copy-start(bf16[8,8,128,128]{3,2,1,0:T(8,128)(2,1)} %get-tuple-element.40.cache_ref) | copy-start | bytes 6291460
  50.2 37.3 %copy-start.1 = (bf16[1,2,32,128]{3,2,1,0:T(8,128)(2,1)S(1)}, bf16[1,2,32,128]{3,2,1,0:T(8,128)(2,1)}, u32[]{:S(2)}) copy-start(bf16[1,2,32,128]{3,2,1,0:T(8,128)(2,1)} %param.7) | copy-start | bytes 49156
  50.3 37.3 %copy-start.2 = (bf16[1,2,2,128]{3,2,1,0:T(2,128)(2,1)S(1)}, bf16[1,2,2,128]{3,2,1,0:T(2,128)(2,1)}, u32[]{:S(2)}) copy-start(bf16[1,2,2,128]{3,2,1,0:T(2,128)(2,1)} %param.8) | copy-start | bytes 3076
  50.3 37.3 %copy-start.3 = (bf16[1,2,2,128]{3,2,1,0:T(2,128)(2,1)S(1)}, bf16[1,2,2,128]{3,2,1,0:T(2,128)(2,1)}, u32[]{:S(2)}) copy-start(bf16[1,2,2,128]{3,2,1,0:T(2,128)(2,1)} %param.9) | copy-start | bytes 3076
  50.3 8.3 %collective-permute-start.7 = (bf16[8,72,128]{2,1,0:T(8,128)(2,1)S(1)}, bf16[8,72,128]{2,1,0:T(8,128)(2,1)S(1)}, u32[]{:S(2)}, u32[]{:S(2)}) collective-permute-start(bf16[8,72,128]{2,1,0:T(8,128)(2,1)S(1)} %get-tuple-element.43), channel_id=1, source_target_pairs={{0,2},{1,3},{2,0},{3,1},{4,6},{5,7},{6,4},{7,5},{8,10},{9,11},{10,... | collective-permute-start | bytes 442376 | tf_op jit(solution)/shard_map/ppermute | solution.py:290
  52.3 7.9 %collective-permute-start.8 = (bf16[8,72,128]{2,1,0:T(8,128)(2,1)S(1)}, bf16[8,72,128]{2,1,0:T(8,128)(2,1)S(1)}, u32[]{:S(2)}, u32[]{:S(2)}) collective-permute-start(bf16[8,72,128]{2,1,0:T(8,128)(2,1)S(1)} %get-tuple-element.44), channel_id=1, source_target_pairs={{0,1},{1,2},{2,3},{3,0},{4,5},{5,6},{6,7},{7,4},{8,9},{9,10},{10,1... | collective-permute-start | bytes 442376 | tf_op jit(solution)/shard_map/ppermute | solution.py:290
  54.2 5.9 %collective-permute-start.6 = (bf16[8,72,128]{2,1,0:T(8,128)(2,1)S(1)}, bf16[8,72,128]{2,1,0:T(8,128)(2,1)S(1)}, u32[]{:S(2)}, u32[]{:S(2)}) collective-permute-start(bf16[8,72,128]{2,1,0:T(8,128)(2,1)S(1)} %get-tuple-element.42), channel_id=1, source_target_pairs={{0,3},{1,0},{2,1},{3,2},{4,7},{5,4},{6,5},{7,6},{8,11},{9,8},{10,9... | collective-permute-start | bytes 442376 | tf_op jit(solution)/shard_map/ppermute | solution.py:290
  58.2 2.5 %collective-permute-start.9 = (bf16[8,72,128]{2,1,0:T(8,128)(2,1)S(1)}, bf16[8,72,128]{2,1,0:T(8,128)(2,1)S(1)}, u32[]{:S(2)}, u32[]{:S(2)}) collective-permute-start(bf16[8,72,128]{2,1,0:T(8,128)(2,1)S(1)} %get-tuple-element.41.refs_0_), channel_id=1, source_target_pairs={{0,4},{4,0},{8,12},{12,8},{16,20},{20,16},{24,28},{28,24},{32,36},... | collective-permute-start | bytes 442376 | tf_op jit(solution)/shard_map/ppermute | solution.py:294
  58.6 2.1 %collective-permute-start.11 = (bf16[8,72,128]{2,1,0:T(8,128)(2,1)S(1)}, bf16[8,72,128]{2,1,0:T(8,128)(2,1)S(1)}, u32[]{:S(2)}, u32[]{:S(2)}) collective-permute-start(bf16[8,72,128]{2,1,0:T(8,128)(2,1)S(1)} %collective-permute-done.7.refs_2_), channel_id=1, source_target_pairs={{0,4},{4,0},{8,12},{12,8},{16,20},{20,16},{24,28},{28,24},{32,36},... | collective-permute-start | bytes 442376 | tf_op jit(solution)/shard_map/ppermute | solution.py:294
  60.2 1.4 %collective-permute-start.12 = (bf16[8,72,128]{2,1,0:T(8,128)(2,1)S(1)}, bf16[8,72,128]{2,1,0:T(8,128)(2,1)S(1)}, u32[]{:S(2)}, u32[]{:S(2)}) collective-permute-start(bf16[8,72,128]{2,1,0:T(8,128)(2,1)S(1)} %collective-permute-done.8.refs_3_), channel_id=1, source_target_pairs={{0,4},{4,0},{8,12},{12,8},{16,20},{20,16},{24,28},{28,24},{32,36},... | collective-permute-start | bytes 442376 | tf_op jit(solution)/shard_map/ppermute | solution.py:294
  60.2 1.6 %collective-permute-start.10 = (bf16[8,72,128]{2,1,0:T(8,128)(2,1)S(1)}, bf16[8,72,128]{2,1,0:T(8,128)(2,1)S(1)}, u32[]{:S(2)}, u32[]{:S(2)}) collective-permute-start(bf16[8,72,128]{2,1,0:T(8,128)(2,1)S(1)} %collective-permute-done.6.refs_1_), channel_id=1, source_target_pairs={{0,4},{4,0},{8,12},{12,8},{16,20},{20,16},{24,28},{28,24},{32,36},... | collective-permute-start | bytes 442376 | tf_op jit(solution)/shard_map/ppermute | solution.py:294

commit v2 on v1

--- a/solution.py
+++ b/solution.py
@@ -10,6 +10,7 @@
 CHIPS = 32
 GROUP = 16
 ROWS = 8
+HALF = 4
 LINES = 64
 TAIL = 8
 BLOCK = LINES + TAIL
@@ -136,25 +137,25 @@
     return outs[:NY], outs[NY]
 
 
-def attend_kernel(lens, token, q_ref, cache_ref, out_ref, token_out):
-    rows, _, size, half = cache_ref.shape
+def attend_rows(base, lens, q_ref, cache_ref, out_ref):
+    _, _, size, half = cache_ref.shape
     positions = 2 * half
     scale = size ** (-0.5)
-    token_out[0] = token[0]
     chip, core, group = coordinates()
-    first = (group * NC + core) * ROWS
+    first = (group * NC + core) * ROWS + base
     at = lax.broadcasted_iota(jnp.int32, (1, positions), 1)
     own = (chip * NC + core) * half
     other = (chip * NC + 1 - core) * half - half
     start = jnp.where(at < half, own, other)
     stats = [[], [], [], []]
-    for j in range(rows):
+    for j in range(HALF):
         valid = at < lens[first + j] - start
+        row = base + j
         weights, pairs = [], []
         for k in range(2):
             lines = [slice(t * 32 + k * GROUP, t * 32 + (k + 1) * GROUP) for t in range(2)]
-            q = jnp.concatenate([q_ref[j, part, :] for part in lines], 0)
-            keys = jnp.concatenate([cache_ref[j, k], cache_ref[j, 2 + k]], 1)
+            q = jnp.concatenate([q_ref[row, part, :] for part in lines], 0)
+            keys = jnp.concatenate([cache_ref[row, k], cache_ref[row, 2 + k]], 1)
             scores = jnp.dot(q, keys, preferred_element_type=F32) * scale
             scores = jnp.where(valid, scores, NEG_FILL)
             high, low = split_pair(jnp.max(scores, 1, keepdims=True))
@@ -163,7 +164,7 @@
             weights.append(weight.astype(BF16))
         values = jnp.concatenate(
             [
-                jnp.concatenate([cache_ref[j, 4 + 2 * i], cache_ref[j, 5 + 2 * i]], 1)
+                jnp.concatenate([cache_ref[row, 4 + 2 * i], cache_ref[row, 5 + 2 * i]], 1)
                 for i in range(2)
             ],
             0,
@@ -173,30 +174,48 @@
             for k in range(2):
                 line = t * 32 + k * GROUP
                 part = o[k * 32 + t * GROUP : k * 32 + (t + 1) * GROUP, k * size : (k + 1) * size]
-                out_ref[j, line : line + GROUP, :] = part.astype(BF16)
+                out_ref[row, line : line + GROUP, :] = part.astype(BF16)
                 for i in range(4):
                     stats[i].append(pairs[k][i][t * GROUP : (t + 1) * GROUP])
     stats = [jnp.concatenate(stat, 0) for stat in stats]
-    lane = lax.broadcasted_iota(jnp.int32, (rows * LINES, 128), 1)
+    lane = lax.broadcasted_iota(jnp.int32, (HALF * LINES, 128), 1)
     table = jnp.where(lane == 0, stats[0], 0.0)
     for i in range(1, 4):
         table = jnp.where(lane == i, stats[i], table)
     table = table.T[:TAIL]
-    for j in range(rows):
+    for j in range(HALF):
         tail = table[:, (j // 2) * 128 : (j // 2 + 1) * 128]
         if j % 2 == 1:
             tail = pltpu.roll(tail, LINES, 1)
-        out_ref[j, LINES:, :] = tail.astype(BF16)
-
-
-def attend(lens, token, queries, cache):
+        out_ref[base + j, LINES:, :] = tail.astype(BF16)
+
+
+def attend(lens, token, queries, cache, count=ROWS, done=None):
     rows, _, size, positions = cache.shape
-    return pl.pallas_call(
-        attend_kernel,
-        in_specs=[SMEM] * 2 + [VMEM] * 2,
+    before = [] if done is None else [done]
+
+    def kernel(lens, token, q_ref, cache_ref, *refs):
+        out_ref, token_out = refs[-2:]
+        token_out[0] = token[0]
+        if before:
+            out_ref[:HALF] = refs[0][...]
+            attend_rows(HALF, lens, q_ref, cache_ref, out_ref)
+        elif count == HALF:
+            attend_rows(0, lens, q_ref, cache_ref, out_ref)
+        else:
+
+            def step(i, carry):
+                attend_rows(i * HALF, lens, q_ref, cache_ref, out_ref)
+                return carry
+
+            lax.fori_loop(0, ROWS // HALF, step, 0)
+
+    return pl.pallas_call(
+        kernel,
+        in_specs=[SMEM] * 2 + [VMEM] * (2 + len(before)),
         out_specs=[VMEM, SMEM],
         out_shape=[
-            jax.ShapeDtypeStruct((rows, BLOCK, size), BF16),
+            jax.ShapeDtypeStruct((count, BLOCK, size), BF16),
             jax.ShapeDtypeStruct((1,), jnp.int32),
         ],
         compiler_params=PARAMS,
@@ -205,7 +224,7 @@
             bytes_accessed=160 * ROWS * positions * size,
             transcendentals=0,
         ),
-    )(lens, token, queries, cache)
+    )(lens, token, queries, cache, *before)
 
 
 def to_owners_kernel(order, *refs):
@@ -306,12 +325,13 @@
     passed, token = pass_on(token, got)
     sends = to_groups(decode_order, got, to_other_core(passed))
 
+    gots = {d: along_kvh(sends[d], d) for d in (1, 3, 2)}
+    half, token = attend(cache_len, token, sends[0], caches[0], count=HALF)
     parts = [None] * NY
-    near = (1, 3, 2, 0)
-    gots = {d: along_kvh(sends[d], d) if d else sends[d] for d in near}
-    for d in near:
-        part, token = attend(cache_len, token, gots[d], caches[d])
-        parts[d] = along_kvh(part, NY - d) if d else part
+    for d in (1, 3, 2):
+        part, _ = attend(cache_len, token, gots[d], caches[d])
+        parts[d] = along_kvh(part, NY - d)
+    parts[0], _ = attend(cache_len, token, sends[0], caches[0], done=half)
 
     part = over_chips(to_owners(decode_order, parts, [to_other_core(part) for part in parts]))
     out = finish(part, own, new_keys[0], new_values[0])

time: 89.4 us -> 89.8 us (level)
  Pallas kernels: 27.7 us -> 30.4 us
  waiting for transfers between devices: 12.3 us -> 10.8 us
    pallas_call x4 -> x5, Pallas kernels: 11 us -> 13.7 us  [attend(): pl.pallas_call(kernel, in_specs=[SMEM] * 2 + [VMEM] * (2 + len(before)),...]
    ppermute x6, waiting for transfers between devices: 3.22 us -> 1.39 us  [along_kvh(): return lax.ppermute(x, 'kvh', [(y, (y + d) % NY) for y in range(NY)])]
  transfers between devices with their start and end apart: 14 -> 14, of which waited for: 7 -> 4; matrix products, arithmetic and copies ran while one was open for 0% -> 0% of each run, Pallas kernels for 22% -> 28%
where the time goes in v2:
time: 89.8 us; the launch traced here: 89.3 us
  Pallas kernels  30.4 us (34%)
  blocking collectives  24.1 us (27%)
  starting transfers between devices  23 us (26%)
  waiting for transfers between devices  10.8 us (12%)
    all_to_all x1, blocking collectives, over_chips(): lax.all_to_all(x, 'seq', split_axis=0, concat_axis=0, axis_index_groups=g...  24.1 us
    pallas_call x5, Pallas kernels, attend(): pl.pallas_call(kernel, in_specs=[SMEM] * 2 + [VMEM] * (2 + len(before)),...  13.7 us
    all_to_all x1, starting transfers between devices, over_chips(): lax.all_to_all(x, 'seq', split_axis=0, concat_axis=0, axis_index_groups=g...  11.6 us
    pallas_call x1, Pallas kernels, by_head(): pl.pallas_call(by_head_kernel, grid_spec=pltpu.PrefetchScalarGridSpec(num...  10.8 us
    ppermute x6, starting transfers between devices, along_kvh(): return lax.ppermute(x, 'kvh', [(y, (y + d) % NY) for y in range(NY)])  10.1 us
    all_to_all x1, waiting for transfers between devices, over_chips(): lax.all_to_all(x, 'seq', split_axis=0, concat_axis=0, axis_index_groups=g...  6.13 us
    ppermute x7, waiting for transfers between devices, to_other_core(): return lax.ppermute(x, 'seq', [(i, i ^ 1) for i in range(CHIPS * NC)])  3.26 us
  transfers between devices with their start and end apart: 14, of which 4 were waited for; matrix products, arithmetic and copies ran while one was open for 0% of the time, Pallas kernels for 28%

profile of v2, /device:TPU:2, one launch (start us, length us, event | category | flops | bytes accessed | tf_op | source)
XLA Modules:
  0.0 89.3 jit_solution(14308829728880373203)
XLA Ops:
  0.0 0.0 collective-permute-start
  0.0 0.5 collective-permute-start.1
  0.5 0.7 copy-done
  1.2 0.9 shard_map.73
  2.1 11.6 %all-to-all-start = ((bf16[32,64,128]{2,1,0:T(8,128)(2,1)}), bf16[32,64,128]{2,1,0:T(8,128)(2,1)S(1)}, u32[]{:S(2)}, u32[]{:S(2)}) async-start(bf16[32,64,128]{2,1,0:T(8,128)(2,1)} %get-tuple-element.26), calls=%async_computation | async-start | bytes 1048576 | tf_op jit(solution)/shard_map/all_to_all | solution.py:303
  13.7 0.0 collective-permute-done.refs_1_
  13.7 0.0 collective-permute-done.1.refs_3_
  13.8 0.0 copy-start.4
  13.8 10.8 %shard_map.74 = (bf16[8,8,128,128]{3,2,1,0:T(8,128)(2,1)}, bf16[8,8,128,128]{3,2,1,0:T(8,128)(2,1)}, bf16[8,8,128,128]{3,2,1,0:T(8,128)(2,1)}, bf16[8,8,128,128]{3,2,1,0:T(8,128)(2,1)}, s32[1]{0:T(128)}) custom-call(s32[1]{0:T(128)} %get-tuple-element.24.core, bf16[16,128,8,128]{3,2,1,0:T(8,128)(2,1)} %refs_0_.1, ...), custom_call_target="tpu_custom_call" | custom-call | bytes 16777216 | tf_op jit(solution)/shard_map/pallas_call | solution.py:122
  24.6 0.0 copy-start.9
  24.6 6.1 %all-to-all-done.got_ref.own_ref = bf16[32,64,128]{2,1,0:T(8,128)(2,1)S(1)} async-done(((bf16[32,64,128]{2,1,0:T(8,128)(2,1)}), bf16[32,64,128]{2,1,0:T(8,128)(2,1)S(1)}, u32[]{:S(2)}, u32[]{:S(2)}) %all-to-all-start) | async-done | bytes 524320 | tf_op jit(solution)/shard_map/all_to_all | solution.py:303
  30.7 1.2 %shard_map.75 = (bf16[32,64,128]{2,1,0:T(8,128)(2,1)S(1)}, s32[1]{0:T(128)}) custom-call(s32[1]{0:T(128)} %get-tuple-element.25.token, bf16[32,64,128]{2,1,0:T(8,128)(2,1)S(1)} %all-to-all-done.got_ref.own_ref), custom_call_target="tpu_custom_call" | custom-call | flops 1073741824 | bytes 16777216 | tf_op jit(solution)/shard_map/pallas_call | solution.py:61
  31.9 0.0 copy-start.8
  31.9 0.1 collective-permute-start.2
  32.0 1.9 %collective-permute-done.2.other_ref = bf16[32,64,128]{2,1,0:T(8,128)(2,1)S(1)} collective-permute-done((bf16[32,64,128]{2,1,0:T(8,128)(2,1)S(1)}, bf16[32,64,128]{2,1,0:T(8,128)(2,1)S(1)}, u32[]{:S(2)}, u32[]{:S(2)}) %collective-permute-start.2) | collective-permute-done | bytes 524320 | tf_op jit(solution)/shard_map/ppermute | solution.py:313
  33.9 0.9 %shard_map.76 = (bf16[8,64,128]{2,1,0:T(8,128)(2,1)S(1)}, bf16[8,64,128]{2,1,0:T(8,128)(2,1)S(1)}, bf16[8,64,128]{2,1,0:T(8,128)(2,1)S(1)}, bf16[8,64,128]{2,1,0:T(8,128)(2,1)S(1)}) custom-call(s32[64]{0:T(128)S(1)} %copy-done.4, bf16[32,64,128]{2,1,0:T(8,128)(2,1)S(1)} %all-to-all-done.got_ref.own_ref, bf16[32,64,128]{2,1,0:T(8,128)(2,1)S(1)} %collective-permute-done.2.other_ref), custom_call_target="tpu_custom_call" | custom-call | flops 1073741824 | bytes 16777216 | tf_op jit(solution)/shard_map/pallas_call | solution.py:90
  34.9 3.1 %collective-permute-start.7 = (bf16[8,64,128]{2,1,0:T(8,128)(2,1)S(1)}, bf16[8,64,128]{2,1,0:T(8,128)(2,1)S(1)}, u32[]{:S(2)}, u32[]{:S(2)}) collective-permute-start(bf16[8,64,128]{2,1,0:T(8,128)(2,1)S(1)} %get-tuple-element.40), channel_id=1, source_target_pairs={{0,3},{1,0},{2,1},{3,2},{4,7},{5,4},{6,5},{7,6},{8,11},{9,8},{10,9... | collective-permute-start | bytes 393224 | tf_op jit(solution)/shard_map/ppermute | solution.py:309
  38.0 0.0 collective-permute-start.3
  38.0 2.2 %collective-permute-start.5 = (bf16[8,64,128]{2,1,0:T(8,128)(2,1)S(1)}, bf16[8,64,128]{2,1,0:T(8,128)(2,1)S(1)}, u32[]{:S(2)}, u32[]{:S(2)}) collective-permute-start(bf16[8,64,128]{2,1,0:T(8,128)(2,1)S(1)} %get-tuple-element.37), channel_id=1, source_target_pairs={{0,2},{1,3},{2,0},{3,1},{4,6},{5,7},{6,4},{7,5},{8,10},{9,11},{10,... | collective-permute-start | bytes 393224 | tf_op jit(solution)/shard_map/ppermute | solution.py:309
  40.2 0.0 copy-done.9
  40.2 2.1 %shard_map.77 = (bf16[4,72,128]{2,1,0:T(8,128)(2,1)S(1)}, s32[1]{0:T(128)}) custom-call(s32[64]{0:T(128)S(1)} %copy-done.9, s32[1]{0:T(128)} %get-tuple-element.27.token, bf16[8,64,128]{2,1,0:T(8,128)(2,1)S(1)} %get-tuple-element.29.q_ref, bf16[8,8,128,128]{3,2,1,0:T(8,128)(2,1)S(1)} %copy-done.5), custom_call_target="tpu_custom_call" | custom-call | flops 1006632960 | bytes 20971520 | tf_op jit(solution)/shard_map/pallas_call | solution.py:213
  42.3 0.0 collective-permute-done.7.q_ref
  42.4 3.2 %shard_map.81 = (bf16[8,72,128]{2,1,0:T(8,128)(2,1)S(1)}, s32[1]{0:T(128)}) custom-call(s32[64]{0:T(128)S(1)} %copy-done.9, s32[1]{0:T(128)} %get-tuple-element.31.token, bf16[8,64,128]{2,1,0:T(8,128)(2,1)S(1)} %collective-permute-done.7.q_ref, bf16[8,8,128,128]{3,2,1,0:T(8,128)(2,1)S(1)} %copy-done.8), custom_call_target="tpu_custom_call" | custom-call | flops 1006632960 | bytes 20971520 | tf_op jit(solution)/shard_map/pallas_call | solution.py:213
  45.6 2.0 %collective-permute-start.8 = (bf16[8,72,128]{2,1,0:T(8,128)(2,1)S(1)}, bf16[8,72,128]{2,1,0:T(8,128)(2,1)S(1)}, u32[]{:S(2)}, u32[]{:S(2)}) collective-permute-start(bf16[8,72,128]{2,1,0:T(8,128)(2,1)S(1)} %get-tuple-element.42), channel_id=1, source_target_pairs={{0,1},{1,2},{2,3},{3,0},{4,5},{5,6},{6,7},{7,4},{8,9},{9,10},{10,1... | collective-permute-start | bytes 442376 | tf_op jit(solution)/shard_map/ppermute | solution.py:309
  47.6 0.0 collective-permute-done.5.q_ref
  47.6 3.1 %shard_map.80 = (bf16[8,72,128]{2,1,0:T(8,128)(2,1)S(1)}, s32[1]{0:T(128)}) custom-call(s32[64]{0:T(128)S(1)} %copy-done.9, s32[1]{0:T(128)} %get-tuple-element.31.token, bf16[8,64,128]{2,1,0:T(8,128)(2,1)S(1)} %collective-permute-done.5.q_ref, bf16[8,8,128,128]{3,2,1,0:T(8,128)(2,1)S(1)} %copy-done.7), custom_call_target="tpu_custom_call" | custom-call | flops 1006632960 | bytes 20971520 | tf_op jit(solution)/shard_map/pallas_call | solution.py:213
  50.7 1.9 %collective-permute-start.6 = (bf16[8,72,128]{2,1,0:T(8,128)(2,1)S(1)}, bf16[8,72,128]{2,1,0:T(8,128)(2,1)S(1)}, u32[]{:S(2)}, u32[]{:S(2)}) collective-permute-start(bf16[8,72,128]{2,1,0:T(8,128)(2,1)S(1)} %get-tuple-element.39), channel_id=1, source_target_pairs={{0,2},{1,3},{2,0},{3,1},{4,6},{5,7},{6,4},{7,5},{8,10},{9,11},{10,... | collective-permute-start | bytes 442376 | tf_op jit(solution)/shard_map/ppermute | solution.py:309
  52.5 0.0 collective-permute-done.3.q_ref
  52.5 3.1 %shard_map.79 = (bf16[8,72,128]{2,1,0:T(8,128)(2,1)S(1)}, s32[1]{0:T(128)}) custom-call(s32[64]{0:T(128)S(1)} %copy-done.9, s32[1]{0:T(128)} %get-tuple-element.31.token, bf16[8,64,128]{2,1,0:T(8,128)(2,1)S(1)} %collective-permute-done.3.q_ref, bf16[8,8,128,128]{3,2,1,0:T(8,128)(2,1)S(1)} %copy-done.6), custom_call_target="tpu_custom_call" | custom-call | flops 1006632960 | bytes 20971520 | tf_op jit(solution)/shard_map/pallas_call | solution.py:213
  55.6 0.0 copy-start.1
  55.6 0.0 copy-start.2
  55.7 0.0 copy-start.3
  55.7 1.0 %collective-permute-start.4 = (bf16[8,72,128]{2,1,0:T(8,128)(2,1)S(1)}, bf16[8,72,128]{2,1,0:T(8,128)(2,1)S(1)}, u32[]{:S(2)}, u32[]{:S(2)}) collective-permute-start(bf16[8,72,128]{2,1,0:T(8,128)(2,1)S(1)} %get-tuple-element.36), channel_id=1, source_target_pairs={{0,3},{1,0},{2,1},{3,2},{4,7},{5,4},{6,5},{7,6},{8,11},{9,8},{10,9... | collective-permute-start | bytes 442376 | tf_op jit(solution)/shard_map/ppermute | solution.py:309
  56.7 2.1 %shard_map.78 = (bf16[8,72,128]{2,1,0:T(8,128)(2,1)S(1)}, s32[1]{0:T(128)}) custom-call(s32[64]{0:T(128)S(1)} %copy-done.9, s32[1]{0:T(128)} %get-tuple-element.31.token, bf16[8,64,128]{2,1,0:T(8,128)(2,1)S(1)} %get-tuple-element.29.q_ref, bf16[8,8,128,128]{3,2,1,0:T(8,128)(2,1)S(1)} %copy-done.5, bf16[4,72,128]{2,1,0:T(8,128)(2,1)S(1)} %get-tuple-element.32.refs_0_), custom_call_target="tpu_custom_call" | custom-call | flops 1006632960 | bytes 20971520 | tf_op jit(solution)/shard_map/pallas_call | solution.py:213
  58.8 0.1 collective-permute-start.9
  58.9 0.0 collective-permute-done.8.refs_3_
  58.9 0.5 collective-permute-start.12
  59.4 0.0 collective-permute-done.6.refs_2_
  59.4 0.1 collective-permute-start.11
  59.5 1.4 %collective-permute-done.4.refs_1_ = bf16[8,72,128]{2,1,0:T(8,128)(2,1)S(1)} collective-permute-done((bf16[8,72,128]{2,1,0:T(8,128)(2,1)S(1)}, bf16[8,72,128]{2,1,0:T(8,128)(2,1)S(1)}, u32[]{:S(2)}, u32[]{:S(2)}) %collective-permute-start.4) | collective-permute-done | bytes 147488 | tf_op jit(solution)/shard_map/ppermute | solution.py:309
  60.9 0.0 collective-permute-start.10
  60.9 0.0 collective-permute-done.9.refs_4_
  60.9 0.0 collective-permute-done.12.refs_7_
  60.9 0.0 collective-permute-done.11.refs_6_
  60.9 1.3 %collective-permute-done.10.refs_5_ = bf16[8,72,128]{2,1,0:T(8,128)(2,1)S(1)} collective-permute-done((bf16[8,72,128]{2,1,0:T(8,128)(2,1)S(1)}, bf16[8,72,128]{2,1,0:T(8,128)(2,1)S(1)}, u32[]{:S(2)}, u32[]{:S(2)}) %collective-permute-start.10) | collective-permute-done | bytes 147488 | tf_op jit(solution)/shard_map/ppermute | solution.py:313
  62.3 1.5 %shard_map.82 = bf16[32,72,128]{2,1,0:T(8,128)(2,1)S(1)} custom-call(s32[64]{0:T(128)S(1)} %copy-done.4, bf16[8,72,128]{2,1,0:T(8,128)(2,1)S(1)} %get-tuple-element.33.refs_0_, bf16[8,72,128]{2,1,0:T(8,128)(2,1)S(1)} %collective-permute-done.4.refs_1_, bf16[8,72,128]{2,1,0:T(8,128)(2,1)S(1)} %collective-permute-done.6.refs_2_, ...), custom_call_target="tpu_custom_call" | custom-call | tf_op jit(solution)/shard_map/pallas_call | solution.py:247
  63.8 24.1 %all_to_all.10.part_ref = bf16[32,72,128]{2,1,0:T(8,128)(2,1)S(1)} all-to-all(bf16[32,72,128]{2,1,0:T(8,128)(2,1)S(1)} %shard_map.82), channel_id=1, replica_groups={{0,8,16,24,32,40,48,56,64,72,80,88,96,104,112,120,128,136,144,152,160,1..., dimensions={0} | all-to-all | bytes 1179648 | tf_op jit(solution)/shard_map/all_to_all | solution.py:303
  87.9 1.4 %shard_map.83 = bf16[64,128]{1,0:T(8,128)(2,1)} custom-call(bf16[32,72,128]{2,1,0:T(8,128)(2,1)S(1)} %all_to_all.10.part_ref, bf16[64,128]{1,0:T(8,128)(2,1)S(1)} %bitcast.5, bf16[2,2,128]{2,1,0:T(2,128)(2,1)S(1)} %bitcast.6, bf16[2,2,128]{2,1,0:T(2,128)(2,1)S(1)} %bitcast.7), custom_call_target="tpu_custom_call" | custom-call | tf_op jit(solution)/shard_map/pallas_call | solution.py:292
  (12 shorter events, 0.0 us)
Async XLA Ops:
  0.0 13.7 %collective-permute-start = (bf16[16,128,8,128]{3,2,1,0:T(8,128)(2,1)}, bf16[16,128,8,128]{3,2,1,0:T(8,128)(2,1)}, u32[]{:S(2)}, u32[]{:S(2)}) collective-permute-start(bf16[16,128,8,128]{3,2,1,0:T(8,128)(2,1)} %refs_0_.1), channel_id=1, source_target_pairs={{0,4},{4,0},{8,12},{12,8},{16,20},{20,16},{24,28},{28,24},{32,36},... | collective-permute-start | bytes 12582920 | tf_op jit(solution)/shard_map/ppermute | solution.py:313
  0.0 13.7 %collective-permute-start.1 = (bf16[16,128,8,128]{3,2,1,0:T(8,128)(2,1)}, bf16[16,128,8,128]{3,2,1,0:T(8,128)(2,1)}, u32[]{:S(2)}, u32[]{:S(2)}) collective-permute-start(bf16[16,128,8,128]{3,2,1,0:T(8,128)(2,1)} %refs_2_.1), channel_id=1, source_target_pairs={{0,4},{4,0},{8,12},{12,8},{16,20},{20,16},{24,28},{28,24},{32,36},... | collective-permute-start | bytes 12582920 | tf_op jit(solution)/shard_map/ppermute | solution.py:313
  0.5 0.7 copy-start
  2.1 28.6 %all-to-all-start = ((bf16[32,64,128]{2,1,0:T(8,128)(2,1)}), bf16[32,64,128]{2,1,0:T(8,128)(2,1)S(1)}, u32[]{:S(2)}, u32[]{:S(2)}) async-start(bf16[32,64,128]{2,1,0:T(8,128)(2,1)} %get-tuple-element.26), calls=%async_computation | async-start | bytes 1048576 | tf_op jit(solution)/shard_map/all_to_all | solution.py:303
  13.8 20.2 %copy-start.4 = (s32[64]{0:T(128)S(1)}, s32[64]{0:T(128)}, u32[]{:S(2)}) copy-start(s32[64]{0:T(128)} %order.3) | copy-start | bytes 772
  24.6 15.6 %copy-start.5 = (bf16[8,8,128,128]{3,2,1,0:T(8,128)(2,1)S(1)}, bf16[8,8,128,128]{3,2,1,0:T(8,128)(2,1)}, u32[]{:S(2)}) copy-start(bf16[8,8,128,128]{3,2,1,0:T(8,128)(2,1)} %get-tuple-element.30.cache_ref) | copy-start | bytes 6291460
  24.6 15.6 %copy-start.9 = (s32[64]{0:T(128)S(1)}, s32[64]{0:T(128)}, u32[]{:S(2)}) copy-start(s32[64]{0:T(128)} %lens.9) | copy-start | bytes 772
  31.9 10.4 %copy-start.8 = (bf16[8,8,128,128]{3,2,1,0:T(8,128)(2,1)S(1)}, bf16[8,8,128,128]{3,2,1,0:T(8,128)(2,1)}, u32[]{:S(2)}) copy-start(bf16[8,8,128,128]{3,2,1,0:T(8,128)(2,1)} %get-tuple-element.41.cache_ref) | copy-start | bytes 6291460
  31.9 2.0 %collective-permute-start.2 = (bf16[32,64,128]{2,1,0:T(8,128)(2,1)S(1)}, bf16[32,64,128]{2,1,0:T(8,128)(2,1)S(1)}, u32[]{:S(2)}, u32[]{:S(2)}) collective-permute-start(bf16[32,64,128]{2,1,0:T(8,128)(2,1)S(1)} %get-tuple-element.28), channel_id=1, source_target_pairs={{0,4},{4,0},{8,12},{12,8},{16,20},{20,16},{24,28},{28,24},{32,36},... | collective-permute-start | bytes 1572872 | tf_op jit(solution)/shard_map/ppermute | solution.py:313
  34.9 12.7 %copy-start.7 = (bf16[8,8,128,128]{3,2,1,0:T(8,128)(2,1)S(1)}, bf16[8,8,128,128]{3,2,1,0:T(8,128)(2,1)}, u32[]{:S(2)}) copy-start(bf16[8,8,128,128]{3,2,1,0:T(8,128)(2,1)} %get-tuple-element.38.cache_ref) | copy-start | bytes 6291460
  34.9 7.5 %collective-permute-start.7 = (bf16[8,64,128]{2,1,0:T(8,128)(2,1)S(1)}, bf16[8,64,128]{2,1,0:T(8,128)(2,1)S(1)}, u32[]{:S(2)}, u32[]{:S(2)}) collective-permute-start(bf16[8,64,128]{2,1,0:T(8,128)(2,1)S(1)} %get-tuple-element.40), channel_id=1, source_target_pairs={{0,3},{1,0},{2,1},{3,2},{4,7},{5,4},{6,5},{7,6},{8,11},{9,8},{10,9... | collective-permute-start | bytes 393224 | tf_op jit(solution)/shard_map/ppermute | solution.py:309
  38.0 14.6 %collective-permute-start.3 = (bf16[8,64,128]{2,1,0:T(8,128)(2,1)S(1)}, bf16[8,64,128]{2,1,0:T(8,128)(2,1)S(1)}, u32[]{:S(2)}, u32[]{:S(2)}) collective-permute-start(bf16[8,64,128]{2,1,0:T(8,128)(2,1)S(1)} %get-tuple-element.34), channel_id=1, source_target_pairs={{0,1},{1,2},{2,3},{3,0},{4,5},{5,6},{6,7},{7,4},{8,9},{9,10},{10,1... | collective-permute-start | bytes 393224 | tf_op jit(solution)/shard_map/ppermute | solution.py:309
  38.0 9.6 %collective-permute-start.5 = (bf16[8,64,128]{2,1,0:T(8,128)(2,1)S(1)}, bf16[8,64,128]{2,1,0:T(8,128)(2,1)S(1)}, u32[]{:S(2)}, u32[]{:S(2)}) collective-permute-start(bf16[8,64,128]{2,1,0:T(8,128)(2,1)S(1)} %get-tuple-element.37), channel_id=1, source_target_pairs={{0,2},{1,3},{2,0},{3,1},{4,6},{5,7},{6,4},{7,5},{8,10},{9,11},{10,... | collective-permute-start | bytes 393224 | tf_op jit(solution)/shard_map/ppermute | solution.py:309
  42.3 10.2 %copy-start.6 = (bf16[8,8,128,128]{3,2,1,0:T(8,128)(2,1)S(1)}, bf16[8,8,128,128]{3,2,1,0:T(8,128)(2,1)}, u32[]{:S(2)}) copy-start(bf16[8,8,128,128]{3,2,1,0:T(8,128)(2,1)} %get-tuple-element.35.cache_ref) | copy-start | bytes 6291460
  45.6 13.3 %collective-permute-start.8 = (bf16[8,72,128]{2,1,0:T(8,128)(2,1)S(1)}, bf16[8,72,128]{2,1,0:T(8,128)(2,1)S(1)}, u32[]{:S(2)}, u32[]{:S(2)}) collective-permute-start(bf16[8,72,128]{2,1,0:T(8,128)(2,1)S(1)} %get-tuple-element.42), channel_id=1, source_target_pairs={{0,1},{1,2},{2,3},{3,0},{4,5},{5,6},{6,7},{7,4},{8,9},{9,10},{10,1... | collective-permute-start | bytes 442376 | tf_op jit(solution)/shard_map/ppermute | solution.py:309
  50.7 8.7 %collective-permute-start.6 = (bf16[8,72,128]{2,1,0:T(8,128)(2,1)S(1)}, bf16[8,72,128]{2,1,0:T(8,128)(2,1)S(1)}, u32[]{:S(2)}, u32[]{:S(2)}) collective-permute-start(bf16[8,72,128]{2,1,0:T(8,128)(2,1)S(1)} %get-tuple-element.39), channel_id=1, source_target_pairs={{0,2},{1,3},{2,0},{3,1},{4,6},{5,7},{6,4},{7,5},{8,10},{9,11},{10,... | collective-permute-start | bytes 442376 | tf_op jit(solution)/shard_map/ppermute | solution.py:309
  55.6 32.3 %copy-start.1 = (bf16[1,2,32,128]{3,2,1,0:T(8,128)(2,1)S(1)}, bf16[1,2,32,128]{3,2,1,0:T(8,128)(2,1)}, u32[]{:S(2)}) copy-start(bf16[1,2,32,128]{3,2,1,0:T(8,128)(2,1)} %param.7) | copy-start | bytes 49156
  55.6 32.2 %copy-start.2 = (bf16[1,2,2,128]{3,2,1,0:T(2,128)(2,1)S(1)}, bf16[1,2,2,128]{3,2,1,0:T(2,128)(2,1)}, u32[]{:S(2)}) copy-start(bf16[1,2,2,128]{3,2,1,0:T(2,128)(2,1)} %param.8) | copy-start | bytes 3076
  55.7 32.2 %copy-start.3 = (bf16[1,2,2,128]{3,2,1,0:T(2,128)(2,1)S(1)}, bf16[1,2,2,128]{3,2,1,0:T(2,128)(2,1)}, u32[]{:S(2)}) copy-start(bf16[1,2,2,128]{3,2,1,0:T(2,128)(2,1)} %param.9) | copy-start | bytes 3076
  55.7 5.2 %collective-permute-start.4 = (bf16[8,72,128]{2,1,0:T(8,128)(2,1)S(1)}, bf16[8,72,128]{2,1,0:T(8,128)(2,1)S(1)}, u32[]{:S(2)}, u32[]{:S(2)}) collective-permute-start(bf16[8,72,128]{2,1,0:T(8,128)(2,1)S(1)} %get-tuple-element.36), channel_id=1, source_target_pairs={{0,3},{1,0},{2,1},{3,2},{4,7},{5,4},{6,5},{7,6},{8,11},{9,8},{10,9... | collective-permute-start | bytes 442376 | tf_op jit(solution)/shard_map/ppermute | solution.py:309
  58.8 2.1 %collective-permute-start.9 = (bf16[8,72,128]{2,1,0:T(8,128)(2,1)S(1)}, bf16[8,72,128]{2,1,0:T(8,128)(2,1)S(1)}, u32[]{:S(2)}, u32[]{:S(2)}) collective-permute-start(bf16[8,72,128]{2,1,0:T(8,128)(2,1)S(1)} %get-tuple-element.33.refs_0_), channel_id=1, source_target_pairs={{0,4},{4,0},{8,12},{12,8},{16,20},{20,16},{24,28},{28,24},{32,36},... | collective-permute-start | bytes 442376 | tf_op jit(solution)/shard_map/ppermute | solution.py:313
  58.9 2.0 %collective-permute-start.12 = (bf16[8,72,128]{2,1,0:T(8,128)(2,1)S(1)}, bf16[8,72,128]{2,1,0:T(8,128)(2,1)S(1)}, u32[]{:S(2)}, u32[]{:S(2)}) collective-permute-start(bf16[8,72,128]{2,1,0:T(8,128)(2,1)S(1)} %collective-permute-done.8.refs_3_), channel_id=1, source_target_pairs={{0,4},{4,0},{8,12},{12,8},{16,20},{20,16},{24,28},{28,24},{32,36},... | collective-permute-start | bytes 442376 | tf_op jit(solution)/shard_map/ppermute | solution.py:313
  59.4 1.5 %collective-permute-start.11 = (bf16[8,72,128]{2,1,0:T(8,128)(2,1)S(1)}, bf16[8,72,128]{2,1,0:T(8,128)(2,1)S(1)}, u32[]{:S(2)}, u32[]{:S(2)}) collective-permute-start(bf16[8,72,128]{2,1,0:T(8,128)(2,1)S(1)} %collective-permute-done.6.refs_2_), channel_id=1, source_target_pairs={{0,4},{4,0},{8,12},{12,8},{16,20},{20,16},{24,28},{28,24},{32,36},... | collective-permute-start | bytes 442376 | tf_op jit(solution)/shard_map/ppermute | solution.py:313
  60.9 1.4 %collective-permute-start.10 = (bf16[8,72,128]{2,1,0:T(8,128)(2,1)S(1)}, bf16[8,72,128]{2,1,0:T(8,128)(2,1)S(1)}, u32[]{:S(2)}, u32[]{:S(2)}) collective-permute-start(bf16[8,72,128]{2,1,0:T(8,128)(2,1)S(1)} %collective-permute-done.4.refs_1_), channel_id=1, source_target_pairs={{0,4},{4,0},{8,12},{12,8},{16,20},{20,16},{24,28},{28,24},{32,36},... | collective-permute-start | bytes 442376 | tf_op jit(solution)/shard_map/ppermute | solution.py:313

commit v3 on v1

--- a/solution.py
+++ b/solution.py
@@ -51,20 +51,16 @@
     )(own)
 
 
-def pass_on_kernel(token, got_ref, out_ref, token_out):
+def pass_on_kernel(token, got_ref, out_ref):
     out_ref[...] = got_ref[...]
-    token_out[0] = token[0]
 
 
 def pass_on(token, got):
     return pl.pallas_call(
         pass_on_kernel,
         in_specs=[SMEM, VMEM],
-        out_specs=[VMEM, SMEM],
-        out_shape=[
-            jax.ShapeDtypeStruct(got.shape, got.dtype),
-            jax.ShapeDtypeStruct((1,), jnp.int32),
-        ],
+        out_specs=VMEM,
+        out_shape=jax.ShapeDtypeStruct(got.shape, got.dtype),
         compiler_params=PARAMS,
         cost_estimate=BRINGING,
     )(token, got)
@@ -136,17 +132,17 @@
     return outs[:NY], outs[NY]
 
 
-def attend_kernel(lens, token, q_ref, cache_ref, out_ref, token_out):
+def attend_kernel(lens, q_ref, cache_ref, out_ref):
     rows, _, size, half = cache_ref.shape
     positions = 2 * half
     scale = size ** (-0.5)
-    token_out[0] = token[0]
     chip, core, group = coordinates()
     first = (group * NC + core) * ROWS
     at = lax.broadcasted_iota(jnp.int32, (1, positions), 1)
     own = (chip * NC + core) * half
     other = (chip * NC + 1 - core) * half - half
     start = jnp.where(at < half, own, other)
+    base = jnp.minimum(lens[first], 0)
     stats = [[], [], [], []]
     for j in range(rows):
         valid = at < lens[first + j] - start
@@ -154,7 +150,7 @@
         for k in range(2):
             lines = [slice(t * 32 + k * GROUP, t * 32 + (k + 1) * GROUP) for t in range(2)]
             q = jnp.concatenate([q_ref[j, part, :] for part in lines], 0)
-            keys = jnp.concatenate([cache_ref[j, k], cache_ref[j, 2 + k]], 1)
+            keys = jnp.concatenate([cache_ref[j, base + k], cache_ref[j, base + 2 + k]], 1)
             scores = jnp.dot(q, keys, preferred_element_type=F32) * scale
             scores = jnp.where(valid, scores, NEG_FILL)
             high, low = split_pair(jnp.max(scores, 1, keepdims=True))
@@ -163,7 +159,7 @@
             weights.append(weight.astype(BF16))
         values = jnp.concatenate(
             [
-                jnp.concatenate([cache_ref[j, 4 + 2 * i], cache_ref[j, 5 + 2 * i]], 1)
+                jnp.concatenate([cache_ref[j, base + 4 + 2 * i], cache_ref[j, base + 5 + 2 * i]], 1)
                 for i in range(2)
             ],
             0,
@@ -189,23 +185,20 @@
         out_ref[j, LINES:, :] = tail.astype(BF16)
 
 
-def attend(lens, token, queries, cache):
+def attend(lens, queries, cache):
     rows, _, size, positions = cache.shape
     return pl.pallas_call(
         attend_kernel,
-        in_specs=[SMEM] * 2 + [VMEM] * 2,
-        out_specs=[VMEM, SMEM],
-        out_shape=[
-            jax.ShapeDtypeStruct((rows, BLOCK, size), BF16),
-            jax.ShapeDtypeStruct((1,), jnp.int32),
-        ],
+        in_specs=[SMEM, VMEM, VMEM],
+        out_specs=VMEM,
+        out_shape=jax.ShapeDtypeStruct((rows, BLOCK, size), BF16),
         compiler_params=PARAMS,
         cost_estimate=pl.CostEstimate(
             flops=120 * ROWS * LINES * positions * size,
             bytes_accessed=160 * ROWS * positions * size,
             transcendentals=0,
         ),
-    )(lens, token, queries, cache)
+    )(lens, queries, cache)
 
 
 def to_owners_kernel(order, *refs):
@@ -303,14 +296,12 @@
     send, core = spread(own)
     got = over_chips(send)
     caches, token = by_head(core, (cache_keys, other_keys), (cache_values, other_values))
-    passed, token = pass_on(token, got)
-    sends = to_groups(decode_order, got, to_other_core(passed))
+    sends = to_groups(decode_order, got, to_other_core(pass_on(token, got)))
 
     parts = [None] * NY
-    near = (1, 3, 2, 0)
-    gots = {d: along_kvh(sends[d], d) if d else sends[d] for d in near}
-    for d in near:
-        part, token = attend(cache_len, token, gots[d], caches[d])
+    for d in range(NY):
+        queries_d = along_kvh(sends[d], d) if d else sends[d]
+        part = attend(cache_len, queries_d, caches[d])
         parts[d] = along_kvh(part, NY - d) if d else part
 
     part = over_chips(to_owners(decode_order, parts, [to_other_core(part) for part in parts]))

time: 89.4 us -> 88.9 us (level)
  waiting for transfers between devices: 12.3 us -> 15.9 us
  Pallas kernels: 27.7 us -> 24.3 us
    pallas_call x5, Pallas kernels: 12.2 us -> 8.89 us  [the longest x4 8.31 us: attend(): pl.pallas_call(attend_kernel, in_specs=[SMEM, VMEM, VMEM], out_specs=VMEM...]
    ppermute x6, waiting for transfers between devices: 3.22 us -> 6.48 us  [along_kvh(): return lax.ppermute(x, 'kvh', [(y, (y + d) % NY) for y in range(NY)])]
  transfers between devices with their start and end apart: 14 -> 14, of which waited for: 7 -> 5; matrix products, arithmetic and copies ran while one was open for 0% -> 0% of each run, Pallas kernels for 22% -> 23%
where the time goes in v3:
time: 88.9 us; the launch traced here: 88.4 us
  Pallas kernels  24.3 us (27%)
  blocking collectives  24.1 us (27%)
  starting transfers between devices  23 us (26%)
  waiting for transfers between devices  15.9 us (18%)
    all_to_all x1, blocking collectives, over_chips(): lax.all_to_all(x, 'seq', split_axis=0, concat_axis=0, axis_index_groups=g...  24.1 us
    all_to_all x1, starting transfers between devices, over_chips(): lax.all_to_all(x, 'seq', split_axis=0, concat_axis=0, axis_index_groups=g...  11.6 us
    pallas_call x1, Pallas kernels, by_head(): pl.pallas_call(by_head_kernel, grid_spec=pltpu.PrefetchScalarGridSpec(num...  10.7 us
    ppermute x6, starting transfers between devices, along_kvh(): return lax.ppermute(x, 'kvh', [(y, (y + d) % NY) for y in range(NY)])  9.99 us
    pallas_call x4, Pallas kernels, attend(): pl.pallas_call(attend_kernel, in_specs=[SMEM, VMEM, VMEM], out_specs=VMEM...  8.31 us
    ppermute x6, waiting for transfers between devices, along_kvh(): return lax.ppermute(x, 'kvh', [(y, (y + d) % NY) for y in range(NY)])  6.48 us
    all_to_all x1, waiting for transfers between devices, over_chips(): lax.all_to_all(x, 'seq', split_axis=0, concat_axis=0, axis_index_groups=g...  6.21 us
    ppermute x7, waiting for transfers between devices, to_other_core(): return lax.ppermute(x, 'seq', [(i, i ^ 1) for i in range(CHIPS * NC)])  3.26 us
  transfers between devices with their start and end apart: 14, of which 5 were waited for; matrix products, arithmetic and copies ran while one was open for 0% of the time, Pallas kernels for 23%

profile of v3, /device:TPU:2, one launch (start us, length us, event | category | flops | bytes accessed | tf_op | source)
XLA Modules:
  0.0 88.4 jit_solution(13344379614308920931)
XLA Ops:
  0.0 0.0 collective-permute-start
  0.0 0.5 collective-permute-start.1
  0.5 0.7 copy-done
  1.2 0.9 %shard_map.73 = (bf16[32,64,128]{2,1,0:T(8,128)(2,1)}, s32[1]{0:T(128)}) custom-call(bf16[64,128]{1,0:T(8,128)(2,1)S(1)} %bitcast.4), custom_call_target="tpu_custom_call" | custom-call | tf_op jit(solution)/shard_map/pallas_call | solution.py:42
  2.1 11.6 %all-to-all-start = ((bf16[32,64,128]{2,1,0:T(8,128)(2,1)}), bf16[32,64,128]{2,1,0:T(8,128)(2,1)S(1)}, u32[]{:S(2)}, u32[]{:S(2)}) async-start(bf16[32,64,128]{2,1,0:T(8,128)(2,1)} %get-tuple-element.16), calls=%async_computation | async-start | bytes 1048576 | tf_op jit(solution)/shard_map/all_to_all | solution.py:277
  13.8 0.0 collective-permute-done.refs_1_
  13.8 0.0 collective-permute-done.1.refs_3_
  13.8 0.0 copy-start.4
  13.8 10.7 %shard_map.74 = (bf16[8,8,128,128]{3,2,1,0:T(8,128)(2,1)}, bf16[8,8,128,128]{3,2,1,0:T(8,128)(2,1)}, bf16[8,8,128,128]{3,2,1,0:T(8,128)(2,1)}, bf16[8,8,128,128]{3,2,1,0:T(8,128)(2,1)}, s32[1]{0:T(128)}) custom-call(s32[1]{0:T(128)} %get-tuple-element.17.core, bf16[16,128,8,128]{3,2,1,0:T(8,128)(2,1)} %refs_0_.1, ...), custom_call_target="tpu_custom_call" | custom-call | bytes 16777216 | tf_op jit(solution)/shard_map/pallas_call | solution.py:117
  24.5 0.0 copy-start.9
  24.5 6.2 %all-to-all-done.got_ref.own_ref = bf16[32,64,128]{2,1,0:T(8,128)(2,1)S(1)} async-done(((bf16[32,64,128]{2,1,0:T(8,128)(2,1)}), bf16[32,64,128]{2,1,0:T(8,128)(2,1)S(1)}, u32[]{:S(2)}, u32[]{:S(2)}) %all-to-all-start) | async-done | bytes 524320 | tf_op jit(solution)/shard_map/all_to_all | solution.py:277
  30.8 0.6 shard_map.75
  31.3 0.1 collective-permute-start.2
  31.4 1.9 %collective-permute-done.2.other_ref = bf16[32,64,128]{2,1,0:T(8,128)(2,1)S(1)} collective-permute-done((bf16[32,64,128]{2,1,0:T(8,128)(2,1)S(1)}, bf16[32,64,128]{2,1,0:T(8,128)(2,1)S(1)}, u32[]{:S(2)}, u32[]{:S(2)}) %collective-permute-start.2) | collective-permute-done | bytes 524320 | tf_op jit(solution)/shard_map/ppermute | solution.py:287
  33.3 0.0 copy-done.4
  33.4 0.9 %shard_map.76 = (bf16[8,64,128]{2,1,0:T(8,128)(2,1)S(1)}, bf16[8,64,128]{2,1,0:T(8,128)(2,1)S(1)}, bf16[8,64,128]{2,1,0:T(8,128)(2,1)S(1)}, bf16[8,64,128]{2,1,0:T(8,128)(2,1)S(1)}) custom-call(s32[64]{0:T(128)S(1)} %copy-done.4, bf16[32,64,128]{2,1,0:T(8,128)(2,1)S(1)} %all-to-all-done.got_ref.own_ref, bf16[32,64,128]{2,1,0:T(8,128)(2,1)S(1)} %collective-permute-done.2.other_ref), custom_call_target="tpu_custom_call" | custom-call | flops 1073741824 | bytes 16777216 | tf_op jit(solution)/shard_map/pallas_call | solution.py:85
  34.3 3.1 %collective-permute-start.7 = (bf16[8,64,128]{2,1,0:T(8,128)(2,1)S(1)}, bf16[8,64,128]{2,1,0:T(8,128)(2,1)S(1)}, u32[]{:S(2)}, u32[]{:S(2)}) collective-permute-start(bf16[8,64,128]{2,1,0:T(8,128)(2,1)S(1)} %get-tuple-element.25), channel_id=1, source_target_pairs={{0,3},{1,0},{2,1},{3,2},{4,7},{5,4},{6,5},{7,6},{8,11},{9,8},{10,9... | collective-permute-start | bytes 393224 | tf_op jit(solution)/shard_map/ppermute | solution.py:283
  37.4 0.6 collective-permute-start.5
  38.0 1.0 %collective-permute-start.3 = (bf16[8,64,128]{2,1,0:T(8,128)(2,1)S(1)}, bf16[8,64,128]{2,1,0:T(8,128)(2,1)S(1)}, u32[]{:S(2)}, u32[]{:S(2)}) collective-permute-start(bf16[8,64,128]{2,1,0:T(8,128)(2,1)S(1)} %get-tuple-element.21), channel_id=1, source_target_pairs={{0,1},{1,2},{2,3},{3,0},{4,5},{5,6},{6,7},{7,4},{8,9},{9,10},{10,1... | collective-permute-start | bytes 393224 | tf_op jit(solution)/shard_map/ppermute | solution.py:283
  39.0 4.3 %collective-permute-done.7.q_ref = bf16[8,64,128]{2,1,0:T(8,128)(2,1)S(1)} collective-permute-done((bf16[8,64,128]{2,1,0:T(8,128)(2,1)S(1)}, bf16[8,64,128]{2,1,0:T(8,128)(2,1)S(1)}, u32[]{:S(2)}, u32[]{:S(2)}) %collective-permute-start.7) | collective-permute-done | bytes 131104 | tf_op jit(solution)/shard_map/ppermute | solution.py:283
  43.3 0.0 copy-done.9
  43.3 2.1 %shard_map.80 = bf16[8,72,128]{2,1,0:T(8,128)(2,1)S(1)} custom-call(s32[64]{0:T(128)S(1)} %copy-done.9, bf16[8,64,128]{2,1,0:T(8,128)(2,1)S(1)} %collective-permute-done.7.q_ref, bf16[8,8,128,128]{3,2,1,0:T(8,128)(2,1)S(1)} %copy-done.8), custom_call_target="tpu_custom_call" | custom-call | flops 1006632960 | bytes 20971520 | tf_op jit(solution)/shard_map/pallas_call | solution.py:190
  45.3 0.0 collective-permute-start.8
  45.4 0.0 collective-permute-done.5.q_ref
  45.4 0.0 copy-done.7
  45.4 2.1 %shard_map.79 = bf16[8,72,128]{2,1,0:T(8,128)(2,1)S(1)} custom-call(s32[64]{0:T(128)S(1)} %copy-done.9, bf16[8,64,128]{2,1,0:T(8,128)(2,1)S(1)} %collective-permute-done.5.q_ref, bf16[8,8,128,128]{3,2,1,0:T(8,128)(2,1)S(1)} %copy-done.7), custom_call_target="tpu_custom_call" | custom-call | flops 1006632960 | bytes 20971520 | tf_op jit(solution)/shard_map/pallas_call | solution.py:190
  47.5 5.2 %collective-permute-start.6 = (bf16[8,72,128]{2,1,0:T(8,128)(2,1)S(1)}, bf16[8,72,128]{2,1,0:T(8,128)(2,1)S(1)}, u32[]{:S(2)}, u32[]{:S(2)}) collective-permute-start(bf16[8,72,128]{2,1,0:T(8,128)(2,1)S(1)} %shard_map.79), channel_id=1, source_target_pairs={{0,2},{1,3},{2,0},{3,1},{4,6},{5,7},{6,4},{7,5},{8,10},{9,11},{10,... | collective-permute-start | bytes 442376 | tf_op jit(solution)/shard_map/ppermute | solution.py:283
  52.7 0.0 collective-permute-done.3.q_ref
  52.7 2.1 %shard_map.78 = bf16[8,72,128]{2,1,0:T(8,128)(2,1)S(1)} custom-call(s32[64]{0:T(128)S(1)} %copy-done.9, bf16[8,64,128]{2,1,0:T(8,128)(2,1)S(1)} %collective-permute-done.3.q_ref, bf16[8,8,128,128]{3,2,1,0:T(8,128)(2,1)S(1)} %copy-done.6), custom_call_target="tpu_custom_call" | custom-call | flops 1006632960 | bytes 20971520 | tf_op jit(solution)/shard_map/pallas_call | solution.py:190
  54.7 0.0 copy-start.3
  54.8 0.1 collective-permute-start.4
  54.9 0.0 copy-done.5
  54.9 2.1 %shard_map.77.refs_0_ = bf16[8,72,128]{2,1,0:T(8,128)(2,1)S(1)} custom-call(s32[64]{0:T(128)S(1)} %copy-done.9, bf16[8,64,128]{2,1,0:T(8,128)(2,1)S(1)} %get-tuple-element.19.q_ref, bf16[8,8,128,128]{3,2,1,0:T(8,128)(2,1)S(1)} %copy-done.5), custom_call_target="tpu_custom_call" | custom-call | flops 1006632960 | bytes 20971520 | tf_op jit(solution)/shard_map/pallas_call | solution.py:190
  57.0 0.2 collective-permute-start.9
  57.2 0.0 collective-permute-done.8.refs_3_
  57.2 0.5 collective-permute-start.12
  57.7 0.0 collective-permute-done.6.refs_2_
  57.7 0.1 collective-permute-start.11
  57.8 2.2 %collective-permute-done.4.refs_1_ = bf16[8,72,128]{2,1,0:T(8,128)(2,1)S(1)} collective-permute-done((bf16[8,72,128]{2,1,0:T(8,128)(2,1)S(1)}, bf16[8,72,128]{2,1,0:T(8,128)(2,1)S(1)}, u32[]{:S(2)}, u32[]{:S(2)}) %collective-permute-start.4) | collective-permute-done | bytes 147488 | tf_op jit(solution)/shard_map/ppermute | solution.py:283
  60.0 0.0 collective-permute-start.10
  60.0 0.0 collective-permute-done.9.refs_4_
  60.0 0.0 collective-permute-done.12.refs_7_
  60.0 0.0 collective-permute-done.11.refs_6_
  60.0 1.3 %collective-permute-done.10.refs_5_ = bf16[8,72,128]{2,1,0:T(8,128)(2,1)S(1)} collective-permute-done((bf16[8,72,128]{2,1,0:T(8,128)(2,1)S(1)}, bf16[8,72,128]{2,1,0:T(8,128)(2,1)S(1)}, u32[]{:S(2)}, u32[]{:S(2)}) %collective-permute-start.10) | collective-permute-done | bytes 147488 | tf_op jit(solution)/shard_map/ppermute | solution.py:287
  61.4 1.5 %shard_map.81 = bf16[32,72,128]{2,1,0:T(8,128)(2,1)S(1)} custom-call(s32[64]{0:T(128)S(1)} %copy-done.4, bf16[8,72,128]{2,1,0:T(8,128)(2,1)S(1)} %shard_map.77.refs_0_, bf16[8,72,128]{2,1,0:T(8,128)(2,1)S(1)} %collective-permute-done.4.refs_1_, bf16[8,72,128]{2,1,0:T(8,128)(2,1)S(1)} %collective-permute-done.6.refs_2_, ...), custom_call_target="tpu_custom_call" | custom-call | tf_op jit(solution)/shard_map/pallas_call | solution.py:221
  62.9 24.1 %all_to_all.10.part_ref = bf16[32,72,128]{2,1,0:T(8,128)(2,1)S(1)} all-to-all(bf16[32,72,128]{2,1,0:T(8,128)(2,1)S(1)} %shard_map.81), channel_id=1, replica_groups={{0,8,16,24,32,40,48,56,64,72,80,88,96,104,112,120,128,136,144,152,160,1..., dimensions={0} | all-to-all | bytes 1179648 | tf_op jit(solution)/shard_map/all_to_all | solution.py:277
  87.0 0.0 copy-done.3
  87.0 1.4 %shard_map.82 = bf16[64,128]{1,0:T(8,128)(2,1)} custom-call(bf16[32,72,128]{2,1,0:T(8,128)(2,1)S(1)} %all_to_all.10.part_ref, bf16[64,128]{1,0:T(8,128)(2,1)S(1)} %bitcast.5, bf16[2,2,128]{2,1,0:T(2,128)(2,1)S(1)} %bitcast.6, bf16[2,2,128]{2,1,0:T(2,128)(2,1)S(1)} %bitcast.7), custom_call_target="tpu_custom_call" | custom-call | tf_op jit(solution)/shard_map/pallas_call | solution.py:266
  (11 shorter events, 0.0 us)
Async XLA Ops:
  0.0 13.8 %collective-permute-start = (bf16[16,128,8,128]{3,2,1,0:T(8,128)(2,1)}, bf16[16,128,8,128]{3,2,1,0:T(8,128)(2,1)}, u32[]{:S(2)}, u32[]{:S(2)}) collective-permute-start(bf16[16,128,8,128]{3,2,1,0:T(8,128)(2,1)} %refs_0_.1), channel_id=1, source_target_pairs={{0,4},{4,0},{8,12},{12,8},{16,20},{20,16},{24,28},{28,24},{32,36},... | collective-permute-start | bytes 12582920 | tf_op jit(solution)/shard_map/ppermute | solution.py:287
  0.0 13.8 %collective-permute-start.1 = (bf16[16,128,8,128]{3,2,1,0:T(8,128)(2,1)}, bf16[16,128,8,128]{3,2,1,0:T(8,128)(2,1)}, u32[]{:S(2)}, u32[]{:S(2)}) collective-permute-start(bf16[16,128,8,128]{3,2,1,0:T(8,128)(2,1)} %refs_2_.1), channel_id=1, source_target_pairs={{0,4},{4,0},{8,12},{12,8},{16,20},{20,16},{24,28},{28,24},{32,36},... | collective-permute-start | bytes 12582920 | tf_op jit(solution)/shard_map/ppermute | solution.py:287
  0.5 0.7 copy-start
  2.1 28.6 %all-to-all-start = ((bf16[32,64,128]{2,1,0:T(8,128)(2,1)}), bf16[32,64,128]{2,1,0:T(8,128)(2,1)S(1)}, u32[]{:S(2)}, u32[]{:S(2)}) async-start(bf16[32,64,128]{2,1,0:T(8,128)(2,1)} %get-tuple-element.16), calls=%async_computation | async-start | bytes 1048576 | tf_op jit(solution)/shard_map/all_to_all | solution.py:277
  13.8 19.6 %copy-start.4 = (s32[64]{0:T(128)S(1)}, s32[64]{0:T(128)}, u32[]{:S(2)}) copy-start(s32[64]{0:T(128)} %order.3) | copy-start | bytes 772
  24.5 18.7 %copy-start.8 = (bf16[8,8,128,128]{3,2,1,0:T(8,128)(2,1)S(1)}, bf16[8,8,128,128]{3,2,1,0:T(8,128)(2,1)}, u32[]{:S(2)}) copy-start(bf16[8,8,128,128]{3,2,1,0:T(8,128)(2,1)} %get-tuple-element.26.cache_ref) | copy-start | bytes 6291460
  24.5 18.7 %copy-start.9 = (s32[64]{0:T(128)S(1)}, s32[64]{0:T(128)}, u32[]{:S(2)}) copy-start(s32[64]{0:T(128)} %lens.7) | copy-start | bytes 772
  31.3 14.1 %copy-start.7 = (bf16[8,8,128,128]{3,2,1,0:T(8,128)(2,1)S(1)}, bf16[8,8,128,128]{3,2,1,0:T(8,128)(2,1)}, u32[]{:S(2)}) copy-start(bf16[8,8,128,128]{3,2,1,0:T(8,128)(2,1)} %get-tuple-element.24.cache_ref) | copy-start | bytes 6291460
  31.3 2.0 %collective-permute-start.2 = (bf16[32,64,128]{2,1,0:T(8,128)(2,1)S(1)}, bf16[32,64,128]{2,1,0:T(8,128)(2,1)S(1)}, u32[]{:S(2)}, u32[]{:S(2)}) collective-permute-start(bf16[32,64,128]{2,1,0:T(8,128)(2,1)S(1)} %shard_map.75), channel_id=1, source_target_pairs={{0,4},{4,0},{8,12},{12,8},{16,20},{20,16},{24,28},{28,24},{32,36},... | collective-permute-start | bytes 1572872 | tf_op jit(solution)/shard_map/ppermute | solution.py:287
  34.3 18.4 %copy-start.6 = (bf16[8,8,128,128]{3,2,1,0:T(8,128)(2,1)S(1)}, bf16[8,8,128,128]{3,2,1,0:T(8,128)(2,1)}, u32[]{:S(2)}) copy-start(bf16[8,8,128,128]{3,2,1,0:T(8,128)(2,1)} %get-tuple-element.22.cache_ref) | copy-start | bytes 6291460
  34.3 9.0 %collective-permute-start.7 = (bf16[8,64,128]{2,1,0:T(8,128)(2,1)S(1)}, bf16[8,64,128]{2,1,0:T(8,128)(2,1)S(1)}, u32[]{:S(2)}, u32[]{:S(2)}) collective-permute-start(bf16[8,64,128]{2,1,0:T(8,128)(2,1)S(1)} %get-tuple-element.25), channel_id=1, source_target_pairs={{0,3},{1,0},{2,1},{3,2},{4,7},{5,4},{6,5},{7,6},{8,11},{9,8},{10,9... | collective-permute-start | bytes 393224 | tf_op jit(solution)/shard_map/ppermute | solution.py:283
  37.4 8.0 %collective-permute-start.5 = (bf16[8,64,128]{2,1,0:T(8,128)(2,1)S(1)}, bf16[8,64,128]{2,1,0:T(8,128)(2,1)S(1)}, u32[]{:S(2)}, u32[]{:S(2)}) collective-permute-start(bf16[8,64,128]{2,1,0:T(8,128)(2,1)S(1)} %get-tuple-element.23), channel_id=1, source_target_pairs={{0,2},{1,3},{2,0},{3,1},{4,6},{5,7},{6,4},{7,5},{8,10},{9,11},{10,... | collective-permute-start | bytes 393224 | tf_op jit(solution)/shard_map/ppermute | solution.py:283
  38.0 14.6 %collective-permute-start.3 = (bf16[8,64,128]{2,1,0:T(8,128)(2,1)S(1)}, bf16[8,64,128]{2,1,0:T(8,128)(2,1)S(1)}, u32[]{:S(2)}, u32[]{:S(2)}) collective-permute-start(bf16[8,64,128]{2,1,0:T(8,128)(2,1)S(1)} %get-tuple-element.21), channel_id=1, source_target_pairs={{0,1},{1,2},{2,3},{3,0},{4,5},{5,6},{6,7},{7,4},{8,9},{9,10},{10,1... | collective-permute-start | bytes 393224 | tf_op jit(solution)/shard_map/ppermute | solution.py:283
  45.3 9.5 %copy-start.5 = (bf16[8,8,128,128]{3,2,1,0:T(8,128)(2,1)S(1)}, bf16[8,8,128,128]{3,2,1,0:T(8,128)(2,1)}, u32[]{:S(2)}) copy-start(bf16[8,8,128,128]{3,2,1,0:T(8,128)(2,1)} %get-tuple-element.20.cache_ref) | copy-start | bytes 6291460
  45.3 11.8 %collective-permute-start.8 = (bf16[8,72,128]{2,1,0:T(8,128)(2,1)S(1)}, bf16[8,72,128]{2,1,0:T(8,128)(2,1)S(1)}, u32[]{:S(2)}, u32[]{:S(2)}) collective-permute-start(bf16[8,72,128]{2,1,0:T(8,128)(2,1)S(1)} %shard_map.80), channel_id=1, source_target_pairs={{0,1},{1,2},{2,3},{3,0},{4,5},{5,6},{6,7},{7,4},{8,9},{9,10},{10,1... | collective-permute-start | bytes 442376 | tf_op jit(solution)/shard_map/ppermute | solution.py:283
  47.5 10.2 %collective-permute-start.6 = (bf16[8,72,128]{2,1,0:T(8,128)(2,1)S(1)}, bf16[8,72,128]{2,1,0:T(8,128)(2,1)S(1)}, u32[]{:S(2)}, u32[]{:S(2)}) collective-permute-start(bf16[8,72,128]{2,1,0:T(8,128)(2,1)S(1)} %shard_map.79), channel_id=1, source_target_pairs={{0,2},{1,3},{2,0},{3,1},{4,6},{5,7},{6,4},{7,5},{8,10},{9,11},{10,... | collective-permute-start | bytes 442376 | tf_op jit(solution)/shard_map/ppermute | solution.py:283
  54.7 32.3 %copy-start.1 = (bf16[1,2,32,128]{3,2,1,0:T(8,128)(2,1)S(1)}, bf16[1,2,32,128]{3,2,1,0:T(8,128)(2,1)}, u32[]{:S(2)}) copy-start(bf16[1,2,32,128]{3,2,1,0:T(8,128)(2,1)} %param.7) | copy-start | bytes 49156
  54.7 32.3 %copy-start.2 = (bf16[1,2,2,128]{3,2,1,0:T(2,128)(2,1)S(1)}, bf16[1,2,2,128]{3,2,1,0:T(2,128)(2,1)}, u32[]{:S(2)}) copy-start(bf16[1,2,2,128]{3,2,1,0:T(2,128)(2,1)} %param.8) | copy-start | bytes 3076
  54.7 32.3 %copy-start.3 = (bf16[1,2,2,128]{3,2,1,0:T(2,128)(2,1)S(1)}, bf16[1,2,2,128]{3,2,1,0:T(2,128)(2,1)}, u32[]{:S(2)}) copy-start(bf16[1,2,2,128]{3,2,1,0:T(2,128)(2,1)} %param.9) | copy-start | bytes 3076
  54.8 5.2 %collective-permute-start.4 = (bf16[8,72,128]{2,1,0:T(8,128)(2,1)S(1)}, bf16[8,72,128]{2,1,0:T(8,128)(2,1)S(1)}, u32[]{:S(2)}, u32[]{:S(2)}) collective-permute-start(bf16[8,72,128]{2,1,0:T(8,128)(2,1)S(1)} %shard_map.78), channel_id=1, source_target_pairs={{0,3},{1,0},{2,1},{3,2},{4,7},{5,4},{6,5},{7,6},{8,11},{9,8},{10,9... | collective-permute-start | bytes 442376 | tf_op jit(solution)/shard_map/ppermute | solution.py:283
  57.0 3.0 %collective-permute-start.9 = (bf16[8,72,128]{2,1,0:T(8,128)(2,1)S(1)}, bf16[8,72,128]{2,1,0:T(8,128)(2,1)S(1)}, u32[]{:S(2)}, u32[]{:S(2)}) collective-permute-start(bf16[8,72,128]{2,1,0:T(8,128)(2,1)S(1)} %shard_map.77.refs_0_), channel_id=1, source_target_pairs={{0,4},{4,0},{8,12},{12,8},{16,20},{20,16},{24,28},{28,24},{32,36},... | collective-permute-start | bytes 442376 | tf_op jit(solution)/shard_map/ppermute | solution.py:287
  57.2 2.8 %collective-permute-start.12 = (bf16[8,72,128]{2,1,0:T(8,128)(2,1)S(1)}, bf16[8,72,128]{2,1,0:T(8,128)(2,1)S(1)}, u32[]{:S(2)}, u32[]{:S(2)}) collective-permute-start(bf16[8,72,128]{2,1,0:T(8,128)(2,1)S(1)} %collective-permute-done.8.refs_3_), channel_id=1, source_target_pairs={{0,4},{4,0},{8,12},{12,8},{16,20},{20,16},{24,28},{28,24},{32,36},... | collective-permute-start | bytes 442376 | tf_op jit(solution)/shard_map/ppermute | solution.py:287
  57.7 2.3 %collective-permute-start.11 = (bf16[8,72,128]{2,1,0:T(8,128)(2,1)S(1)}, bf16[8,72,128]{2,1,0:T(8,128)(2,1)S(1)}, u32[]{:S(2)}, u32[]{:S(2)}) collective-permute-start(bf16[8,72,128]{2,1,0:T(8,128)(2,1)S(1)} %collective-permute-done.6.refs_2_), channel_id=1, source_target_pairs={{0,4},{4,0},{8,12},{12,8},{16,20},{20,16},{24,28},{28,24},{32,36},... | collective-permute-start | bytes 442376 | tf_op jit(solution)/shard_map/ppermute | solution.py:287
  60.0 1.4 %collective-permute-start.10 = (bf16[8,72,128]{2,1,0:T(8,128)(2,1)S(1)}, bf16[8,72,128]{2,1,0:T(8,128)(2,1)S(1)}, u32[]{:S(2)}, u32[]{:S(2)}) collective-permute-start(bf16[8,72,128]{2,1,0:T(8,128)(2,1)S(1)} %collective-permute-done.4.refs_1_), channel_id=1, source_target_pairs={{0,4},{4,0},{8,12},{12,8},{16,20},{20,16},{24,28},{28,24},{32,36},... | collective-permute-start | bytes 442376 | tf_op jit(solution)/shard_map/ppermute | solution.py:287

commit v4 on v3

--- a/solution.py
+++ b/solution.py
@@ -132,7 +132,8 @@
     return outs[:NY], outs[NY]
 
 
-def attend_kernel(lens, q_ref, cache_ref, out_ref):
+def attend_kernel(lens, q_ref, cache_ref, *refs):
+    out_ref, token = refs[-2:]
     rows, _, size, half = cache_ref.shape
     positions = 2 * half
     scale = size ** (-0.5)
@@ -143,6 +144,7 @@
     other = (chip * NC + 1 - core) * half - half
     start = jnp.where(at < half, own, other)
     base = jnp.minimum(lens[first], 0)
+    token[0] = base
     stats = [[], [], [], []]
     for j in range(rows):
         valid = at < lens[first + j] - start
@@ -185,20 +187,23 @@
         out_ref[j, LINES:, :] = tail.astype(BF16)
 
 
-def attend(lens, queries, cache):
+def attend(lens, queries, cache, before):
     rows, _, size, positions = cache.shape
     return pl.pallas_call(
         attend_kernel,
-        in_specs=[SMEM, VMEM, VMEM],
-        out_specs=VMEM,
-        out_shape=jax.ShapeDtypeStruct((rows, BLOCK, size), BF16),
+        in_specs=[SMEM, VMEM, VMEM] + [SMEM] * len(before),
+        out_specs=[VMEM, SMEM],
+        out_shape=[
+            jax.ShapeDtypeStruct((rows, BLOCK, size), BF16),
+            jax.ShapeDtypeStruct((1,), jnp.int32),
+        ],
         compiler_params=PARAMS,
         cost_estimate=pl.CostEstimate(
             flops=120 * ROWS * LINES * positions * size,
             bytes_accessed=160 * ROWS * positions * size,
             transcendentals=0,
         ),
-    )(lens, queries, cache)
+    )(lens, queries, cache, *before)
 
 
 def to_owners_kernel(order, *refs):
@@ -299,9 +304,11 @@
     sends = to_groups(decode_order, got, to_other_core(pass_on(token, got)))
 
     parts = [None] * NY
-    for d in range(NY):
-        queries_d = along_kvh(sends[d], d) if d else sends[d]
-        part = attend(cache_len, queries_d, caches[d])
+    near = (1, 3, 2, 0)
+    gots = {d: along_kvh(sends[d], d) if d else sends[d] for d in near}
+    before = ()
+    for d in near:
+        part, *before = attend(cache_len, gots[d], caches[d], before)
         parts[d] = along_kvh(part, NY - d) if d else part
 
     part = over_chips(to_owners(decode_order, parts, [to_other_core(part) for part in parts]))

time: 88.9 us -> 88.1 us (level)
  waiting for transfers between devices: 15.9 us -> 11.5 us
  Pallas kernels: 24.3 us -> 26.6 us
    ppermute x6, waiting for transfers between devices: 6.48 us -> 2.06 us  [along_kvh(): return lax.ppermute(x, 'kvh', [(y, (y + d) % NY) for y in range(NY)])]
    pallas_call x4, Pallas kernels: 8.31 us -> 10.5 us  [attend(): pl.pallas_call(attend_kernel, in_specs=[SMEM, VMEM, VMEM] + [SMEM] * len(...]
  transfers between devices with their start and end apart: 14 -> 14, of which waited for: 5 -> 8; matrix products, arithmetic and copies ran while one was open for 0% -> 0% of each run, Pallas kernels for 23% -> 25%
where the time goes in v4:
time: 88.1 us; the launch traced here: 86.9 us
  Pallas kernels  26.6 us (30%)
  blocking collectives  24.1 us (27%)
  starting transfers between devices  23.7 us (27%)
  waiting for transfers between devices  11.5 us (13%)
    all_to_all x1, blocking collectives, over_chips(): lax.all_to_all(x, 'seq', split_axis=0, concat_axis=0, axis_index_groups=g...  24.1 us
    all_to_all x1, starting transfers between devices, over_chips(): lax.all_to_all(x, 'seq', split_axis=0, concat_axis=0, axis_index_groups=g...  11.6 us
    pallas_call x1, Pallas kernels, by_head(): pl.pallas_call(by_head_kernel, grid_spec=pltpu.PrefetchScalarGridSpec(num...  10.8 us
    ppermute x6, starting transfers between devices, along_kvh(): return lax.ppermute(x, 'kvh', [(y, (y + d) % NY) for y in range(NY)])  10.6 us
    pallas_call x4, Pallas kernels, attend(): pl.pallas_call(attend_kernel, in_specs=[SMEM, VMEM, VMEM] + [SMEM] * len(...  10.5 us
    all_to_all x1, waiting for transfers between devices, over_chips(): lax.all_to_all(x, 'seq', split_axis=0, concat_axis=0, axis_index_groups=g...  6.18 us
    ppermute x7, waiting for transfers between devices, to_other_core(): return lax.ppermute(x, 'seq', [(i, i ^ 1) for i in range(CHIPS * NC)])  3.27 us
    ppermute x6, waiting for transfers between devices, along_kvh(): return lax.ppermute(x, 'kvh', [(y, (y + d) % NY) for y in range(NY)])  2.06 us
  transfers between devices with their start and end apart: 14, of which 8 were waited for; matrix products, arithmetic and copies ran while one was open for 0% of the time, Pallas kernels for 25%

profile of v4, /device:TPU:2, one launch (start us, length us, event | category | flops | bytes accessed | tf_op | source)
XLA Modules:
  0.0 86.9 jit_solution(4037237699124803741)
XLA Ops:
  0.0 0.0 collective-permute-start
  0.0 0.5 collective-permute-start.1
  0.5 0.7 copy-done
  1.2 0.9 %shard_map.73 = (bf16[32,64,128]{2,1,0:T(8,128)(2,1)}, s32[1]{0:T(128)}) custom-call(bf16[64,128]{1,0:T(8,128)(2,1)S(1)} %bitcast.4), custom_call_target="tpu_custom_call" | custom-call | tf_op jit(solution)/shard_map/pallas_call | solution.py:42
  2.1 11.6 %all-to-all-start = ((bf16[32,64,128]{2,1,0:T(8,128)(2,1)}), bf16[32,64,128]{2,1,0:T(8,128)(2,1)S(1)}, u32[]{:S(2)}, u32[]{:S(2)}) async-start(bf16[32,64,128]{2,1,0:T(8,128)(2,1)} %get-tuple-element.23), calls=%async_computation | async-start | bytes 1048576 | tf_op jit(solution)/shard_map/all_to_all | solution.py:282
  13.8 0.0 collective-permute-done.refs_1_
  13.8 0.0 collective-permute-done.1.refs_3_
  13.8 0.0 copy-start.4
  13.8 10.8 %shard_map.74 = (bf16[8,8,128,128]{3,2,1,0:T(8,128)(2,1)}, bf16[8,8,128,128]{3,2,1,0:T(8,128)(2,1)}, bf16[8,8,128,128]{3,2,1,0:T(8,128)(2,1)}, bf16[8,8,128,128]{3,2,1,0:T(8,128)(2,1)}, s32[1]{0:T(128)}) custom-call(s32[1]{0:T(128)} %get-tuple-element.24.core, bf16[16,128,8,128]{3,2,1,0:T(8,128)(2,1)} %refs_0_.1, ...), custom_call_target="tpu_custom_call" | custom-call | bytes 16777216 | tf_op jit(solution)/shard_map/pallas_call | solution.py:117
  24.6 0.0 copy-start.9
  24.6 6.2 %all-to-all-done.got_ref.own_ref = bf16[32,64,128]{2,1,0:T(8,128)(2,1)S(1)} async-done(((bf16[32,64,128]{2,1,0:T(8,128)(2,1)}), bf16[32,64,128]{2,1,0:T(8,128)(2,1)S(1)}, u32[]{:S(2)}, u32[]{:S(2)}) %all-to-all-start) | async-done | bytes 524320 | tf_op jit(solution)/shard_map/all_to_all | solution.py:282
  30.8 0.6 shard_map.75
  31.4 0.0 copy-start.7
  31.4 0.1 collective-permute-start.2
  31.5 1.9 %collective-permute-done.2.other_ref = bf16[32,64,128]{2,1,0:T(8,128)(2,1)S(1)} collective-permute-done((bf16[32,64,128]{2,1,0:T(8,128)(2,1)S(1)}, bf16[32,64,128]{2,1,0:T(8,128)(2,1)S(1)}, u32[]{:S(2)}, u32[]{:S(2)}) %collective-permute-start.2) | collective-permute-done | bytes 524320 | tf_op jit(solution)/shard_map/ppermute | solution.py:292
  33.4 0.0 copy-done.4
  33.4 0.9 %shard_map.76 = (bf16[8,64,128]{2,1,0:T(8,128)(2,1)S(1)}, bf16[8,64,128]{2,1,0:T(8,128)(2,1)S(1)}, bf16[8,64,128]{2,1,0:T(8,128)(2,1)S(1)}, bf16[8,64,128]{2,1,0:T(8,128)(2,1)S(1)}) custom-call(s32[64]{0:T(128)S(1)} %copy-done.4, bf16[32,64,128]{2,1,0:T(8,128)(2,1)S(1)} %all-to-all-done.got_ref.own_ref, bf16[32,64,128]{2,1,0:T(8,128)(2,1)S(1)} %collective-permute-done.2.other_ref), custom_call_target="tpu_custom_call" | custom-call | flops 1073741824 | bytes 16777216 | tf_op jit(solution)/shard_map/pallas_call | solution.py:85
  34.3 0.0 copy-start.6
  34.3 1.7 %collective-permute-start.5 = (bf16[8,64,128]{2,1,0:T(8,128)(2,1)S(1)}, bf16[8,64,128]{2,1,0:T(8,128)(2,1)S(1)}, u32[]{:S(2)}, u32[]{:S(2)}) collective-permute-start(bf16[8,64,128]{2,1,0:T(8,128)(2,1)S(1)} %get-tuple-element.32), channel_id=1, source_target_pairs={{0,1},{1,2},{2,3},{3,0},{4,5},{5,6},{6,7},{7,4},{8,9},{9,10},{10,1... | collective-permute-start | bytes 393224 | tf_op jit(solution)/shard_map/ppermute | solution.py:288
  36.0 1.7 %collective-permute-start.4 = (bf16[8,64,128]{2,1,0:T(8,128)(2,1)S(1)}, bf16[8,64,128]{2,1,0:T(8,128)(2,1)S(1)}, u32[]{:S(2)}, u32[]{:S(2)}) collective-permute-start(bf16[8,64,128]{2,1,0:T(8,128)(2,1)S(1)} %get-tuple-element.30), channel_id=1, source_target_pairs={{0,3},{1,0},{2,1},{3,2},{4,7},{5,4},{6,5},{7,6},{8,11},{9,8},{10,9... | collective-permute-start | bytes 393224 | tf_op jit(solution)/shard_map/ppermute | solution.py:288
  37.6 2.0 %collective-permute-start.3 = (bf16[8,64,128]{2,1,0:T(8,128)(2,1)S(1)}, bf16[8,64,128]{2,1,0:T(8,128)(2,1)S(1)}, u32[]{:S(2)}, u32[]{:S(2)}) collective-permute-start(bf16[8,64,128]{2,1,0:T(8,128)(2,1)S(1)} %get-tuple-element.28), channel_id=1, source_target_pairs={{0,2},{1,3},{2,0},{3,1},{4,6},{5,7},{6,4},{7,5},{8,10},{9,11},{10,... | collective-permute-start | bytes 393224 | tf_op jit(solution)/shard_map/ppermute | solution.py:288
  39.6 1.6 %collective-permute-done.5.q_ref = bf16[8,64,128]{2,1,0:T(8,128)(2,1)S(1)} collective-permute-done((bf16[8,64,128]{2,1,0:T(8,128)(2,1)S(1)}, bf16[8,64,128]{2,1,0:T(8,128)(2,1)S(1)}, u32[]{:S(2)}, u32[]{:S(2)}) %collective-permute-start.5) | collective-permute-done | bytes 131104 | tf_op jit(solution)/shard_map/ppermute | solution.py:288
  41.2 2.1 %shard_map.77 = (bf16[8,72,128]{2,1,0:T(8,128)(2,1)S(1)}, s32[1]{0:T(128)}) custom-call(s32[64]{0:T(128)S(1)} %copy-done.9, bf16[8,64,128]{2,1,0:T(8,128)(2,1)S(1)} %collective-permute-done.5.q_ref, bf16[8,8,128,128]{3,2,1,0:T(8,128)(2,1)S(1)} %copy-done.8), custom_call_target="tpu_custom_call" | custom-call | flops 1006632960 | bytes 20971520 | tf_op jit(solution)/shard_map/pallas_call | solution.py:192
  43.4 2.6 %collective-permute-start.6 = (bf16[8,72,128]{2,1,0:T(8,128)(2,1)S(1)}, bf16[8,72,128]{2,1,0:T(8,128)(2,1)S(1)}, u32[]{:S(2)}, u32[]{:S(2)}) collective-permute-start(bf16[8,72,128]{2,1,0:T(8,128)(2,1)S(1)} %get-tuple-element.38), channel_id=1, source_target_pairs={{0,3},{1,0},{2,1},{3,2},{4,7},{5,4},{6,5},{7,6},{8,11},{9,8},{10,9... | collective-permute-start | bytes 442376 | tf_op jit(solution)/shard_map/ppermute | solution.py:288
  46.0 0.0 collective-permute-done.4.q_ref
  46.0 2.8 %shard_map.78 = (bf16[8,72,128]{2,1,0:T(8,128)(2,1)S(1)}, s32[1]{0:T(128)}) custom-call(s32[64]{0:T(128)S(1)} %copy-done.9, bf16[8,64,128]{2,1,0:T(8,128)(2,1)S(1)} %collective-permute-done.4.q_ref, bf16[8,8,128,128]{3,2,1,0:T(8,128)(2,1)S(1)} %copy-done.7, s32[1]{0:T(128)} %get-tuple-element.34.refs_0_), custom_call_target="tpu_custom_call" | custom-call | flops 1006632960 | bytes 20971520 | tf_op jit(solution)/shard_map/pallas_call | solution.py:192
  48.8 0.1 collective-permute-start.8
  48.8 0.0 collective-permute-done.3.q_ref
  48.9 2.8 %shard_map.79 = (bf16[8,72,128]{2,1,0:T(8,128)(2,1)S(1)}, s32[1]{0:T(128)}) custom-call(s32[64]{0:T(128)S(1)} %copy-done.9, bf16[8,64,128]{2,1,0:T(8,128)(2,1)S(1)} %collective-permute-done.3.q_ref, bf16[8,8,128,128]{3,2,1,0:T(8,128)(2,1)S(1)} %copy-done.6, s32[1]{0:T(128)} %get-tuple-element.35.refs_0_), custom_call_target="tpu_custom_call" | custom-call | flops 1006632960 | bytes 20971520 | tf_op jit(solution)/shard_map/pallas_call | solution.py:192
  51.7 0.0 copy-start.1
  51.7 0.0 copy-start.2
  51.7 0.0 copy-start.3
  51.7 2.6 %collective-permute-start.7 = (bf16[8,72,128]{2,1,0:T(8,128)(2,1)S(1)}, bf16[8,72,128]{2,1,0:T(8,128)(2,1)S(1)}, u32[]{:S(2)}, u32[]{:S(2)}) collective-permute-start(bf16[8,72,128]{2,1,0:T(8,128)(2,1)S(1)} %get-tuple-element.39), channel_id=1, source_target_pairs={{0,2},{1,3},{2,0},{3,1},{4,6},{5,7},{6,4},{7,5},{8,10},{9,11},{10,... | collective-permute-start | bytes 442376 | tf_op jit(solution)/shard_map/ppermute | solution.py:288
  54.3 2.8 %shard_map.80 = (bf16[8,72,128]{2,1,0:T(8,128)(2,1)S(1)}, s32[1]{0:T(128)}) custom-call(s32[64]{0:T(128)S(1)} %copy-done.9, bf16[8,64,128]{2,1,0:T(8,128)(2,1)S(1)} %get-tuple-element.26.q_ref, bf16[8,8,128,128]{3,2,1,0:T(8,128)(2,1)S(1)} %copy-done.5, s32[1]{0:T(128)} %get-tuple-element.36.refs_0_), custom_call_target="tpu_custom_call" | custom-call | flops 1006632960 | bytes 20971520 | tf_op jit(solution)/shard_map/pallas_call | solution.py:192
  57.1 0.3 collective-permute-start.9
  57.4 0.0 collective-permute-done.6.refs_1_
  57.4 0.5 collective-permute-start.10
  57.9 0.0 collective-permute-done.8.refs_3_
  57.9 0.1 collective-permute-start.12
  58.0 0.5 collective-permute-done.7.refs_2_
  58.5 0.0 collective-permute-start.11
  58.5 0.3 collective-permute-done.9.refs_4_
  58.7 0.2 collective-permute-done.10.refs_5_
  59.0 0.3 collective-permute-done.12.refs_7_
  59.3 0.6 collective-permute-done.11.refs_6_
  59.8 1.5 %shard_map.81 = bf16[32,72,128]{2,1,0:T(8,128)(2,1)S(1)} custom-call(s32[64]{0:T(128)S(1)} %copy-done.4, bf16[8,72,128]{2,1,0:T(8,128)(2,1)S(1)} %get-tuple-element.37.refs_0_, bf16[8,72,128]{2,1,0:T(8,128)(2,1)S(1)} %collective-permute-done.6.refs_1_, bf16[8,72,128]{2,1,0:T(8,128)(2,1)S(1)} %collective-permute-done.7.refs_2_, ...), custom_call_target="tpu_custom_call" | custom-call | tf_op jit(solution)/shard_map/pallas_call | solution.py:226
  61.4 24.1 %all_to_all.10.part_ref = bf16[32,72,128]{2,1,0:T(8,128)(2,1)S(1)} all-to-all(bf16[32,72,128]{2,1,0:T(8,128)(2,1)S(1)} %shard_map.81), channel_id=1, replica_groups={{0,8,16,24,32,40,48,56,64,72,80,88,96,104,112,120,128,136,144,152,160,1..., dimensions={0} | all-to-all | bytes 1179648 | tf_op jit(solution)/shard_map/all_to_all | solution.py:282
  85.5 1.4 %shard_map.82 = bf16[64,128]{1,0:T(8,128)(2,1)} custom-call(bf16[32,72,128]{2,1,0:T(8,128)(2,1)S(1)} %all_to_all.10.part_ref, bf16[64,128]{1,0:T(8,128)(2,1)S(1)} %bitcast.5, bf16[2,2,128]{2,1,0:T(2,128)(2,1)S(1)} %bitcast.6, bf16[2,2,128]{2,1,0:T(2,128)(2,1)S(1)} %bitcast.7), custom_call_target="tpu_custom_call" | custom-call | tf_op jit(solution)/shard_map/pallas_call | solution.py:271
  (11 shorter events, 0.0 us)
Async XLA Ops:
  0.0 13.8 %collective-permute-start = (bf16[16,128,8,128]{3,2,1,0:T(8,128)(2,1)}, bf16[16,128,8,128]{3,2,1,0:T(8,128)(2,1)}, u32[]{:S(2)}, u32[]{:S(2)}) collective-permute-start(bf16[16,128,8,128]{3,2,1,0:T(8,128)(2,1)} %refs_0_.1), channel_id=1, source_target_pairs={{0,4},{4,0},{8,12},{12,8},{16,20},{20,16},{24,28},{28,24},{32,36},... | collective-permute-start | bytes 12582920 | tf_op jit(solution)/shard_map/ppermute | solution.py:292
  0.0 13.8 %collective-permute-start.1 = (bf16[16,128,8,128]{3,2,1,0:T(8,128)(2,1)}, bf16[16,128,8,128]{3,2,1,0:T(8,128)(2,1)}, u32[]{:S(2)}, u32[]{:S(2)}) collective-permute-start(bf16[16,128,8,128]{3,2,1,0:T(8,128)(2,1)} %refs_2_.1), channel_id=1, source_target_pairs={{0,4},{4,0},{8,12},{12,8},{16,20},{20,16},{24,28},{28,24},{32,36},... | collective-permute-start | bytes 12582920 | tf_op jit(solution)/shard_map/ppermute | solution.py:292
  0.5 0.7 copy-start
  2.1 28.6 %all-to-all-start = ((bf16[32,64,128]{2,1,0:T(8,128)(2,1)}), bf16[32,64,128]{2,1,0:T(8,128)(2,1)S(1)}, u32[]{:S(2)}, u32[]{:S(2)}) async-start(bf16[32,64,128]{2,1,0:T(8,128)(2,1)} %get-tuple-element.23), calls=%async_computation | async-start | bytes 1048576 | tf_op jit(solution)/shard_map/all_to_all | solution.py:282
  13.8 19.6 %copy-start.4 = (s32[64]{0:T(128)S(1)}, s32[64]{0:T(128)}, u32[]{:S(2)}) copy-start(s32[64]{0:T(128)} %order.3) | copy-start | bytes 772
  24.6 16.6 %copy-start.8 = (bf16[8,8,128,128]{3,2,1,0:T(8,128)(2,1)S(1)}, bf16[8,8,128,128]{3,2,1,0:T(8,128)(2,1)}, u32[]{:S(2)}) copy-start(bf16[8,8,128,128]{3,2,1,0:T(8,128)(2,1)} %get-tuple-element.33.cache_ref) | copy-start | bytes 6291460
  24.6 16.6 %copy-start.9 = (s32[64]{0:T(128)S(1)}, s32[64]{0:T(128)}, u32[]{:S(2)}) copy-start(s32[64]{0:T(128)} %lens.7) | copy-start | bytes 772
  31.4 14.6 %copy-start.7 = (bf16[8,8,128,128]{3,2,1,0:T(8,128)(2,1)S(1)}, bf16[8,8,128,128]{3,2,1,0:T(8,128)(2,1)}, u32[]{:S(2)}) copy-start(bf16[8,8,128,128]{3,2,1,0:T(8,128)(2,1)} %get-tuple-element.31.cache_ref) | copy-start | bytes 6291460
  31.4 2.0 %collective-permute-start.2 = (bf16[32,64,128]{2,1,0:T(8,128)(2,1)S(1)}, bf16[32,64,128]{2,1,0:T(8,128)(2,1)S(1)}, u32[]{:S(2)}, u32[]{:S(2)}) collective-permute-start(bf16[32,64,128]{2,1,0:T(8,128)(2,1)S(1)} %shard_map.75), channel_id=1, source_target_pairs={{0,4},{4,0},{8,12},{12,8},{16,20},{20,16},{24,28},{28,24},{32,36},... | collective-permute-start | bytes 1572872 | tf_op jit(solution)/shard_map/ppermute | solution.py:292
  34.3 14.6 %copy-start.6 = (bf16[8,8,128,128]{3,2,1,0:T(8,128)(2,1)S(1)}, bf16[8,8,128,128]{3,2,1,0:T(8,128)(2,1)}, u32[]{:S(2)}) copy-start(bf16[8,8,128,128]{3,2,1,0:T(8,128)(2,1)} %get-tuple-element.29.cache_ref) | copy-start | bytes 6291460
  34.3 6.9 %collective-permute-start.5 = (bf16[8,64,128]{2,1,0:T(8,128)(2,1)S(1)}, bf16[8,64,128]{2,1,0:T(8,128)(2,1)S(1)}, u32[]{:S(2)}, u32[]{:S(2)}) collective-permute-start(bf16[8,64,128]{2,1,0:T(8,128)(2,1)S(1)} %get-tuple-element.32), channel_id=1, source_target_pairs={{0,1},{1,2},{2,3},{3,0},{4,5},{5,6},{6,7},{7,4},{8,9},{9,10},{10,1... | collective-permute-start | bytes 393224 | tf_op jit(solution)/shard_map/ppermute | solution.py:288
  36.0 10.0 %collective-permute-start.4 = (bf16[8,64,128]{2,1,0:T(8,128)(2,1)S(1)}, bf16[8,64,128]{2,1,0:T(8,128)(2,1)S(1)}, u32[]{:S(2)}, u32[]{:S(2)}) collective-permute-start(bf16[8,64,128]{2,1,0:T(8,128)(2,1)S(1)} %get-tuple-element.30), channel_id=1, source_target_pairs={{0,3},{1,0},{2,1},{3,2},{4,7},{5,4},{6,5},{7,6},{8,11},{9,8},{10,9... | collective-permute-start | bytes 393224 | tf_op jit(solution)/shard_map/ppermute | solution.py:288
  37.6 11.2 %collective-permute-start.3 = (bf16[8,64,128]{2,1,0:T(8,128)(2,1)S(1)}, bf16[8,64,128]{2,1,0:T(8,128)(2,1)S(1)}, u32[]{:S(2)}, u32[]{:S(2)}) collective-permute-start(bf16[8,64,128]{2,1,0:T(8,128)(2,1)S(1)} %get-tuple-element.28), channel_id=1, source_target_pairs={{0,2},{1,3},{2,0},{3,1},{4,6},{5,7},{6,4},{7,5},{8,10},{9,11},{10,... | collective-permute-start | bytes 393224 | tf_op jit(solution)/shard_map/ppermute | solution.py:288
  43.3 11.0 %copy-start.5 = (bf16[8,8,128,128]{3,2,1,0:T(8,128)(2,1)S(1)}, bf16[8,8,128,128]{3,2,1,0:T(8,128)(2,1)}, u32[]{:S(2)}) copy-start(bf16[8,8,128,128]{3,2,1,0:T(8,128)(2,1)} %get-tuple-element.27.cache_ref) | copy-start | bytes 6291460
  43.4 14.0 %collective-permute-start.6 = (bf16[8,72,128]{2,1,0:T(8,128)(2,1)S(1)}, bf16[8,72,128]{2,1,0:T(8,128)(2,1)S(1)}, u32[]{:S(2)}, u32[]{:S(2)}) collective-permute-start(bf16[8,72,128]{2,1,0:T(8,128)(2,1)S(1)} %get-tuple-element.38), channel_id=1, source_target_pairs={{0,3},{1,0},{2,1},{3,2},{4,7},{5,4},{6,5},{7,6},{8,11},{9,8},{10,9... | collective-permute-start | bytes 442376 | tf_op jit(solution)/shard_map/ppermute | solution.py:288
  48.8 9.1 %collective-permute-start.8 = (bf16[8,72,128]{2,1,0:T(8,128)(2,1)S(1)}, bf16[8,72,128]{2,1,0:T(8,128)(2,1)S(1)}, u32[]{:S(2)}, u32[]{:S(2)}) collective-permute-start(bf16[8,72,128]{2,1,0:T(8,128)(2,1)S(1)} %get-tuple-element.40), channel_id=1, source_target_pairs={{0,1},{1,2},{2,3},{3,0},{4,5},{5,6},{6,7},{7,4},{8,9},{9,10},{10,1... | collective-permute-start | bytes 442376 | tf_op jit(solution)/shard_map/ppermute | solution.py:288
  51.7 33.8 %copy-start.1 = (bf16[1,2,32,128]{3,2,1,0:T(8,128)(2,1)S(1)}, bf16[1,2,32,128]{3,2,1,0:T(8,128)(2,1)}, u32[]{:S(2)}) copy-start(bf16[1,2,32,128]{3,2,1,0:T(8,128)(2,1)} %param.7) | copy-start | bytes 49156
  51.7 33.8 %copy-start.2 = (bf16[1,2,2,128]{3,2,1,0:T(2,128)(2,1)S(1)}, bf16[1,2,2,128]{3,2,1,0:T(2,128)(2,1)}, u32[]{:S(2)}) copy-start(bf16[1,2,2,128]{3,2,1,0:T(2,128)(2,1)} %param.8) | copy-start | bytes 3076
  51.7 33.8 %copy-start.3 = (bf16[1,2,2,128]{3,2,1,0:T(2,128)(2,1)S(1)}, bf16[1,2,2,128]{3,2,1,0:T(2,128)(2,1)}, u32[]{:S(2)}) copy-start(bf16[1,2,2,128]{3,2,1,0:T(2,128)(2,1)} %param.9) | copy-start | bytes 3076
  51.7 6.7 %collective-permute-start.7 = (bf16[8,72,128]{2,1,0:T(8,128)(2,1)S(1)}, bf16[8,72,128]{2,1,0:T(8,128)(2,1)S(1)}, u32[]{:S(2)}, u32[]{:S(2)}) collective-permute-start(bf16[8,72,128]{2,1,0:T(8,128)(2,1)S(1)} %get-tuple-element.39), channel_id=1, source_target_pairs={{0,2},{1,3},{2,0},{3,1},{4,6},{5,7},{6,4},{7,5},{8,10},{9,11},{10,... | collective-permute-start | bytes 442376 | tf_op jit(solution)/shard_map/ppermute | solution.py:288
  57.1 1.6 %collective-permute-start.9 = (bf16[8,72,128]{2,1,0:T(8,128)(2,1)S(1)}, bf16[8,72,128]{2,1,0:T(8,128)(2,1)S(1)}, u32[]{:S(2)}, u32[]{:S(2)}) collective-permute-start(bf16[8,72,128]{2,1,0:T(8,128)(2,1)S(1)} %get-tuple-element.37.refs_0_), channel_id=1, source_target_pairs={{0,4},{4,0},{8,12},{12,8},{16,20},{20,16},{24,28},{28,24},{32,36},... | collective-permute-start | bytes 442376 | tf_op jit(solution)/shard_map/ppermute | solution.py:292
  57.4 1.6 %collective-permute-start.10 = (bf16[8,72,128]{2,1,0:T(8,128)(2,1)S(1)}, bf16[8,72,128]{2,1,0:T(8,128)(2,1)S(1)}, u32[]{:S(2)}, u32[]{:S(2)}) collective-permute-start(bf16[8,72,128]{2,1,0:T(8,128)(2,1)S(1)} %collective-permute-done.6.refs_1_), channel_id=1, source_target_pairs={{0,4},{4,0},{8,12},{12,8},{16,20},{20,16},{24,28},{28,24},{32,36},... | collective-permute-start | bytes 442376 | tf_op jit(solution)/shard_map/ppermute | solution.py:292
  57.9 1.4 %collective-permute-start.12 = (bf16[8,72,128]{2,1,0:T(8,128)(2,1)S(1)}, bf16[8,72,128]{2,1,0:T(8,128)(2,1)S(1)}, u32[]{:S(2)}, u32[]{:S(2)}) collective-permute-start(bf16[8,72,128]{2,1,0:T(8,128)(2,1)S(1)} %collective-permute-done.8.refs_3_), channel_id=1, source_target_pairs={{0,4},{4,0},{8,12},{12,8},{16,20},{20,16},{24,28},{28,24},{32,36},... | collective-permute-start | bytes 442376 | tf_op jit(solution)/shard_map/ppermute | solution.py:292
  58.5 1.4 %collective-permute-start.11 = (bf16[8,72,128]{2,1,0:T(8,128)(2,1)S(1)}, bf16[8,72,128]{2,1,0:T(8,128)(2,1)S(1)}, u32[]{:S(2)}, u32[]{:S(2)}) collective-permute-start(bf16[8,72,128]{2,1,0:T(8,128)(2,1)S(1)} %collective-permute-done.7.refs_2_), channel_id=1, source_target_pairs={{0,4},{4,0},{8,12},{12,8},{16,20},{20,16},{24,28},{28,24},{32,36},... | collective-permute-start | bytes 442376 | tf_op jit(solution)/shard_map/ppermute | solution.py:292

commit v5 on v4

--- a/solution.py
+++ b/solution.py
@@ -17,6 +17,7 @@
 BF16 = jnp.bfloat16
 SMEM = pl.BlockSpec(memory_space=pltpu.SMEM)
 VMEM = pl.BlockSpec(memory_space=pltpu.VMEM)
+ANY = pl.BlockSpec(memory_space=pl.ANY)
 PARAMS = pltpu.CompilerParams(vmem_limit_bytes=16 * 2**20)
 BRINGING = pl.CostEstimate(flops=2**30, bytes_accessed=2**24, transcendentals=0)
 
@@ -133,7 +134,7 @@
 
 
 def attend_kernel(lens, q_ref, cache_ref, *refs):
-    out_ref, token = refs[-2:]
+    out_ref = refs[-1]
     rows, _, size, half = cache_ref.shape
     positions = 2 * half
     scale = size ** (-0.5)
@@ -144,7 +145,6 @@
     other = (chip * NC + 1 - core) * half - half
     start = jnp.where(at < half, own, other)
     base = jnp.minimum(lens[first], 0)
-    token[0] = base
     stats = [[], [], [], []]
     for j in range(rows):
         valid = at < lens[first + j] - start
@@ -191,12 +191,9 @@
     rows, _, size, positions = cache.shape
     return pl.pallas_call(
         attend_kernel,
-        in_specs=[SMEM, VMEM, VMEM] + [SMEM] * len(before),
-        out_specs=[VMEM, SMEM],
-        out_shape=[
-            jax.ShapeDtypeStruct((rows, BLOCK, size), BF16),
-            jax.ShapeDtypeStruct((1,), jnp.int32),
-        ],
+        in_specs=[SMEM, VMEM, VMEM] + [ANY] * len(before),
+        out_specs=VMEM,
+        out_shape=jax.ShapeDtypeStruct((rows, BLOCK, size), BF16),
         compiler_params=PARAMS,
         cost_estimate=pl.CostEstimate(
             flops=120 * ROWS * LINES * positions * size,
@@ -207,7 +204,8 @@
 
 
 def to_owners_kernel(order, *refs):
-    own, other, out_ref, slots = refs[:NY], refs[NY : 2 * NY], refs[2 * NY], refs[2 * NY + 1]
+    own, other = refs[:NY], refs[NY : 2 * NY]
+    out_ref, slots, keep = refs[2 * NY :]
     _, core, y = coordinates()
     for slot in range(CHIPS * NC):
         slots[order[slot]] = slot
@@ -215,20 +213,22 @@
         group = lax.rem(y + d, NY)
         for c, source in ((core, own[d]), (1 - core, other[d])):
             for row in range(ROWS):
-                slot = slots[(group * NC + c) * ROWS + row]
-
-                @pl.when(lax.rem(slot, NC) == core)
-                def _():
-                    out_ref[slot // NC] = source[row]
+                keep[slots[(group * NC + c) * ROWS + row]] = source[row]
+    for chip in range(CHIPS):
+        out_ref[chip] = keep[chip * NC + core]
 
 
 def to_owners(order, own, other):
+    block = own[0].shape[1:]
     return pl.pallas_call(
         to_owners_kernel,
         in_specs=[SMEM] + [VMEM] * (2 * NY),
         out_specs=VMEM,
-        out_shape=jax.ShapeDtypeStruct((CHIPS,) + own[0].shape[1:], BF16),
-        scratch_shapes=[pltpu.SMEM((CHIPS * NC,), jnp.int32)],
+        out_shape=jax.ShapeDtypeStruct((CHIPS,) + block, BF16),
+        scratch_shapes=[
+            pltpu.SMEM((CHIPS * NC,), jnp.int32),
+            pltpu.VMEM((CHIPS * NC,) + block, BF16),
+        ],
         compiler_params=PARAMS,
     )(order, *own, *other)
 
@@ -308,7 +308,8 @@
     gots = {d: along_kvh(sends[d], d) if d else sends[d] for d in near}
     before = ()
     for d in near:
-        part, *before = attend(cache_len, gots[d], caches[d], before)
+        part = attend(cache_len, gots[d], caches[d], before)
+        before = (part,)
         parts[d] = along_kvh(part, NY - d) if d else part
 
     part = over_chips(to_owners(decode_order, parts, [to_other_core(part) for part in parts]))

time: 88.1 us -> 85.9 us (0.975)
  Pallas kernels: 26.6 us -> 23.6 us
  waiting for transfers between devices: 11.5 us -> 13.2 us
    pallas_call x4, Pallas kernels: 10.5 us -> 8.31 us  [attend(): pl.pallas_call(attend_kernel, in_specs=[SMEM, VMEM, VMEM] + [ANY] * len(b...]
    ppermute x6, waiting for transfers between devices: 2.06 us -> 4.03 us  [along_kvh(): return lax.ppermute(x, 'kvh', [(y, (y + d) % NY) for y in range(NY)])]
  transfers between devices with their start and end apart: 14 -> 14, of which waited for: 8 -> 8; matrix products, arithmetic and copies ran while one was open for 0% -> 0% of each run, Pallas kernels for 25% -> 21%
where the time goes in v5:
time: 85.9 us; the launch traced here: 85.5 us
  blocking collectives  24.3 us (28%)
  Pallas kernels  23.6 us (27%)
  starting transfers between devices  23.4 us (27%)
  waiting for transfers between devices  13.2 us (15%)
    all_to_all x1, blocking collectives, over_chips(): lax.all_to_all(x, 'seq', split_axis=0, concat_axis=0, axis_index_groups=g...  24.3 us
    all_to_all x1, starting transfers between devices, over_chips(): lax.all_to_all(x, 'seq', split_axis=0, concat_axis=0, axis_index_groups=g...  11.6 us
    pallas_call x1, Pallas kernels, by_head(): pl.pallas_call(by_head_kernel, grid_spec=pltpu.PrefetchScalarGridSpec(num...  10.7 us
    ppermute x6, starting transfers between devices, along_kvh(): return lax.ppermute(x, 'kvh', [(y, (y + d) % NY) for y in range(NY)])  10.5 us
    pallas_call x4, Pallas kernels, attend(): pl.pallas_call(attend_kernel, in_specs=[SMEM, VMEM, VMEM] + [ANY] * len(b...  8.31 us
    all_to_all x1, waiting for transfers between devices, over_chips(): lax.all_to_all(x, 'seq', split_axis=0, concat_axis=0, axis_index_groups=g...  6.21 us
    ppermute x6, waiting for transfers between devices, along_kvh(): return lax.ppermute(x, 'kvh', [(y, (y + d) % NY) for y in range(NY)])  4.03 us
    ppermute x7, waiting for transfers between devices, to_other_core(): return lax.ppermute(x, 'seq', [(i, i ^ 1) for i in range(CHIPS * NC)])  2.97 us
  transfers between devices with their start and end apart: 14, of which 8 were waited for; matrix products, arithmetic and copies ran while one was open for 0% of the time, Pallas kernels for 21%

profile of v5, /device:TPU:2, one launch (start us, length us, event | category | flops | bytes accessed | tf_op | source)
XLA Modules:
  0.0 85.5 jit_solution(1305456575919565323)
XLA Ops:
  0.0 0.0 collective-permute-start
  0.0 0.5 collective-permute-start.1
  0.5 0.7 copy-done
  1.2 0.9 %shard_map.73 = (bf16[32,64,128]{2,1,0:T(8,128)(2,1)}, s32[1]{0:T(128)}) custom-call(bf16[64,128]{1,0:T(8,128)(2,1)S(1)} %bitcast.4), custom_call_target="tpu_custom_call" | custom-call | tf_op jit(solution)/shard_map/pallas_call | solution.py:43
  2.1 11.6 %all-to-all-start = ((bf16[32,64,128]{2,1,0:T(8,128)(2,1)}), bf16[32,64,128]{2,1,0:T(8,128)(2,1)S(1)}, u32[]{:S(2)}, u32[]{:S(2)}) async-start(bf16[32,64,128]{2,1,0:T(8,128)(2,1)} %get-tuple-element.16), calls=%async_computation | async-start | bytes 1048576 | tf_op jit(solution)/shard_map/all_to_all | solution.py:282
  13.8 0.0 collective-permute-done.refs_1_
  13.8 0.0 collective-permute-done.1.refs_3_
  13.8 0.0 copy-start.4
  13.8 10.7 %shard_map.74 = (bf16[8,8,128,128]{3,2,1,0:T(8,128)(2,1)}, bf16[8,8,128,128]{3,2,1,0:T(8,128)(2,1)}, bf16[8,8,128,128]{3,2,1,0:T(8,128)(2,1)}, bf16[8,8,128,128]{3,2,1,0:T(8,128)(2,1)}, s32[1]{0:T(128)}) custom-call(s32[1]{0:T(128)} %get-tuple-element.17.core, bf16[16,128,8,128]{3,2,1,0:T(8,128)(2,1)} %refs_0_.1, ...), custom_call_target="tpu_custom_call" | custom-call | bytes 16777216 | tf_op jit(solution)/shard_map/pallas_call | solution.py:118
  24.5 0.0 copy-start.9
  24.5 6.2 %all-to-all-done.got_ref.own_ref = bf16[32,64,128]{2,1,0:T(8,128)(2,1)S(1)} async-done(((bf16[32,64,128]{2,1,0:T(8,128)(2,1)}), bf16[32,64,128]{2,1,0:T(8,128)(2,1)S(1)}, u32[]{:S(2)}, u32[]{:S(2)}) %all-to-all-start) | async-done | bytes 524320 | tf_op jit(solution)/shard_map/all_to_all | solution.py:282
  30.8 0.6 shard_map.75
  31.3 0.0 copy-start.7
  31.3 0.1 collective-permute-start.2
  31.4 1.9 %collective-permute-done.2.other_ref = bf16[32,64,128]{2,1,0:T(8,128)(2,1)S(1)} collective-permute-done((bf16[32,64,128]{2,1,0:T(8,128)(2,1)S(1)}, bf16[32,64,128]{2,1,0:T(8,128)(2,1)S(1)}, u32[]{:S(2)}, u32[]{:S(2)}) %collective-permute-start.2) | collective-permute-done | bytes 524320 | tf_op jit(solution)/shard_map/ppermute | solution.py:292
  33.4 0.9 %shard_map.76 = (bf16[8,64,128]{2,1,0:T(8,128)(2,1)S(1)}, bf16[8,64,128]{2,1,0:T(8,128)(2,1)S(1)}, bf16[8,64,128]{2,1,0:T(8,128)(2,1)S(1)}, bf16[8,64,128]{2,1,0:T(8,128)(2,1)S(1)}) custom-call(s32[64]{0:T(128)S(1)} %copy-done.4, bf16[32,64,128]{2,1,0:T(8,128)(2,1)S(1)} %all-to-all-done.got_ref.own_ref, bf16[32,64,128]{2,1,0:T(8,128)(2,1)S(1)} %collective-permute-done.2.other_ref), custom_call_target="tpu_custom_call" | custom-call | flops 1073741824 | bytes 16777216 | tf_op jit(solution)/shard_map/pallas_call | solution.py:86
  34.3 1.7 %collective-permute-start.5 = (bf16[8,64,128]{2,1,0:T(8,128)(2,1)S(1)}, bf16[8,64,128]{2,1,0:T(8,128)(2,1)S(1)}, u32[]{:S(2)}, u32[]{:S(2)}) collective-permute-start(bf16[8,64,128]{2,1,0:T(8,128)(2,1)S(1)} %get-tuple-element.25), channel_id=1, source_target_pairs={{0,1},{1,2},{2,3},{3,0},{4,5},{5,6},{6,7},{7,4},{8,9},{9,10},{10,1... | collective-permute-start | bytes 393224 | tf_op jit(solution)/shard_map/ppermute | solution.py:288
  35.9 1.7 %collective-permute-start.4 = (bf16[8,64,128]{2,1,0:T(8,128)(2,1)S(1)}, bf16[8,64,128]{2,1,0:T(8,128)(2,1)S(1)}, u32[]{:S(2)}, u32[]{:S(2)}) collective-permute-start(bf16[8,64,128]{2,1,0:T(8,128)(2,1)S(1)} %get-tuple-element.23), channel_id=1, source_target_pairs={{0,3},{1,0},{2,1},{3,2},{4,7},{5,4},{6,5},{7,6},{8,11},{9,8},{10,9... | collective-permute-start | bytes 393224 | tf_op jit(solution)/shard_map/ppermute | solution.py:288
  37.6 2.0 %collective-permute-start.3 = (bf16[8,64,128]{2,1,0:T(8,128)(2,1)S(1)}, bf16[8,64,128]{2,1,0:T(8,128)(2,1)S(1)}, u32[]{:S(2)}, u32[]{:S(2)}) collective-permute-start(bf16[8,64,128]{2,1,0:T(8,128)(2,1)S(1)} %get-tuple-element.21), channel_id=1, source_target_pairs={{0,2},{1,3},{2,0},{3,1},{4,6},{5,7},{6,4},{7,5},{8,10},{9,11},{10,... | collective-permute-start | bytes 393224 | tf_op jit(solution)/shard_map/ppermute | solution.py:288
  39.6 1.6 %collective-permute-done.5.q_ref = bf16[8,64,128]{2,1,0:T(8,128)(2,1)S(1)} collective-permute-done((bf16[8,64,128]{2,1,0:T(8,128)(2,1)S(1)}, bf16[8,64,128]{2,1,0:T(8,128)(2,1)S(1)}, u32[]{:S(2)}, u32[]{:S(2)}) %collective-permute-start.5) | collective-permute-done | bytes 131104 | tf_op jit(solution)/shard_map/ppermute | solution.py:288
  41.2 0.0 copy-done.8
  41.2 2.1 %shard_map.77.refs_0_ = bf16[8,72,128]{2,1,0:T(8,128)(2,1)S(1)} custom-call(s32[64]{0:T(128)S(1)} %copy-done.9, bf16[8,64,128]{2,1,0:T(8,128)(2,1)S(1)} %collective-permute-done.5.q_ref, bf16[8,8,128,128]{3,2,1,0:T(8,128)(2,1)S(1)} %copy-done.8), custom_call_target="tpu_custom_call" | custom-call | flops 1006632960 | bytes 20971520 | tf_op jit(solution)/shard_map/pallas_call | solution.py:192
  43.3 0.1 collective-permute-done.4.q_ref
  43.4 2.1 %shard_map.78.refs_0_ = bf16[8,72,128]{2,1,0:T(8,128)(2,1)S(1)} custom-call(s32[64]{0:T(128)S(1)} %copy-done.9, bf16[8,64,128]{2,1,0:T(8,128)(2,1)S(1)} %collective-permute-done.4.q_ref, bf16[8,8,128,128]{3,2,1,0:T(8,128)(2,1)S(1)} %copy-done.7, bf16[8,72,128]{2,1,0:T(8,128)(2,1)S(1)} %shard_map.77.refs_0_), custom_call_target="tpu_custom_call" | custom-call | flops 1006632960 | bytes 20971520 | tf_op jit(solution)/shard_map/pallas_call | solution.py:192
  45.5 0.0 collective-permute-done.3.q_ref
  45.5 0.0 copy-done.6
  45.5 2.1 %shard_map.79.refs_0_ = bf16[8,72,128]{2,1,0:T(8,128)(2,1)S(1)} custom-call(s32[64]{0:T(128)S(1)} %copy-done.9, bf16[8,64,128]{2,1,0:T(8,128)(2,1)S(1)} %collective-permute-done.3.q_ref, bf16[8,8,128,128]{3,2,1,0:T(8,128)(2,1)S(1)} %copy-done.6, bf16[8,72,128]{2,1,0:T(8,128)(2,1)S(1)} %shard_map.78.refs_0_), custom_call_target="tpu_custom_call" | custom-call | flops 1006632960 | bytes 20971520 | tf_op jit(solution)/shard_map/pallas_call | solution.py:192
  47.6 0.0 copy-start.3
  47.6 1.9 %collective-permute-start.7 = (bf16[8,72,128]{2,1,0:T(8,128)(2,1)S(1)}, bf16[8,72,128]{2,1,0:T(8,128)(2,1)S(1)}, u32[]{:S(2)}, u32[]{:S(2)}) collective-permute-start(bf16[8,72,128]{2,1,0:T(8,128)(2,1)S(1)} %shard_map.79.refs_0_), channel_id=1, source_target_pairs={{0,2},{1,3},{2,0},{3,1},{4,6},{5,7},{6,4},{7,5},{8,10},{9,11},{10,... | collective-permute-start | bytes 442376 | tf_op jit(solution)/shard_map/ppermute | solution.py:288
  49.6 2.7 %collective-permute-start.8 = (bf16[8,72,128]{2,1,0:T(8,128)(2,1)S(1)}, bf16[8,72,128]{2,1,0:T(8,128)(2,1)S(1)}, u32[]{:S(2)}, u32[]{:S(2)}) collective-permute-start(bf16[8,72,128]{2,1,0:T(8,128)(2,1)S(1)} %shard_map.78.refs_0_), channel_id=1, source_target_pairs={{0,1},{1,2},{2,3},{3,0},{4,5},{5,6},{6,7},{7,4},{8,9},{9,10},{10,1... | collective-permute-start | bytes 442376 | tf_op jit(solution)/shard_map/ppermute | solution.py:288
  52.2 0.6 collective-permute-start.6
  52.8 0.0 copy-done.5
  52.8 2.1 %shard_map.80.refs_0_ = bf16[8,72,128]{2,1,0:T(8,128)(2,1)S(1)} custom-call(s32[64]{0:T(128)S(1)} %copy-done.9, bf16[8,64,128]{2,1,0:T(8,128)(2,1)S(1)} %get-tuple-element.19.q_ref, bf16[8,8,128,128]{3,2,1,0:T(8,128)(2,1)S(1)} %copy-done.5, bf16[8,72,128]{2,1,0:T(8,128)(2,1)S(1)} %shard_map.79.refs_0_), custom_call_target="tpu_custom_call" | custom-call | flops 1006632960 | bytes 20971520 | tf_op jit(solution)/shard_map/pallas_call | solution.py:192
  54.9 0.2 collective-permute-start.9
  55.1 0.8 collective-permute-done.7.refs_2_
  55.9 0.0 collective-permute-start.11
  55.9 1.6 %collective-permute-done.8.refs_3_ = bf16[8,72,128]{2,1,0:T(8,128)(2,1)S(1)} collective-permute-done((bf16[8,72,128]{2,1,0:T(8,128)(2,1)S(1)}, bf16[8,72,128]{2,1,0:T(8,128)(2,1)S(1)}, u32[]{:S(2)}, u32[]{:S(2)}) %collective-permute-start.8) | collective-permute-done | bytes 147488 | tf_op jit(solution)/shard_map/ppermute | solution.py:288
  57.4 0.0 collective-permute-start.12
  57.4 0.0 collective-permute-done.6.refs_1_
  57.4 0.5 collective-permute-start.10
  58.0 0.0 collective-permute-done.9.refs_4_
  58.0 0.0 collective-permute-done.11.refs_6_
  58.0 0.9 collective-permute-done.12.refs_7_
  58.8 0.2 collective-permute-done.10.refs_5_
  59.0 0.8 shard_map.81
  59.8 24.3 %all_to_all.10.part_ref = bf16[32,72,128]{2,1,0:T(8,128)(2,1)S(1)} all-to-all(bf16[32,72,128]{2,1,0:T(8,128)(2,1)S(1)} %shard_map.81), channel_id=1, replica_groups={{0,8,16,24,32,40,48,56,64,72,80,88,96,104,112,120,128,136,144,152,160,1..., dimensions={0} | all-to-all | bytes 1179648 | tf_op jit(solution)/shard_map/all_to_all | solution.py:282
  84.1 0.0 copy-done.1
  84.1 1.4 %shard_map.82 = bf16[64,128]{1,0:T(8,128)(2,1)} custom-call(bf16[32,72,128]{2,1,0:T(8,128)(2,1)S(1)} %all_to_all.10.part_ref, bf16[64,128]{1,0:T(8,128)(2,1)S(1)} %bitcast.5, bf16[2,2,128]{2,1,0:T(2,128)(2,1)S(1)} %bitcast.6, bf16[2,2,128]{2,1,0:T(2,128)(2,1)S(1)} %bitcast.7), custom_call_target="tpu_custom_call" | custom-call | tf_op jit(solution)/shard_map/pallas_call | solution.py:271
  (11 shorter events, 0.0 us)
Async XLA Ops:
  0.0 13.8 %collective-permute-start = (bf16[16,128,8,128]{3,2,1,0:T(8,128)(2,1)}, bf16[16,128,8,128]{3,2,1,0:T(8,128)(2,1)}, u32[]{:S(2)}, u32[]{:S(2)}) collective-permute-start(bf16[16,128,8,128]{3,2,1,0:T(8,128)(2,1)} %refs_0_.1), channel_id=1, source_target_pairs={{0,4},{4,0},{8,12},{12,8},{16,20},{20,16},{24,28},{28,24},{32,36},... | collective-permute-start | bytes 12582920 | tf_op jit(solution)/shard_map/ppermute | solution.py:292
  0.0 13.8 %collective-permute-start.1 = (bf16[16,128,8,128]{3,2,1,0:T(8,128)(2,1)}, bf16[16,128,8,128]{3,2,1,0:T(8,128)(2,1)}, u32[]{:S(2)}, u32[]{:S(2)}) collective-permute-start(bf16[16,128,8,128]{3,2,1,0:T(8,128)(2,1)} %refs_2_.1), channel_id=1, source_target_pairs={{0,4},{4,0},{8,12},{12,8},{16,20},{20,16},{24,28},{28,24},{32,36},... | collective-permute-start | bytes 12582920 | tf_op jit(solution)/shard_map/ppermute | solution.py:292
  0.5 0.7 copy-start
  2.1 28.6 %all-to-all-start = ((bf16[32,64,128]{2,1,0:T(8,128)(2,1)}), bf16[32,64,128]{2,1,0:T(8,128)(2,1)S(1)}, u32[]{:S(2)}, u32[]{:S(2)}) async-start(bf16[32,64,128]{2,1,0:T(8,128)(2,1)} %get-tuple-element.16), calls=%async_computation | async-start | bytes 1048576 | tf_op jit(solution)/shard_map/all_to_all | solution.py:282
  13.8 19.6 %copy-start.4 = (s32[64]{0:T(128)S(1)}, s32[64]{0:T(128)}, u32[]{:S(2)}) copy-start(s32[64]{0:T(128)} %order.3) | copy-start | bytes 772
  24.5 16.7 %copy-start.8 = (bf16[8,8,128,128]{3,2,1,0:T(8,128)(2,1)S(1)}, bf16[8,8,128,128]{3,2,1,0:T(8,128)(2,1)}, u32[]{:S(2)}) copy-start(bf16[8,8,128,128]{3,2,1,0:T(8,128)(2,1)} %get-tuple-element.26.cache_ref) | copy-start | bytes 6291460
  24.5 16.7 %copy-start.9 = (s32[64]{0:T(128)S(1)}, s32[64]{0:T(128)}, u32[]{:S(2)}) copy-start(s32[64]{0:T(128)} %lens.7) | copy-start | bytes 772
  31.3 12.0 %copy-start.7 = (bf16[8,8,128,128]{3,2,1,0:T(8,128)(2,1)S(1)}, bf16[8,8,128,128]{3,2,1,0:T(8,128)(2,1)}, u32[]{:S(2)}) copy-start(bf16[8,8,128,128]{3,2,1,0:T(8,128)(2,1)} %get-tuple-element.24.cache_ref) | copy-start | bytes 6291460
  31.3 2.0 %collective-permute-start.2 = (bf16[32,64,128]{2,1,0:T(8,128)(2,1)S(1)}, bf16[32,64,128]{2,1,0:T(8,128)(2,1)S(1)}, u32[]{:S(2)}, u32[]{:S(2)}) collective-permute-start(bf16[32,64,128]{2,1,0:T(8,128)(2,1)S(1)} %shard_map.75), channel_id=1, source_target_pairs={{0,4},{4,0},{8,12},{12,8},{16,20},{20,16},{24,28},{28,24},{32,36},... | collective-permute-start | bytes 1572872 | tf_op jit(solution)/shard_map/ppermute | solution.py:292
  34.3 11.2 %copy-start.6 = (bf16[8,8,128,128]{3,2,1,0:T(8,128)(2,1)S(1)}, bf16[8,8,128,128]{3,2,1,0:T(8,128)(2,1)}, u32[]{:S(2)}) copy-start(bf16[8,8,128,128]{3,2,1,0:T(8,128)(2,1)} %get-tuple-element.22.cache_ref) | copy-start | bytes 6291460
  34.3 6.9 %collective-permute-start.5 = (bf16[8,64,128]{2,1,0:T(8,128)(2,1)S(1)}, bf16[8,64,128]{2,1,0:T(8,128)(2,1)S(1)}, u32[]{:S(2)}, u32[]{:S(2)}) collective-permute-start(bf16[8,64,128]{2,1,0:T(8,128)(2,1)S(1)} %get-tuple-element.25), channel_id=1, source_target_pairs={{0,1},{1,2},{2,3},{3,0},{4,5},{5,6},{6,7},{7,4},{8,9},{9,10},{10,1... | collective-permute-start | bytes 393224 | tf_op jit(solution)/shard_map/ppermute | solution.py:288
  35.9 7.4 %collective-permute-start.4 = (bf16[8,64,128]{2,1,0:T(8,128)(2,1)S(1)}, bf16[8,64,128]{2,1,0:T(8,128)(2,1)S(1)}, u32[]{:S(2)}, u32[]{:S(2)}) collective-permute-start(bf16[8,64,128]{2,1,0:T(8,128)(2,1)S(1)} %get-tuple-element.23), channel_id=1, source_target_pairs={{0,3},{1,0},{2,1},{3,2},{4,7},{5,4},{6,5},{7,6},{8,11},{9,8},{10,9... | collective-permute-start | bytes 393224 | tf_op jit(solution)/shard_map/ppermute | solution.py:288
  37.6 7.8 %collective-permute-start.3 = (bf16[8,64,128]{2,1,0:T(8,128)(2,1)S(1)}, bf16[8,64,128]{2,1,0:T(8,128)(2,1)S(1)}, u32[]{:S(2)}, u32[]{:S(2)}) collective-permute-start(bf16[8,64,128]{2,1,0:T(8,128)(2,1)S(1)} %get-tuple-element.21), channel_id=1, source_target_pairs={{0,2},{1,3},{2,0},{3,1},{4,6},{5,7},{6,4},{7,5},{8,10},{9,11},{10,... | collective-permute-start | bytes 393224 | tf_op jit(solution)/shard_map/ppermute | solution.py:288
  43.3 9.5 %copy-start.5 = (bf16[8,8,128,128]{3,2,1,0:T(8,128)(2,1)S(1)}, bf16[8,8,128,128]{3,2,1,0:T(8,128)(2,1)}, u32[]{:S(2)}) copy-start(bf16[8,8,128,128]{3,2,1,0:T(8,128)(2,1)} %get-tuple-element.20.cache_ref) | copy-start | bytes 6291460
  47.6 36.5 %copy-start.1 = (bf16[1,2,32,128]{3,2,1,0:T(8,128)(2,1)S(1)}, bf16[1,2,32,128]{3,2,1,0:T(8,128)(2,1)}, u32[]{:S(2)}) copy-start(bf16[1,2,32,128]{3,2,1,0:T(8,128)(2,1)} %param.7) | copy-start | bytes 49156
  47.6 36.5 %copy-start.2 = (bf16[1,2,2,128]{3,2,1,0:T(2,128)(2,1)S(1)}, bf16[1,2,2,128]{3,2,1,0:T(2,128)(2,1)}, u32[]{:S(2)}) copy-start(bf16[1,2,2,128]{3,2,1,0:T(2,128)(2,1)} %param.8) | copy-start | bytes 3076
  47.6 36.5 %copy-start.3 = (bf16[1,2,2,128]{3,2,1,0:T(2,128)(2,1)S(1)}, bf16[1,2,2,128]{3,2,1,0:T(2,128)(2,1)}, u32[]{:S(2)}) copy-start(bf16[1,2,2,128]{3,2,1,0:T(2,128)(2,1)} %param.9) | copy-start | bytes 3076
  47.6 8.2 %collective-permute-start.7 = (bf16[8,72,128]{2,1,0:T(8,128)(2,1)S(1)}, bf16[8,72,128]{2,1,0:T(8,128)(2,1)S(1)}, u32[]{:S(2)}, u32[]{:S(2)}) collective-permute-start(bf16[8,72,128]{2,1,0:T(8,128)(2,1)S(1)} %shard_map.79.refs_0_), channel_id=1, source_target_pairs={{0,2},{1,3},{2,0},{3,1},{4,6},{5,7},{6,4},{7,5},{8,10},{9,11},{10,... | collective-permute-start | bytes 442376 | tf_op jit(solution)/shard_map/ppermute | solution.py:288
  49.6 7.9 %collective-permute-start.8 = (bf16[8,72,128]{2,1,0:T(8,128)(2,1)S(1)}, bf16[8,72,128]{2,1,0:T(8,128)(2,1)S(1)}, u32[]{:S(2)}, u32[]{:S(2)}) collective-permute-start(bf16[8,72,128]{2,1,0:T(8,128)(2,1)S(1)} %shard_map.78.refs_0_), channel_id=1, source_target_pairs={{0,1},{1,2},{2,3},{3,0},{4,5},{5,6},{6,7},{7,4},{8,9},{9,10},{10,1... | collective-permute-start | bytes 442376 | tf_op jit(solution)/shard_map/ppermute | solution.py:288
  52.2 5.2 %collective-permute-start.6 = (bf16[8,72,128]{2,1,0:T(8,128)(2,1)S(1)}, bf16[8,72,128]{2,1,0:T(8,128)(2,1)S(1)}, u32[]{:S(2)}, u32[]{:S(2)}) collective-permute-start(bf16[8,72,128]{2,1,0:T(8,128)(2,1)S(1)} %shard_map.77.refs_0_), channel_id=1, source_target_pairs={{0,3},{1,0},{2,1},{3,2},{4,7},{5,4},{6,5},{7,6},{8,11},{9,8},{10,9... | collective-permute-start | bytes 442376 | tf_op jit(solution)/shard_map/ppermute | solution.py:288
  54.9 3.1 %collective-permute-start.9 = (bf16[8,72,128]{2,1,0:T(8,128)(2,1)S(1)}, bf16[8,72,128]{2,1,0:T(8,128)(2,1)S(1)}, u32[]{:S(2)}, u32[]{:S(2)}) collective-permute-start(bf16[8,72,128]{2,1,0:T(8,128)(2,1)S(1)} %shard_map.80.refs_0_), channel_id=1, source_target_pairs={{0,4},{4,0},{8,12},{12,8},{16,20},{20,16},{24,28},{28,24},{32,36},... | collective-permute-start | bytes 442376 | tf_op jit(solution)/shard_map/ppermute | solution.py:292
  55.9 2.1 %collective-permute-start.11 = (bf16[8,72,128]{2,1,0:T(8,128)(2,1)S(1)}, bf16[8,72,128]{2,1,0:T(8,128)(2,1)S(1)}, u32[]{:S(2)}, u32[]{:S(2)}) collective-permute-start(bf16[8,72,128]{2,1,0:T(8,128)(2,1)S(1)} %collective-permute-done.7.refs_2_), channel_id=1, source_target_pairs={{0,4},{4,0},{8,12},{12,8},{16,20},{20,16},{24,28},{28,24},{32,36},... | collective-permute-start | bytes 442376 | tf_op jit(solution)/shard_map/ppermute | solution.py:292
  57.4 1.4 %collective-permute-start.12 = (bf16[8,72,128]{2,1,0:T(8,128)(2,1)S(1)}, bf16[8,72,128]{2,1,0:T(8,128)(2,1)S(1)}, u32[]{:S(2)}, u32[]{:S(2)}) collective-permute-start(bf16[8,72,128]{2,1,0:T(8,128)(2,1)S(1)} %collective-permute-done.8.refs_3_), channel_id=1, source_target_pairs={{0,4},{4,0},{8,12},{12,8},{16,20},{20,16},{24,28},{28,24},{32,36},... | collective-permute-start | bytes 442376 | tf_op jit(solution)/shard_map/ppermute | solution.py:292
  57.4 1.6 %collective-permute-start.10 = (bf16[8,72,128]{2,1,0:T(8,128)(2,1)S(1)}, bf16[8,72,128]{2,1,0:T(8,128)(2,1)S(1)}, u32[]{:S(2)}, u32[]{:S(2)}) collective-permute-start(bf16[8,72,128]{2,1,0:T(8,128)(2,1)S(1)} %collective-permute-done.6.refs_1_), channel_id=1, source_target_pairs={{0,4},{4,0},{8,12},{12,8},{16,20},{20,16},{24,28},{28,24},{32,36},... | collective-permute-start | bytes 442376 | tf_op jit(solution)/shard_map/ppermute | solution.py:292

commit v6 on v5

--- a/solution.py
+++ b/solution.py
@@ -12,12 +12,12 @@
 ROWS = 8
 LINES = 64
 TAIL = 8
+NEAR = (0, 2, 3, 1)
 BLOCK = LINES + TAIL
 F32 = jnp.float32
 BF16 = jnp.bfloat16
 SMEM = pl.BlockSpec(memory_space=pltpu.SMEM)
 VMEM = pl.BlockSpec(memory_space=pltpu.VMEM)
-ANY = pl.BlockSpec(memory_space=pl.ANY)
 PARAMS = pltpu.CompilerParams(vmem_limit_bytes=16 * 2**20)
 BRINGING = pl.CostEstimate(flops=2**30, bytes_accessed=2**24, transcendentals=0)
 
@@ -72,13 +72,13 @@
     _, core, y = coordinates()
     for slot in range(CHIPS * NC):
         slots[order[slot]] = slot
-    for d in range(NY):
+    for out, d in zip(outs, NEAR):
         group = lax.rem(y + d, NY)
         for row in range(ROWS):
             slot = slots[(group * NC + core) * ROWS + row]
             chip = slot // NC
             mine = lax.rem(slot, NC) == core
-            outs[d][row] = jnp.where(mine, own_ref[chip], other_ref[chip])
+            out[row] = jnp.where(mine, own_ref[chip], other_ref[chip])
 
 
 def to_groups(order, own, other):
@@ -102,13 +102,13 @@
     token[0] = core[0]
     for slot in range(4):
         keep[slot] = ins[slot][0].reshape(positions * kv, size).astype(F32)
-    for d in range(NY):
+    for out, d in zip(outs, NEAR):
         quarter = lax.rem(y + NY - d, NY)
         for k in range(2):
             head = pl.ds(2 * quarter + k, positions, stride=kv)
             for i in range(2):
-                outs[d][0, i * 2 + k] = keep[i, head, :].astype(BF16).T
-                outs[d][0, 4 + i * 2 + k] = keep[2 + i, head, :].astype(BF16)
+                out[0, i * 2 + k] = keep[i, head, :].astype(BF16).T
+                out[0, 4 + i * 2 + k] = keep[2 + i, head, :].astype(BF16)
 
 
 def by_head(core, keys, values):
@@ -133,8 +133,7 @@
     return outs[:NY], outs[NY]
 
 
-def attend_kernel(lens, q_ref, cache_ref, *refs):
-    out_ref = refs[-1]
+def attend_kernel(lens, q_ref, cache_ref, out_ref):
     rows, _, size, half = cache_ref.shape
     positions = 2 * half
     scale = size ** (-0.5)
@@ -187,11 +186,11 @@
         out_ref[j, LINES:, :] = tail.astype(BF16)
 
 
-def attend(lens, queries, cache, before):
+def attend(lens, queries, cache):
     rows, _, size, positions = cache.shape
     return pl.pallas_call(
         attend_kernel,
-        in_specs=[SMEM, VMEM, VMEM] + [ANY] * len(before),
+        in_specs=[SMEM, VMEM, VMEM],
         out_specs=VMEM,
         out_shape=jax.ShapeDtypeStruct((rows, BLOCK, size), BF16),
         compiler_params=PARAMS,
@@ -200,7 +199,7 @@
             bytes_accessed=160 * ROWS * positions * size,
             transcendentals=0,
         ),
-    )(lens, queries, cache, *before)
+    )(lens, queries, cache)
 
 
 def to_owners_kernel(order, *refs):
@@ -209,9 +208,9 @@
     _, core, y = coordinates()
     for slot in range(CHIPS * NC):
         slots[order[slot]] = slot
-    for d in range(NY):
+    for i, d in enumerate(NEAR):
         group = lax.rem(y + d, NY)
-        for c, source in ((core, own[d]), (1 - core, other[d])):
+        for c, source in ((core, own[i]), (1 - core, other[i])):
             for row in range(ROWS):
                 keep[slots[(group * NC + c) * ROWS + row]] = source[row]
     for chip in range(CHIPS):
@@ -303,14 +302,10 @@
     caches, token = by_head(core, (cache_keys, other_keys), (cache_values, other_values))
     sends = to_groups(decode_order, got, to_other_core(pass_on(token, got)))
 
-    parts = [None] * NY
-    near = (1, 3, 2, 0)
-    gots = {d: along_kvh(sends[d], d) if d else sends[d] for d in near}
-    before = ()
-    for d in near:
-        part = attend(cache_len, gots[d], caches[d], before)
-        before = (part,)
-        parts[d] = along_kvh(part, NY - d) if d else part
+    parts = []
+    for d, send, cache in zip(NEAR, sends, caches):
+        part = attend(cache_len, along_kvh(send, d) if d else send, cache)
+        parts.append(along_kvh(part, NY - d) if d else part)
 
     part = over_chips(to_owners(decode_order, parts, [to_other_core(part) for part in parts]))
     out = finish(part, own, new_keys[0], new_values[0])

time: 85.9 us -> 85.9 us (level)
  transfers between devices with their start and end apart: 14 -> 14, of which waited for: 8 -> 6; matrix products, arithmetic and copies ran while one was open for 0% -> 0% of each run, Pallas kernels for 21% -> 23%
where the time goes in v6:
time: 85.9 us; the launch traced here: 85.4 us
  blocking collectives  24.3 us (28%)
  starting transfers between devices  24.1 us (28%)
  Pallas kernels  23.6 us (27%)
  waiting for transfers between devices  12.5 us (15%)
    all_to_all x1, blocking collectives, over_chips(): lax.all_to_all(x, 'seq', split_axis=0, concat_axis=0, axis_index_groups=g...  24.3 us
    all_to_all x1, starting transfers between devices, over_chips(): lax.all_to_all(x, 'seq', split_axis=0, concat_axis=0, axis_index_groups=g...  11.6 us
    pallas_call x1, Pallas kernels, by_head(): pl.pallas_call(by_head_kernel, grid_spec=pltpu.PrefetchScalarGridSpec(num...  10.7 us
    ppermute x6, starting transfers between devices, along_kvh(): return lax.ppermute(x, 'kvh', [(y, (y + d) % NY) for y in range(NY)])  10.6 us
    pallas_call x4, Pallas kernels, attend(): pl.pallas_call(attend_kernel, in_specs=[SMEM, VMEM, VMEM], out_specs=VMEM...  8.31 us
    all_to_all x1, waiting for transfers between devices, over_chips(): lax.all_to_all(x, 'seq', split_axis=0, concat_axis=0, axis_index_groups=g...  6.2 us
    ppermute x6, waiting for transfers between devices, along_kvh(): return lax.ppermute(x, 'kvh', [(y, (y + d) % NY) for y in range(NY)])  3.34 us
    ppermute x7, waiting for transfers between devices, to_other_core(): return lax.ppermute(x, 'seq', [(i, i ^ 1) for i in range(CHIPS * NC)])  2.97 us
  transfers between devices with their start and end apart: 14, of which 6 were waited for; matrix products, arithmetic and copies ran while one was open for 0% of the time, Pallas kernels for 23%

profile of v6, /device:TPU:2, one launch (start us, length us, event | category | flops | bytes accessed | tf_op | source)
XLA Modules:
  0.0 85.4 jit_solution(5754076223558644621)
XLA Ops:
  0.0 0.0 collective-permute-start
  0.0 0.5 collective-permute-start.1
  0.5 0.7 copy-done
  1.2 0.9 %shard_map.73 = (bf16[32,64,128]{2,1,0:T(8,128)(2,1)}, s32[1]{0:T(128)}) custom-call(bf16[64,128]{1,0:T(8,128)(2,1)S(1)} %bitcast.4), custom_call_target="tpu_custom_call" | custom-call | tf_op jit(solution)/shard_map/pallas_call | solution.py:43
  2.1 11.6 %all-to-all-start = ((bf16[32,64,128]{2,1,0:T(8,128)(2,1)}), bf16[32,64,128]{2,1,0:T(8,128)(2,1)S(1)}, u32[]{:S(2)}, u32[]{:S(2)}) async-start(bf16[32,64,128]{2,1,0:T(8,128)(2,1)} %get-tuple-element.16), calls=%async_computation | async-start | bytes 1048576 | tf_op jit(solution)/shard_map/all_to_all | solution.py:281
  13.8 0.0 collective-permute-done.refs_1_
  13.8 0.0 collective-permute-done.1.refs_3_
  13.8 0.0 copy-start.4
  13.8 10.7 %shard_map.74 = (bf16[8,8,128,128]{3,2,1,0:T(8,128)(2,1)}, bf16[8,8,128,128]{3,2,1,0:T(8,128)(2,1)}, bf16[8,8,128,128]{3,2,1,0:T(8,128)(2,1)}, bf16[8,8,128,128]{3,2,1,0:T(8,128)(2,1)}, s32[1]{0:T(128)}) custom-call(s32[1]{0:T(128)} %get-tuple-element.17.core, bf16[16,128,8,128]{3,2,1,0:T(8,128)(2,1)} %refs_0_.1, ...), custom_call_target="tpu_custom_call" | custom-call | bytes 16777216 | tf_op jit(solution)/shard_map/pallas_call | solution.py:118
  24.5 0.0 copy-start.9
  24.6 6.2 %all-to-all-done.got_ref.own_ref = bf16[32,64,128]{2,1,0:T(8,128)(2,1)S(1)} async-done(((bf16[32,64,128]{2,1,0:T(8,128)(2,1)}), bf16[32,64,128]{2,1,0:T(8,128)(2,1)S(1)}, u32[]{:S(2)}, u32[]{:S(2)}) %all-to-all-start) | async-done | bytes 524320 | tf_op jit(solution)/shard_map/all_to_all | solution.py:281
  30.8 0.6 shard_map.75
  31.3 0.0 copy-start.7
  31.3 0.1 collective-permute-start.2
  31.4 1.9 %collective-permute-done.2.other_ref = bf16[32,64,128]{2,1,0:T(8,128)(2,1)S(1)} collective-permute-done((bf16[32,64,128]{2,1,0:T(8,128)(2,1)S(1)}, bf16[32,64,128]{2,1,0:T(8,128)(2,1)S(1)}, u32[]{:S(2)}, u32[]{:S(2)}) %collective-permute-start.2) | collective-permute-done | bytes 524320 | tf_op jit(solution)/shard_map/ppermute | solution.py:291
  33.3 0.0 copy-done.4
  33.4 0.9 %shard_map.76 = (bf16[8,64,128]{2,1,0:T(8,128)(2,1)S(1)}, bf16[8,64,128]{2,1,0:T(8,128)(2,1)S(1)}, bf16[8,64,128]{2,1,0:T(8,128)(2,1)S(1)}, bf16[8,64,128]{2,1,0:T(8,128)(2,1)S(1)}) custom-call(s32[64]{0:T(128)S(1)} %copy-done.4, bf16[32,64,128]{2,1,0:T(8,128)(2,1)S(1)} %all-to-all-done.got_ref.own_ref, bf16[32,64,128]{2,1,0:T(8,128)(2,1)S(1)} %collective-permute-done.2.other_ref), custom_call_target="tpu_custom_call" | custom-call | flops 1073741824 | bytes 16777216 | tf_op jit(solution)/shard_map/pallas_call | solution.py:86
  34.3 0.0 copy-start.6
  34.3 1.7 %collective-permute-start.7 = (bf16[8,64,128]{2,1,0:T(8,128)(2,1)S(1)}, bf16[8,64,128]{2,1,0:T(8,128)(2,1)S(1)}, u32[]{:S(2)}, u32[]{:S(2)}) collective-permute-start(bf16[8,64,128]{2,1,0:T(8,128)(2,1)S(1)} %get-tuple-element.25), channel_id=1, source_target_pairs={{0,1},{1,2},{2,3},{3,0},{4,5},{5,6},{6,7},{7,4},{8,9},{9,10},{10,1... | collective-permute-start | bytes 393224 | tf_op jit(solution)/shard_map/ppermute | solution.py:287
  35.9 1.7 %collective-permute-start.5 = (bf16[8,64,128]{2,1,0:T(8,128)(2,1)S(1)}, bf16[8,64,128]{2,1,0:T(8,128)(2,1)S(1)}, u32[]{:S(2)}, u32[]{:S(2)}) collective-permute-start(bf16[8,64,128]{2,1,0:T(8,128)(2,1)S(1)} %get-tuple-element.23), channel_id=1, source_target_pairs={{0,3},{1,0},{2,1},{3,2},{4,7},{5,4},{6,5},{7,6},{8,11},{9,8},{10,9... | collective-permute-start | bytes 393224 | tf_op jit(solution)/shard_map/ppermute | solution.py:287
  37.6 2.0 %collective-permute-start.3 = (bf16[8,64,128]{2,1,0:T(8,128)(2,1)S(1)}, bf16[8,64,128]{2,1,0:T(8,128)(2,1)S(1)}, u32[]{:S(2)}, u32[]{:S(2)}) collective-permute-start(bf16[8,64,128]{2,1,0:T(8,128)(2,1)S(1)} %get-tuple-element.21), channel_id=1, source_target_pairs={{0,2},{1,3},{2,0},{3,1},{4,6},{5,7},{6,4},{7,5},{8,10},{9,11},{10,... | collective-permute-start | bytes 393224 | tf_op jit(solution)/shard_map/ppermute | solution.py:287
  39.6 1.6 %collective-permute-done.7.q_ref = bf16[8,64,128]{2,1,0:T(8,128)(2,1)S(1)} collective-permute-done((bf16[8,64,128]{2,1,0:T(8,128)(2,1)S(1)}, bf16[8,64,128]{2,1,0:T(8,128)(2,1)S(1)}, u32[]{:S(2)}, u32[]{:S(2)}) %collective-permute-start.7) | collective-permute-done | bytes 131104 | tf_op jit(solution)/shard_map/ppermute | solution.py:287
  41.2 0.0 copy-done.9
  41.2 2.1 %shard_map.80 = bf16[8,72,128]{2,1,0:T(8,128)(2,1)S(1)} custom-call(s32[64]{0:T(128)S(1)} %copy-done.9, bf16[8,64,128]{2,1,0:T(8,128)(2,1)S(1)} %collective-permute-done.7.q_ref, bf16[8,8,128,128]{3,2,1,0:T(8,128)(2,1)S(1)} %copy-done.8), custom_call_target="tpu_custom_call" | custom-call | flops 1006632960 | bytes 20971520 | tf_op jit(solution)/shard_map/pallas_call | solution.py:191
  43.3 2.6 %collective-permute-start.8 = (bf16[8,72,128]{2,1,0:T(8,128)(2,1)S(1)}, bf16[8,72,128]{2,1,0:T(8,128)(2,1)S(1)}, u32[]{:S(2)}, u32[]{:S(2)}) collective-permute-start(bf16[8,72,128]{2,1,0:T(8,128)(2,1)S(1)} %shard_map.80), channel_id=1, source_target_pairs={{0,3},{1,0},{2,1},{3,2},{4,7},{5,4},{6,5},{7,6},{8,11},{9,8},{10,9... | collective-permute-start | bytes 442376 | tf_op jit(solution)/shard_map/ppermute | solution.py:287
  45.9 0.0 collective-permute-done.5.q_ref
  45.9 2.1 %shard_map.79 = bf16[8,72,128]{2,1,0:T(8,128)(2,1)S(1)} custom-call(s32[64]{0:T(128)S(1)} %copy-done.9, bf16[8,64,128]{2,1,0:T(8,128)(2,1)S(1)} %collective-permute-done.5.q_ref, bf16[8,8,128,128]{3,2,1,0:T(8,128)(2,1)S(1)} %copy-done.7), custom_call_target="tpu_custom_call" | custom-call | flops 1006632960 | bytes 20971520 | tf_op jit(solution)/shard_map/pallas_call | solution.py:191
  47.9 0.0 collective-permute-start.6
  48.0 0.0 collective-permute-done.3.q_ref
  48.0 2.1 %shard_map.78 = bf16[8,72,128]{2,1,0:T(8,128)(2,1)S(1)} custom-call(s32[64]{0:T(128)S(1)} %copy-done.9, bf16[8,64,128]{2,1,0:T(8,128)(2,1)S(1)} %collective-permute-done.3.q_ref, bf16[8,8,128,128]{3,2,1,0:T(8,128)(2,1)S(1)} %copy-done.6), custom_call_target="tpu_custom_call" | custom-call | flops 1006632960 | bytes 20971520 | tf_op jit(solution)/shard_map/pallas_call | solution.py:191
  50.1 0.0 copy-start.3
  50.1 2.7 %collective-permute-start.4 = (bf16[8,72,128]{2,1,0:T(8,128)(2,1)S(1)}, bf16[8,72,128]{2,1,0:T(8,128)(2,1)S(1)}, u32[]{:S(2)}, u32[]{:S(2)}) collective-permute-start(bf16[8,72,128]{2,1,0:T(8,128)(2,1)S(1)} %shard_map.78), channel_id=1, source_target_pairs={{0,2},{1,3},{2,0},{3,1},{4,6},{5,7},{6,4},{7,5},{8,10},{9,11},{10,... | collective-permute-start | bytes 442376 | tf_op jit(solution)/shard_map/ppermute | solution.py:287
  52.8 2.1 %shard_map.77.refs_0_ = bf16[8,72,128]{2,1,0:T(8,128)(2,1)S(1)} custom-call(s32[64]{0:T(128)S(1)} %copy-done.9, bf16[8,64,128]{2,1,0:T(8,128)(2,1)S(1)} %get-tuple-element.19.q_ref, bf16[8,8,128,128]{3,2,1,0:T(8,128)(2,1)S(1)} %copy-done.5), custom_call_target="tpu_custom_call" | custom-call | flops 1006632960 | bytes 20971520 | tf_op jit(solution)/shard_map/pallas_call | solution.py:191
  54.9 0.2 collective-permute-start.9
  55.1 0.0 collective-permute-done.8.refs_3_
  55.1 0.5 collective-permute-start.12
  55.6 1.7 %collective-permute-done.6.refs_2_ = bf16[8,72,128]{2,1,0:T(8,128)(2,1)S(1)} collective-permute-done((bf16[8,72,128]{2,1,0:T(8,128)(2,1)S(1)}, bf16[8,72,128]{2,1,0:T(8,128)(2,1)S(1)}, u32[]{:S(2)}, u32[]{:S(2)}) %collective-permute-start.6) | collective-permute-done | bytes 147488 | tf_op jit(solution)/shard_map/ppermute | solution.py:287
  57.4 0.0 collective-permute-start.11
  57.4 0.0 collective-permute-done.4.refs_1_
  57.4 0.5 collective-permute-start.10
  57.9 0.0 collective-permute-done.9.refs_4_
  57.9 0.0 collective-permute-done.12.refs_7_
  57.9 0.9 collective-permute-done.11.refs_6_
  58.7 0.2 collective-permute-done.10.refs_5_
  59.0 0.8 shard_map.81
  59.7 24.3 %all_to_all.10.part_ref = bf16[32,72,128]{2,1,0:T(8,128)(2,1)S(1)} all-to-all(bf16[32,72,128]{2,1,0:T(8,128)(2,1)S(1)} %shard_map.81), channel_id=1, replica_groups={{0,8,16,24,32,40,48,56,64,72,80,88,96,104,112,120,128,136,144,152,160,1..., dimensions={0} | all-to-all | bytes 1179648 | tf_op jit(solution)/shard_map/all_to_all | solution.py:281
  84.0 0.0 copy-done.1
  84.0 1.4 %shard_map.82 = bf16[64,128]{1,0:T(8,128)(2,1)} custom-call(bf16[32,72,128]{2,1,0:T(8,128)(2,1)S(1)} %all_to_all.10.part_ref, bf16[64,128]{1,0:T(8,128)(2,1)S(1)} %bitcast.5, bf16[2,2,128]{2,1,0:T(2,128)(2,1)S(1)} %bitcast.6, bf16[2,2,128]{2,1,0:T(2,128)(2,1)S(1)} %bitcast.7), custom_call_target="tpu_custom_call" | custom-call | tf_op jit(solution)/shard_map/pallas_call | solution.py:270
  (11 shorter events, 0.0 us)
Async XLA Ops:
  0.0 13.8 %collective-permute-start = (bf16[16,128,8,128]{3,2,1,0:T(8,128)(2,1)}, bf16[16,128,8,128]{3,2,1,0:T(8,128)(2,1)}, u32[]{:S(2)}, u32[]{:S(2)}) collective-permute-start(bf16[16,128,8,128]{3,2,1,0:T(8,128)(2,1)} %refs_0_.1), channel_id=1, source_target_pairs={{0,4},{4,0},{8,12},{12,8},{16,20},{20,16},{24,28},{28,24},{32,36},... | collective-permute-start | bytes 12582920 | tf_op jit(solution)/shard_map/ppermute | solution.py:291
  0.0 13.8 %collective-permute-start.1 = (bf16[16,128,8,128]{3,2,1,0:T(8,128)(2,1)}, bf16[16,128,8,128]{3,2,1,0:T(8,128)(2,1)}, u32[]{:S(2)}, u32[]{:S(2)}) collective-permute-start(bf16[16,128,8,128]{3,2,1,0:T(8,128)(2,1)} %refs_2_.1), channel_id=1, source_target_pairs={{0,4},{4,0},{8,12},{12,8},{16,20},{20,16},{24,28},{28,24},{32,36},... | collective-permute-start | bytes 12582920 | tf_op jit(solution)/shard_map/ppermute | solution.py:291
  0.5 0.7 copy-start
  2.1 28.6 %all-to-all-start = ((bf16[32,64,128]{2,1,0:T(8,128)(2,1)}), bf16[32,64,128]{2,1,0:T(8,128)(2,1)S(1)}, u32[]{:S(2)}, u32[]{:S(2)}) async-start(bf16[32,64,128]{2,1,0:T(8,128)(2,1)} %get-tuple-element.16), calls=%async_computation | async-start | bytes 1048576 | tf_op jit(solution)/shard_map/all_to_all | solution.py:281
  13.8 19.6 %copy-start.4 = (s32[64]{0:T(128)S(1)}, s32[64]{0:T(128)}, u32[]{:S(2)}) copy-start(s32[64]{0:T(128)} %order.3) | copy-start | bytes 772
  24.5 16.7 %copy-start.8 = (bf16[8,8,128,128]{3,2,1,0:T(8,128)(2,1)S(1)}, bf16[8,8,128,128]{3,2,1,0:T(8,128)(2,1)}, u32[]{:S(2)}) copy-start(bf16[8,8,128,128]{3,2,1,0:T(8,128)(2,1)} %get-tuple-element.26.cache_ref) | copy-start | bytes 6291460
  24.5 16.7 %copy-start.9 = (s32[64]{0:T(128)S(1)}, s32[64]{0:T(128)}, u32[]{:S(2)}) copy-start(s32[64]{0:T(128)} %lens.7) | copy-start | bytes 772
  31.3 14.5 %copy-start.7 = (bf16[8,8,128,128]{3,2,1,0:T(8,128)(2,1)S(1)}, bf16[8,8,128,128]{3,2,1,0:T(8,128)(2,1)}, u32[]{:S(2)}) copy-start(bf16[8,8,128,128]{3,2,1,0:T(8,128)(2,1)} %get-tuple-element.24.cache_ref) | copy-start | bytes 6291460
  31.3 2.0 %collective-permute-start.2 = (bf16[32,64,128]{2,1,0:T(8,128)(2,1)S(1)}, bf16[32,64,128]{2,1,0:T(8,128)(2,1)S(1)}, u32[]{:S(2)}, u32[]{:S(2)}) collective-permute-start(bf16[32,64,128]{2,1,0:T(8,128)(2,1)S(1)} %shard_map.75), channel_id=1, source_target_pairs={{0,4},{4,0},{8,12},{12,8},{16,20},{20,16},{24,28},{28,24},{32,36},... | collective-permute-start | bytes 1572872 | tf_op jit(solution)/shard_map/ppermute | solution.py:291
  34.3 13.7 %copy-start.6 = (bf16[8,8,128,128]{3,2,1,0:T(8,128)(2,1)S(1)}, bf16[8,8,128,128]{3,2,1,0:T(8,128)(2,1)}, u32[]{:S(2)}) copy-start(bf16[8,8,128,128]{3,2,1,0:T(8,128)(2,1)} %get-tuple-element.22.cache_ref) | copy-start | bytes 6291460
  34.3 6.9 %collective-permute-start.7 = (bf16[8,64,128]{2,1,0:T(8,128)(2,1)S(1)}, bf16[8,64,128]{2,1,0:T(8,128)(2,1)S(1)}, u32[]{:S(2)}, u32[]{:S(2)}) collective-permute-start(bf16[8,64,128]{2,1,0:T(8,128)(2,1)S(1)} %get-tuple-element.25), channel_id=1, source_target_pairs={{0,1},{1,2},{2,3},{3,0},{4,5},{5,6},{6,7},{7,4},{8,9},{9,10},{10,1... | collective-permute-start | bytes 393224 | tf_op jit(solution)/shard_map/ppermute | solution.py:287
  35.9 9.9 %collective-permute-start.5 = (bf16[8,64,128]{2,1,0:T(8,128)(2,1)S(1)}, bf16[8,64,128]{2,1,0:T(8,128)(2,1)S(1)}, u32[]{:S(2)}, u32[]{:S(2)}) collective-permute-start(bf16[8,64,128]{2,1,0:T(8,128)(2,1)S(1)} %get-tuple-element.23), channel_id=1, source_target_pairs={{0,3},{1,0},{2,1},{3,2},{4,7},{5,4},{6,5},{7,6},{8,11},{9,8},{10,9... | collective-permute-start | bytes 393224 | tf_op jit(solution)/shard_map/ppermute | solution.py:287
  37.6 10.4 %collective-permute-start.3 = (bf16[8,64,128]{2,1,0:T(8,128)(2,1)S(1)}, bf16[8,64,128]{2,1,0:T(8,128)(2,1)S(1)}, u32[]{:S(2)}, u32[]{:S(2)}) collective-permute-start(bf16[8,64,128]{2,1,0:T(8,128)(2,1)S(1)} %get-tuple-element.21), channel_id=1, source_target_pairs={{0,2},{1,3},{2,0},{3,1},{4,6},{5,7},{6,4},{7,5},{8,10},{9,11},{10,... | collective-permute-start | bytes 393224 | tf_op jit(solution)/shard_map/ppermute | solution.py:287
  43.3 9.6 %copy-start.5 = (bf16[8,8,128,128]{3,2,1,0:T(8,128)(2,1)S(1)}, bf16[8,8,128,128]{3,2,1,0:T(8,128)(2,1)}, u32[]{:S(2)}) copy-start(bf16[8,8,128,128]{3,2,1,0:T(8,128)(2,1)} %get-tuple-element.20.cache_ref) | copy-start | bytes 6291460
  43.3 11.9 %collective-permute-start.8 = (bf16[8,72,128]{2,1,0:T(8,128)(2,1)S(1)}, bf16[8,72,128]{2,1,0:T(8,128)(2,1)S(1)}, u32[]{:S(2)}, u32[]{:S(2)}) collective-permute-start(bf16[8,72,128]{2,1,0:T(8,128)(2,1)S(1)} %shard_map.80), channel_id=1, source_target_pairs={{0,3},{1,0},{2,1},{3,2},{4,7},{5,4},{6,5},{7,6},{8,11},{9,8},{10,9... | collective-permute-start | bytes 442376 | tf_op jit(solution)/shard_map/ppermute | solution.py:287
  47.9 9.4 %collective-permute-start.6 = (bf16[8,72,128]{2,1,0:T(8,128)(2,1)S(1)}, bf16[8,72,128]{2,1,0:T(8,128)(2,1)S(1)}, u32[]{:S(2)}, u32[]{:S(2)}) collective-permute-start(bf16[8,72,128]{2,1,0:T(8,128)(2,1)S(1)} %shard_map.79), channel_id=1, source_target_pairs={{0,1},{1,2},{2,3},{3,0},{4,5},{5,6},{6,7},{7,4},{8,9},{9,10},{10,1... | collective-permute-start | bytes 442376 | tf_op jit(solution)/shard_map/ppermute | solution.py:287
  50.1 33.9 %copy-start.1 = (bf16[1,2,32,128]{3,2,1,0:T(8,128)(2,1)S(1)}, bf16[1,2,32,128]{3,2,1,0:T(8,128)(2,1)}, u32[]{:S(2)}) copy-start(bf16[1,2,32,128]{3,2,1,0:T(8,128)(2,1)} %param.7) | copy-start | bytes 49156
  50.1 33.9 %copy-start.2 = (bf16[1,2,2,128]{3,2,1,0:T(2,128)(2,1)S(1)}, bf16[1,2,2,128]{3,2,1,0:T(2,128)(2,1)}, u32[]{:S(2)}) copy-start(bf16[1,2,2,128]{3,2,1,0:T(2,128)(2,1)} %param.8) | copy-start | bytes 3076
  50.1 33.9 %copy-start.3 = (bf16[1,2,2,128]{3,2,1,0:T(2,128)(2,1)S(1)}, bf16[1,2,2,128]{3,2,1,0:T(2,128)(2,1)}, u32[]{:S(2)}) copy-start(bf16[1,2,2,128]{3,2,1,0:T(2,128)(2,1)} %param.9) | copy-start | bytes 3076
  50.1 7.3 %collective-permute-start.4 = (bf16[8,72,128]{2,1,0:T(8,128)(2,1)S(1)}, bf16[8,72,128]{2,1,0:T(8,128)(2,1)S(1)}, u32[]{:S(2)}, u32[]{:S(2)}) collective-permute-start(bf16[8,72,128]{2,1,0:T(8,128)(2,1)S(1)} %shard_map.78), channel_id=1, source_target_pairs={{0,2},{1,3},{2,0},{3,1},{4,6},{5,7},{6,4},{7,5},{8,10},{9,11},{10,... | collective-permute-start | bytes 442376 | tf_op jit(solution)/shard_map/ppermute | solution.py:287
  54.9 3.0 %collective-permute-start.9 = (bf16[8,72,128]{2,1,0:T(8,128)(2,1)S(1)}, bf16[8,72,128]{2,1,0:T(8,128)(2,1)S(1)}, u32[]{:S(2)}, u32[]{:S(2)}) collective-permute-start(bf16[8,72,128]{2,1,0:T(8,128)(2,1)S(1)} %shard_map.77.refs_0_), channel_id=1, source_target_pairs={{0,4},{4,0},{8,12},{12,8},{16,20},{20,16},{24,28},{28,24},{32,36},... | collective-permute-start | bytes 442376 | tf_op jit(solution)/shard_map/ppermute | solution.py:291
  55.1 2.7 %collective-permute-start.12 = (bf16[8,72,128]{2,1,0:T(8,128)(2,1)S(1)}, bf16[8,72,128]{2,1,0:T(8,128)(2,1)S(1)}, u32[]{:S(2)}, u32[]{:S(2)}) collective-permute-start(bf16[8,72,128]{2,1,0:T(8,128)(2,1)S(1)} %collective-permute-done.8.refs_3_), channel_id=1, source_target_pairs={{0,4},{4,0},{8,12},{12,8},{16,20},{20,16},{24,28},{28,24},{32,36},... | collective-permute-start | bytes 442376 | tf_op jit(solution)/shard_map/ppermute | solution.py:291
  57.4 1.4 %collective-permute-start.11 = (bf16[8,72,128]{2,1,0:T(8,128)(2,1)S(1)}, bf16[8,72,128]{2,1,0:T(8,128)(2,1)S(1)}, u32[]{:S(2)}, u32[]{:S(2)}) collective-permute-start(bf16[8,72,128]{2,1,0:T(8,128)(2,1)S(1)} %collective-permute-done.6.refs_2_), channel_id=1, source_target_pairs={{0,4},{4,0},{8,12},{12,8},{16,20},{20,16},{24,28},{28,24},{32,36},... | collective-permute-start | bytes 442376 | tf_op jit(solution)/shard_map/ppermute | solution.py:291
  57.4 1.6 %collective-permute-start.10 = (bf16[8,72,128]{2,1,0:T(8,128)(2,1)S(1)}, bf16[8,72,128]{2,1,0:T(8,128)(2,1)S(1)}, u32[]{:S(2)}, u32[]{:S(2)}) collective-permute-start(bf16[8,72,128]{2,1,0:T(8,128)(2,1)S(1)} %collective-permute-done.4.refs_1_), channel_id=1, source_target_pairs={{0,4},{4,0},{8,12},{12,8},{16,20},{20,16},{24,28},{28,24},{32,36},... | collective-permute-start | bytes 442376 | tf_op jit(solution)/shard_map/ppermute | solution.py:291

commit v7 on v5

--- a/solution.py
+++ b/solution.py
@@ -133,9 +133,9 @@
     return outs[:NY], outs[NY]
 
 
-def attend_kernel(lens, q_ref, cache_ref, *refs):
+def attend_kernel(picked, lens, q_ref, cache_ref, *refs):
     out_ref = refs[-1]
-    rows, _, size, half = cache_ref.shape
+    _, _, size, half = cache_ref.shape
     positions = 2 * half
     scale = size ** (-0.5)
     chip, core, group = coordinates()
@@ -146,7 +146,7 @@
     start = jnp.where(at < half, own, other)
     base = jnp.minimum(lens[first], 0)
     stats = [[], [], [], []]
-    for j in range(rows):
+    for j in picked:
         valid = at < lens[first + j] - start
         weights, pairs = [], []
         for k in range(2):
@@ -175,32 +175,38 @@
                 for i in range(4):
                     stats[i].append(pairs[k][i][t * GROUP : (t + 1) * GROUP])
     stats = [jnp.concatenate(stat, 0) for stat in stats]
-    lane = lax.broadcasted_iota(jnp.int32, (rows * LINES, 128), 1)
+    lane = lax.broadcasted_iota(jnp.int32, (len(picked) * LINES, 128), 1)
     table = jnp.where(lane == 0, stats[0], 0.0)
     for i in range(1, 4):
         table = jnp.where(lane == i, stats[i], table)
     table = table.T[:TAIL]
-    for j in range(rows):
-        tail = table[:, (j // 2) * 128 : (j // 2 + 1) * 128]
-        if j % 2 == 1:
+    for n, j in enumerate(picked):
+        tail = table[:, (n // 2) * 128 : (n // 2 + 1) * 128]
+        if n % 2 == 1:
             tail = pltpu.roll(tail, LINES, 1)
         out_ref[j, LINES:, :] = tail.astype(BF16)
 
 
-def attend(lens, queries, cache, before):
-    rows, _, size, positions = cache.shape
-    return pl.pallas_call(
-        attend_kernel,
-        in_specs=[SMEM, VMEM, VMEM] + [ANY] * len(before),
+def attend(lens, queries, cache, before, picked=range(ROWS), done=()):
+    _, _, size, positions = cache.shape
+
+    def kernel(lens, q_ref, cache_ref, *refs):
+        if done:
+            refs[-1][: picked[0]] = refs[0][...]
+        attend_kernel(picked, lens, q_ref, cache_ref, *refs)
+
+    return pl.pallas_call(
+        kernel,
+        in_specs=[SMEM, VMEM, VMEM] + [VMEM] * len(done) + [ANY] * len(before),
         out_specs=VMEM,
-        out_shape=jax.ShapeDtypeStruct((rows, BLOCK, size), BF16),
+        out_shape=jax.ShapeDtypeStruct((picked[-1] + 1, BLOCK, size), BF16),
         compiler_params=PARAMS,
         cost_estimate=pl.CostEstimate(
             flops=120 * ROWS * LINES * positions * size,
             bytes_accessed=160 * ROWS * positions * size,
             transcendentals=0,
         ),
-    )(lens, queries, cache, *before)
+    )(lens, queries, cache, *done, *before)
 
 
 def to_owners_kernel(order, *refs):
@@ -304,13 +310,16 @@
     sends = to_groups(decode_order, got, to_other_core(pass_on(token, got)))
 
     parts = [None] * NY
-    near = (1, 3, 2, 0)
-    gots = {d: along_kvh(sends[d], d) if d else sends[d] for d in near}
-    before = ()
+    near = (1, 3, 2)
+    gots = {d: along_kvh(sends[d], d) for d in near}
+    half = attend(cache_len, sends[0], caches[0], (), range(ROWS // 2))
+    before = (half,)
     for d in near:
         part = attend(cache_len, gots[d], caches[d], before)
         before = (part,)
-        parts[d] = along_kvh(part, NY - d) if d else part
+        parts[d] = along_kvh(part, NY - d)
+    rest = range(ROWS // 2, ROWS)
+    parts[0] = attend(cache_len, sends[0], caches[0], before, rest, (half,))
 
     part = over_chips(to_owners(decode_order, parts, [to_other_core(part) for part in parts]))
     out = finish(part, own, new_keys[0], new_values[0])

time: 85.9 us -> 87.6 us (1.020)
  starting transfers between devices: 23.4 us -> 26 us
  waiting for transfers between devices: 13.2 us -> 11.2 us
  Pallas kernels: 23.6 us -> 24.5 us
    ppermute x6, starting transfers between devices: 10.5 us -> 12.6 us  [along_kvh(): return lax.ppermute(x, 'kvh', [(y, (y + d) % NY) for y in range(NY)])]
    ppermute x6, waiting for transfers between devices: 4.03 us -> 2.01 us  [along_kvh(): return lax.ppermute(x, 'kvh', [(y, (y + d) % NY) for y in range(NY)])]
    pallas_call x4 -> x5, Pallas kernels: 8.31 us -> 9.22 us  [attend(): pl.pallas_call(kernel, in_specs=[SMEM, VMEM, VMEM] + [VMEM] * len(done) +...]
  transfers between devices with their start and end apart: 14 -> 14, of which waited for: 8 -> 6; matrix products, arithmetic and copies ran while one was open for 0% -> 0% of each run, Pallas kernels for 21% -> 22%
where the time goes in v7:
time: 87.6 us; the launch traced here: 87 us
  starting transfers between devices  26 us (30%)
  Pallas kernels  24.5 us (28%)
  blocking collectives  24.3 us (28%)
  waiting for transfers between devices  11.2 us (13%)
    all_to_all x1, blocking collectives, over_chips(): lax.all_to_all(x, 'seq', split_axis=0, concat_axis=0, axis_index_groups=g...  24.3 us
    ppermute x6, starting transfers between devices, along_kvh(): return lax.ppermute(x, 'kvh', [(y, (y + d) % NY) for y in range(NY)])  12.6 us
    all_to_all x1, starting transfers between devices, over_chips(): lax.all_to_all(x, 'seq', split_axis=0, concat_axis=0, axis_index_groups=g...  11.6 us
    pallas_call x1, Pallas kernels, by_head(): pl.pallas_call(by_head_kernel, grid_spec=pltpu.PrefetchScalarGridSpec(num...  10.7 us
    pallas_call x5, Pallas kernels, attend(): pl.pallas_call(kernel, in_specs=[SMEM, VMEM, VMEM] + [VMEM] * len(done) +...  9.22 us
    all_to_all x1, waiting for transfers between devices, over_chips(): lax.all_to_all(x, 'seq', split_axis=0, concat_axis=0, axis_index_groups=g...  6.21 us
    ppermute x7, waiting for transfers between devices, to_other_core(): return lax.ppermute(x, 'seq', [(i, i ^ 1) for i in range(CHIPS * NC)])  2.97 us
    ppermute x6, waiting for transfers between devices, along_kvh(): return lax.ppermute(x, 'kvh', [(y, (y + d) % NY) for y in range(NY)])  2.01 us
  transfers between devices with their start and end apart: 14, of which 6 were waited for; matrix products, arithmetic and copies ran while one was open for 0% of the time, Pallas kernels for 22%

profile of v7, /device:TPU:2, one launch (start us, length us, event | category | flops | bytes accessed | tf_op | source)
XLA Modules:
  0.0 87.0 jit_solution(13240102946761930410)
XLA Ops:
  0.0 0.0 collective-permute-start
  0.0 0.5 collective-permute-start.1
  0.5 0.7 copy-done
  1.2 0.9 %shard_map.73 = (bf16[32,64,128]{2,1,0:T(8,128)(2,1)}, s32[1]{0:T(128)}) custom-call(bf16[64,128]{1,0:T(8,128)(2,1)S(1)} %bitcast.4), custom_call_target="tpu_custom_call" | custom-call | tf_op jit(solution)/shard_map/pallas_call | solution.py:43
  2.1 11.6 %all-to-all-start = ((bf16[32,64,128]{2,1,0:T(8,128)(2,1)}), bf16[32,64,128]{2,1,0:T(8,128)(2,1)S(1)}, u32[]{:S(2)}, u32[]{:S(2)}) async-start(bf16[32,64,128]{2,1,0:T(8,128)(2,1)} %get-tuple-element.16), calls=%async_computation | async-start | bytes 1048576 | tf_op jit(solution)/shard_map/all_to_all | solution.py:288
  13.8 0.0 collective-permute-done.refs_1_
  13.8 0.0 collective-permute-done.1.refs_3_
  13.8 0.0 copy-start.4
  13.8 10.7 %shard_map.74 = (bf16[8,8,128,128]{3,2,1,0:T(8,128)(2,1)}, bf16[8,8,128,128]{3,2,1,0:T(8,128)(2,1)}, bf16[8,8,128,128]{3,2,1,0:T(8,128)(2,1)}, bf16[8,8,128,128]{3,2,1,0:T(8,128)(2,1)}, s32[1]{0:T(128)}) custom-call(s32[1]{0:T(128)} %get-tuple-element.17.core, bf16[16,128,8,128]{3,2,1,0:T(8,128)(2,1)} %refs_0_.1, ...), custom_call_target="tpu_custom_call" | custom-call | bytes 16777216 | tf_op jit(solution)/shard_map/pallas_call | solution.py:118
  24.5 0.0 copy-start.9
  24.5 6.2 %all-to-all-done.got_ref.own_ref = bf16[32,64,128]{2,1,0:T(8,128)(2,1)S(1)} async-done(((bf16[32,64,128]{2,1,0:T(8,128)(2,1)}), bf16[32,64,128]{2,1,0:T(8,128)(2,1)S(1)}, u32[]{:S(2)}, u32[]{:S(2)}) %all-to-all-start) | async-done | bytes 524320 | tf_op jit(solution)/shard_map/all_to_all | solution.py:288
  30.8 0.6 shard_map.75
  31.3 0.1 collective-permute-start.2
  31.4 1.9 %collective-permute-done.2.other_ref = bf16[32,64,128]{2,1,0:T(8,128)(2,1)S(1)} collective-permute-done((bf16[32,64,128]{2,1,0:T(8,128)(2,1)S(1)}, bf16[32,64,128]{2,1,0:T(8,128)(2,1)S(1)}, u32[]{:S(2)}, u32[]{:S(2)}) %collective-permute-start.2) | collective-permute-done | bytes 524320 | tf_op jit(solution)/shard_map/ppermute | solution.py:298
  33.4 0.9 %shard_map.76 = (bf16[8,64,128]{2,1,0:T(8,128)(2,1)S(1)}, bf16[8,64,128]{2,1,0:T(8,128)(2,1)S(1)}, bf16[8,64,128]{2,1,0:T(8,128)(2,1)S(1)}, bf16[8,64,128]{2,1,0:T(8,128)(2,1)S(1)}) custom-call(s32[64]{0:T(128)S(1)} %copy-done.4, bf16[32,64,128]{2,1,0:T(8,128)(2,1)S(1)} %all-to-all-done.got_ref.own_ref, bf16[32,64,128]{2,1,0:T(8,128)(2,1)S(1)} %collective-permute-done.2.other_ref), custom_call_target="tpu_custom_call" | custom-call | flops 1073741824 | bytes 16777216 | tf_op jit(solution)/shard_map/pallas_call | solution.py:86
  34.3 1.7 %collective-permute-start.5 = (bf16[8,64,128]{2,1,0:T(8,128)(2,1)S(1)}, bf16[8,64,128]{2,1,0:T(8,128)(2,1)S(1)}, u32[]{:S(2)}, u32[]{:S(2)}) collective-permute-start(bf16[8,64,128]{2,1,0:T(8,128)(2,1)S(1)} %get-tuple-element.25), channel_id=1, source_target_pairs={{0,1},{1,2},{2,3},{3,0},{4,5},{5,6},{6,7},{7,4},{8,9},{9,10},{10,1... | collective-permute-start | bytes 393224 | tf_op jit(solution)/shard_map/ppermute | solution.py:294
  35.9 2.9 %collective-permute-start.3 = (bf16[8,64,128]{2,1,0:T(8,128)(2,1)S(1)}, bf16[8,64,128]{2,1,0:T(8,128)(2,1)S(1)}, u32[]{:S(2)}, u32[]{:S(2)}) collective-permute-start(bf16[8,64,128]{2,1,0:T(8,128)(2,1)S(1)} %get-tuple-element.21), channel_id=1, source_target_pairs={{0,2},{1,3},{2,0},{3,1},{4,6},{5,7},{6,4},{7,5},{8,10},{9,11},{10,... | collective-permute-start | bytes 393224 | tf_op jit(solution)/shard_map/ppermute | solution.py:294
  38.9 1.3 %collective-permute-start.4 = (bf16[8,64,128]{2,1,0:T(8,128)(2,1)S(1)}, bf16[8,64,128]{2,1,0:T(8,128)(2,1)S(1)}, u32[]{:S(2)}, u32[]{:S(2)}) collective-permute-start(bf16[8,64,128]{2,1,0:T(8,128)(2,1)S(1)} %get-tuple-element.23), channel_id=1, source_target_pairs={{0,3},{1,0},{2,1},{3,2},{4,7},{5,4},{6,5},{7,6},{8,11},{9,8},{10,9... | collective-permute-start | bytes 393224 | tf_op jit(solution)/shard_map/ppermute | solution.py:294
  40.2 0.0 copy-done.5
  40.2 1.5 %shard_map.77.refs_0_ = bf16[4,72,128]{2,1,0:T(8,128)(2,1)S(1)} custom-call(s32[64]{0:T(128)S(1)} %copy-done.9, bf16[8,64,128]{2,1,0:T(8,128)(2,1)S(1)} %get-tuple-element.19.q_ref, bf16[8,8,128,128]{3,2,1,0:T(8,128)(2,1)S(1)} %copy-done.5), custom_call_target="tpu_custom_call" | custom-call | flops 1006632960 | bytes 20971520 | tf_op jit(solution)/shard_map/pallas_call | solution.py:198
  41.7 0.0 collective-permute-done.5.q_ref
  41.7 0.0 copy-done.8
  41.7 2.1 %shard_map.78.refs_0_ = bf16[8,72,128]{2,1,0:T(8,128)(2,1)S(1)} custom-call(s32[64]{0:T(128)S(1)} %copy-done.9, bf16[8,64,128]{2,1,0:T(8,128)(2,1)S(1)} %collective-permute-done.5.q_ref, bf16[8,8,128,128]{3,2,1,0:T(8,128)(2,1)S(1)} %copy-done.8, bf16[4,72,128]{2,1,0:T(8,128)(2,1)S(1)} %shard_map.77.refs_0_), custom_call_target="tpu_custom_call" | custom-call | flops 1006632960 | bytes 20971520 | tf_op jit(solution)/shard_map/pallas_call | solution.py:198
  43.8 0.9 collective-permute-done.4.q_ref
  44.7 2.1 %shard_map.79.refs_0_ = bf16[8,72,128]{2,1,0:T(8,128)(2,1)S(1)} custom-call(s32[64]{0:T(128)S(1)} %copy-done.9, bf16[8,64,128]{2,1,0:T(8,128)(2,1)S(1)} %collective-permute-done.4.q_ref, bf16[8,8,128,128]{3,2,1,0:T(8,128)(2,1)S(1)} %copy-done.7, bf16[8,72,128]{2,1,0:T(8,128)(2,1)S(1)} %shard_map.78.refs_0_), custom_call_target="tpu_custom_call" | custom-call | flops 1006632960 | bytes 20971520 | tf_op jit(solution)/shard_map/pallas_call | solution.py:198
  46.7 0.0 collective-permute-done.3.q_ref
  46.7 0.0 copy-done.6
  46.8 2.1 %shard_map.80.refs_1_ = bf16[8,72,128]{2,1,0:T(8,128)(2,1)S(1)} custom-call(s32[64]{0:T(128)S(1)} %copy-done.9, bf16[8,64,128]{2,1,0:T(8,128)(2,1)S(1)} %collective-permute-done.3.q_ref, bf16[8,8,128,128]{3,2,1,0:T(8,128)(2,1)S(1)} %copy-done.6, bf16[8,72,128]{2,1,0:T(8,128)(2,1)S(1)} %shard_map.79.refs_0_), custom_call_target="tpu_custom_call" | custom-call | flops 1006632960 | bytes 20971520 | tf_op jit(solution)/shard_map/pallas_call | solution.py:198
  48.9 0.0 copy-start.3
  48.9 3.5 %collective-permute-start.7 = (bf16[8,72,128]{2,1,0:T(8,128)(2,1)S(1)}, bf16[8,72,128]{2,1,0:T(8,128)(2,1)S(1)}, u32[]{:S(2)}, u32[]{:S(2)}) collective-permute-start(bf16[8,72,128]{2,1,0:T(8,128)(2,1)S(1)} %shard_map.80.refs_1_), channel_id=1, source_target_pairs={{0,2},{1,3},{2,0},{3,1},{4,6},{5,7},{6,4},{7,5},{8,10},{9,11},{10,... | collective-permute-start | bytes 442376 | tf_op jit(solution)/shard_map/ppermute | solution.py:294
  52.4 0.2 collective-permute-start.8
  52.5 3.1 %collective-permute-start.6 = (bf16[8,72,128]{2,1,0:T(8,128)(2,1)S(1)}, bf16[8,72,128]{2,1,0:T(8,128)(2,1)S(1)}, u32[]{:S(2)}, u32[]{:S(2)}) collective-permute-start(bf16[8,72,128]{2,1,0:T(8,128)(2,1)S(1)} %shard_map.78.refs_0_), channel_id=1, source_target_pairs={{0,3},{1,0},{2,1},{3,2},{4,7},{5,4},{6,5},{7,6},{8,11},{9,8},{10,9... | collective-permute-start | bytes 442376 | tf_op jit(solution)/shard_map/ppermute | solution.py:294
  55.6 1.5 %shard_map.81.refs_0_ = bf16[8,72,128]{2,1,0:T(8,128)(2,1)S(1)} custom-call(s32[64]{0:T(128)S(1)} %copy-done.9, bf16[8,64,128]{2,1,0:T(8,128)(2,1)S(1)} %get-tuple-element.19.q_ref, bf16[8,8,128,128]{3,2,1,0:T(8,128)(2,1)S(1)} %copy-done.5, bf16[4,72,128]{2,1,0:T(8,128)(2,1)S(1)} %shard_map.77.refs_0_, bf16[8,72,128]{2,1,0:T(8,128)(2,1)S(1)} %shard_map.80.refs_1_), custom_call_target="tpu_custom_call" | custom-call | flops 1006632960 | bytes 20971520 | tf_op jit(solution)/shard_map/pallas_call | solution.py:198
  57.1 0.2 collective-permute-start.9
  57.3 0.0 collective-permute-done.7.refs_2_
  57.3 0.5 collective-permute-start.11
  57.8 1.1 %collective-permute-done.8.refs_3_ = bf16[8,72,128]{2,1,0:T(8,128)(2,1)S(1)} collective-permute-done((bf16[8,72,128]{2,1,0:T(8,128)(2,1)S(1)}, bf16[8,72,128]{2,1,0:T(8,128)(2,1)S(1)}, u32[]{:S(2)}, u32[]{:S(2)}) %collective-permute-start.8) | collective-permute-done | bytes 147488 | tf_op jit(solution)/shard_map/ppermute | solution.py:294
  58.9 0.0 collective-permute-start.12
  58.9 0.0 collective-permute-done.6.refs_1_
  58.9 0.5 collective-permute-start.10
  59.4 0.0 collective-permute-done.9.refs_4_
  59.5 0.0 collective-permute-done.11.refs_6_
  59.5 0.9 collective-permute-done.12.refs_7_
  60.3 0.2 collective-permute-done.10.refs_5_
  60.5 0.8 shard_map.82
  61.3 24.3 %all_to_all.10.part_ref = bf16[32,72,128]{2,1,0:T(8,128)(2,1)S(1)} all-to-all(bf16[32,72,128]{2,1,0:T(8,128)(2,1)S(1)} %shard_map.82), channel_id=1, replica_groups={{0,8,16,24,32,40,48,56,64,72,80,88,96,104,112,120,128,136,144,152,160,1..., dimensions={0} | all-to-all | bytes 1179648 | tf_op jit(solution)/shard_map/all_to_all | solution.py:288
  85.6 0.0 copy-done.1
  85.6 1.4 %shard_map.83 = bf16[64,128]{1,0:T(8,128)(2,1)} custom-call(bf16[32,72,128]{2,1,0:T(8,128)(2,1)S(1)} %all_to_all.10.part_ref, bf16[64,128]{1,0:T(8,128)(2,1)S(1)} %bitcast.5, bf16[2,2,128]{2,1,0:T(2,128)(2,1)S(1)} %bitcast.6, bf16[2,2,128]{2,1,0:T(2,128)(2,1)S(1)} %bitcast.7), custom_call_target="tpu_custom_call" | custom-call | tf_op jit(solution)/shard_map/pallas_call | solution.py:277
  (12 shorter events, 0.0 us)
Async XLA Ops:
  0.0 13.8 %collective-permute-start = (bf16[16,128,8,128]{3,2,1,0:T(8,128)(2,1)}, bf16[16,128,8,128]{3,2,1,0:T(8,128)(2,1)}, u32[]{:S(2)}, u32[]{:S(2)}) collective-permute-start(bf16[16,128,8,128]{3,2,1,0:T(8,128)(2,1)} %refs_0_.1), channel_id=1, source_target_pairs={{0,4},{4,0},{8,12},{12,8},{16,20},{20,16},{24,28},{28,24},{32,36},... | collective-permute-start | bytes 12582920 | tf_op jit(solution)/shard_map/ppermute | solution.py:298
  0.0 13.8 %collective-permute-start.1 = (bf16[16,128,8,128]{3,2,1,0:T(8,128)(2,1)}, bf16[16,128,8,128]{3,2,1,0:T(8,128)(2,1)}, u32[]{:S(2)}, u32[]{:S(2)}) collective-permute-start(bf16[16,128,8,128]{3,2,1,0:T(8,128)(2,1)} %refs_2_.1), channel_id=1, source_target_pairs={{0,4},{4,0},{8,12},{12,8},{16,20},{20,16},{24,28},{28,24},{32,36},... | collective-permute-start | bytes 12582920 | tf_op jit(solution)/shard_map/ppermute | solution.py:298
  0.5 0.7 copy-start
  2.1 28.6 %all-to-all-start = ((bf16[32,64,128]{2,1,0:T(8,128)(2,1)}), bf16[32,64,128]{2,1,0:T(8,128)(2,1)S(1)}, u32[]{:S(2)}, u32[]{:S(2)}) async-start(bf16[32,64,128]{2,1,0:T(8,128)(2,1)} %get-tuple-element.16), calls=%async_computation | async-start | bytes 1048576 | tf_op jit(solution)/shard_map/all_to_all | solution.py:288
  13.8 19.6 %copy-start.4 = (s32[64]{0:T(128)S(1)}, s32[64]{0:T(128)}, u32[]{:S(2)}) copy-start(s32[64]{0:T(128)} %order.3) | copy-start | bytes 772
  24.5 15.7 %copy-start.5 = (bf16[8,8,128,128]{3,2,1,0:T(8,128)(2,1)S(1)}, bf16[8,8,128,128]{3,2,1,0:T(8,128)(2,1)}, u32[]{:S(2)}) copy-start(bf16[8,8,128,128]{3,2,1,0:T(8,128)(2,1)} %get-tuple-element.20.cache_ref) | copy-start | bytes 6291460
  24.5 15.7 %copy-start.9 = (s32[64]{0:T(128)S(1)}, s32[64]{0:T(128)}, u32[]{:S(2)}) copy-start(s32[64]{0:T(128)} %lens.9) | copy-start | bytes 772
  31.3 10.4 %copy-start.8 = (bf16[8,8,128,128]{3,2,1,0:T(8,128)(2,1)S(1)}, bf16[8,8,128,128]{3,2,1,0:T(8,128)(2,1)}, u32[]{:S(2)}) copy-start(bf16[8,8,128,128]{3,2,1,0:T(8,128)(2,1)} %get-tuple-element.26.cache_ref) | copy-start | bytes 6291460
  31.3 2.0 %collective-permute-start.2 = (bf16[32,64,128]{2,1,0:T(8,128)(2,1)S(1)}, bf16[32,64,128]{2,1,0:T(8,128)(2,1)S(1)}, u32[]{:S(2)}, u32[]{:S(2)}) collective-permute-start(bf16[32,64,128]{2,1,0:T(8,128)(2,1)S(1)} %shard_map.75), channel_id=1, source_target_pairs={{0,4},{4,0},{8,12},{12,8},{16,20},{20,16},{24,28},{28,24},{32,36},... | collective-permute-start | bytes 1572872 | tf_op jit(solution)/shard_map/ppermute | solution.py:298
  34.3 10.4 %copy-start.7 = (bf16[8,8,128,128]{3,2,1,0:T(8,128)(2,1)S(1)}, bf16[8,8,128,128]{3,2,1,0:T(8,128)(2,1)}, u32[]{:S(2)}) copy-start(bf16[8,8,128,128]{3,2,1,0:T(8,128)(2,1)} %get-tuple-element.24.cache_ref) | copy-start | bytes 6291460
  34.3 7.4 %collective-permute-start.5 = (bf16[8,64,128]{2,1,0:T(8,128)(2,1)S(1)}, bf16[8,64,128]{2,1,0:T(8,128)(2,1)S(1)}, u32[]{:S(2)}, u32[]{:S(2)}) collective-permute-start(bf16[8,64,128]{2,1,0:T(8,128)(2,1)S(1)} %get-tuple-element.25), channel_id=1, source_target_pairs={{0,1},{1,2},{2,3},{3,0},{4,5},{5,6},{6,7},{7,4},{8,9},{9,10},{10,1... | collective-permute-start | bytes 393224 | tf_op jit(solution)/shard_map/ppermute | solution.py:294
  35.9 10.8 %collective-permute-start.3 = (bf16[8,64,128]{2,1,0:T(8,128)(2,1)S(1)}, bf16[8,64,128]{2,1,0:T(8,128)(2,1)S(1)}, u32[]{:S(2)}, u32[]{:S(2)}) collective-permute-start(bf16[8,64,128]{2,1,0:T(8,128)(2,1)S(1)} %get-tuple-element.21), channel_id=1, source_target_pairs={{0,2},{1,3},{2,0},{3,1},{4,6},{5,7},{6,4},{7,5},{8,10},{9,11},{10,... | collective-permute-start | bytes 393224 | tf_op jit(solution)/shard_map/ppermute | solution.py:294
  38.9 5.8 %collective-permute-start.4 = (bf16[8,64,128]{2,1,0:T(8,128)(2,1)S(1)}, bf16[8,64,128]{2,1,0:T(8,128)(2,1)S(1)}, u32[]{:S(2)}, u32[]{:S(2)}) collective-permute-start(bf16[8,64,128]{2,1,0:T(8,128)(2,1)S(1)} %get-tuple-element.23), channel_id=1, source_target_pairs={{0,3},{1,0},{2,1},{3,2},{4,7},{5,4},{6,5},{7,6},{8,11},{9,8},{10,9... | collective-permute-start | bytes 393224 | tf_op jit(solution)/shard_map/ppermute | solution.py:294
  41.7 5.1 %copy-start.6 = (bf16[8,8,128,128]{3,2,1,0:T(8,128)(2,1)S(1)}, bf16[8,8,128,128]{3,2,1,0:T(8,128)(2,1)}, u32[]{:S(2)}) copy-start(bf16[8,8,128,128]{3,2,1,0:T(8,128)(2,1)} %get-tuple-element.22.cache_ref) | copy-start | bytes 6291460
  48.9 36.7 %copy-start.1 = (bf16[1,2,32,128]{3,2,1,0:T(8,128)(2,1)S(1)}, bf16[1,2,32,128]{3,2,1,0:T(8,128)(2,1)}, u32[]{:S(2)}) copy-start(bf16[1,2,32,128]{3,2,1,0:T(8,128)(2,1)} %param.7) | copy-start | bytes 49156
  48.9 36.7 %copy-start.2 = (bf16[1,2,2,128]{3,2,1,0:T(2,128)(2,1)S(1)}, bf16[1,2,2,128]{3,2,1,0:T(2,128)(2,1)}, u32[]{:S(2)}) copy-start(bf16[1,2,2,128]{3,2,1,0:T(2,128)(2,1)} %param.8) | copy-start | bytes 3076
  48.9 36.7 %copy-start.3 = (bf16[1,2,2,128]{3,2,1,0:T(2,128)(2,1)S(1)}, bf16[1,2,2,128]{3,2,1,0:T(2,128)(2,1)}, u32[]{:S(2)}) copy-start(bf16[1,2,2,128]{3,2,1,0:T(2,128)(2,1)} %param.9) | copy-start | bytes 3076
  48.9 8.4 %collective-permute-start.7 = (bf16[8,72,128]{2,1,0:T(8,128)(2,1)S(1)}, bf16[8,72,128]{2,1,0:T(8,128)(2,1)S(1)}, u32[]{:S(2)}, u32[]{:S(2)}) collective-permute-start(bf16[8,72,128]{2,1,0:T(8,128)(2,1)S(1)} %shard_map.80.refs_1_), channel_id=1, source_target_pairs={{0,2},{1,3},{2,0},{3,1},{4,6},{5,7},{6,4},{7,5},{8,10},{9,11},{10,... | collective-permute-start | bytes 442376 | tf_op jit(solution)/shard_map/ppermute | solution.py:294
  52.4 6.6 %collective-permute-start.8 = (bf16[8,72,128]{2,1,0:T(8,128)(2,1)S(1)}, bf16[8,72,128]{2,1,0:T(8,128)(2,1)S(1)}, u32[]{:S(2)}, u32[]{:S(2)}) collective-permute-start(bf16[8,72,128]{2,1,0:T(8,128)(2,1)S(1)} %shard_map.79.refs_0_), channel_id=1, source_target_pairs={{0,1},{1,2},{2,3},{3,0},{4,5},{5,6},{6,7},{7,4},{8,9},{9,10},{10,1... | collective-permute-start | bytes 442376 | tf_op jit(solution)/shard_map/ppermute | solution.py:294
  52.5 6.4 %collective-permute-start.6 = (bf16[8,72,128]{2,1,0:T(8,128)(2,1)S(1)}, bf16[8,72,128]{2,1,0:T(8,128)(2,1)S(1)}, u32[]{:S(2)}, u32[]{:S(2)}) collective-permute-start(bf16[8,72,128]{2,1,0:T(8,128)(2,1)S(1)} %shard_map.78.refs_0_), channel_id=1, source_target_pairs={{0,3},{1,0},{2,1},{3,2},{4,7},{5,4},{6,5},{7,6},{8,11},{9,8},{10,9... | collective-permute-start | bytes 442376 | tf_op jit(solution)/shard_map/ppermute | solution.py:294
  57.1 2.4 %collective-permute-start.9 = (bf16[8,72,128]{2,1,0:T(8,128)(2,1)S(1)}, bf16[8,72,128]{2,1,0:T(8,128)(2,1)S(1)}, u32[]{:S(2)}, u32[]{:S(2)}) collective-permute-start(bf16[8,72,128]{2,1,0:T(8,128)(2,1)S(1)} %shard_map.81.refs_0_), channel_id=1, source_target_pairs={{0,4},{4,0},{8,12},{12,8},{16,20},{20,16},{24,28},{28,24},{32,36},... | collective-permute-start | bytes 442376 | tf_op jit(solution)/shard_map/ppermute | solution.py:298
  57.3 2.2 %collective-permute-start.11 = (bf16[8,72,128]{2,1,0:T(8,128)(2,1)S(1)}, bf16[8,72,128]{2,1,0:T(8,128)(2,1)S(1)}, u32[]{:S(2)}, u32[]{:S(2)}) collective-permute-start(bf16[8,72,128]{2,1,0:T(8,128)(2,1)S(1)} %collective-permute-done.7.refs_2_), channel_id=1, source_target_pairs={{0,4},{4,0},{8,12},{12,8},{16,20},{20,16},{24,28},{28,24},{32,36},... | collective-permute-start | bytes 442376 | tf_op jit(solution)/shard_map/ppermute | solution.py:298
  58.9 1.4 %collective-permute-start.12 = (bf16[8,72,128]{2,1,0:T(8,128)(2,1)S(1)}, bf16[8,72,128]{2,1,0:T(8,128)(2,1)S(1)}, u32[]{:S(2)}, u32[]{:S(2)}) collective-permute-start(bf16[8,72,128]{2,1,0:T(8,128)(2,1)S(1)} %collective-permute-done.8.refs_3_), channel_id=1, source_target_pairs={{0,4},{4,0},{8,12},{12,8},{16,20},{20,16},{24,28},{28,24},{32,36},... | collective-permute-start | bytes 442376 | tf_op jit(solution)/shard_map/ppermute | solution.py:298
  58.9 1.6 %collective-permute-start.10 = (bf16[8,72,128]{2,1,0:T(8,128)(2,1)S(1)}, bf16[8,72,128]{2,1,0:T(8,128)(2,1)S(1)}, u32[]{:S(2)}, u32[]{:S(2)}) collective-permute-start(bf16[8,72,128]{2,1,0:T(8,128)(2,1)S(1)} %collective-permute-done.6.refs_1_), channel_id=1, source_target_pairs={{0,4},{4,0},{8,12},{12,8},{16,20},{20,16},{24,28},{28,24},{32,36},... | collective-permute-start | bytes 442376 | tf_op jit(solution)/shard_map/ppermute | solution.py:298
